TPU v7x, 768 devices: a whole 4x8x12 slice. The times are simulated.
768 devices in a mesh: row: 16 (over y, core), col: 8 (over z_hi, x), depth: 6 (over z_lo).
Axes of the slice: x: 4, y: 8, z: 12 (z_hi: 2, z_lo: 6; z = z_hi * 6 + z_lo), core: 2. Of those that a mesh axis runs over, the one named last changes fastest.
Arguments:
- propagation: bfloat16 [6, 2048, 49152], P('depth', 'col', 'row'), may hold values from -0.21875 to 0.21875
- tile_mask: int32 [6, 16, 384], P('depth', 'col', 'row'), may hold values from 0 to 1
- features: bfloat16 [6, 2048, 256], P('depth', 'col', 'row'), may hold values from -6 to 6
- teleport: bfloat16 [49152, 256], P(('row', 'col', 'depth')), may hold values from -6 to 6
Outputs:
- logits: float32 [49152, 256], P(('row', 'col', 'depth'))
All inputs are finite; a program needn't handle non-finite values.
Results may differ from a plain program's by a relative error of at most 0.0003.
Values may be sent and summed in bfloat16 or wider, within the bound.
No kernel may reach another device: no remote copies, remote signals or barrier semaphores. Data moves between devices by JAX's collectives and lax.ppermute only.
A program may use at most 32 MiB of HBM per device.

v0:
```python
import jax
import jax.numpy as jnp
from jax import lax
from jax.sharding import PartitionSpec as P


def local(propagation, tile_mask, features, teleport):
    keep = jnp.repeat(jnp.repeat(tile_mask, 128, axis=1), 128, axis=2).astype(jnp.bfloat16)
    masked = (propagation * keep)[0]
    classes_all = lax.all_gather(features, "row", axis=2, tiled=True)[0]
    summed = lax.psum_scatter(
        lax.dot_general(
            masked, classes_all, (((0,), (0,)), ((), ())), preferred_element_type=jnp.float32
        ),
        ("col", "depth"),
        scatter_dimension=0,
        tiled=True,
    )
    return 0.9 * summed + 0.1 * teleport.astype(jnp.float32)


def solution(mesh):
    return jax.shard_map(
        local,
        mesh=mesh,
        in_specs=(
            P("depth", "col", "row"),
            P("depth", "col", "row"),
            P("depth", "col", "row"),
            P(("row", "col", "depth"), None),
        ),
        out_specs=P(("row", "col", "depth"), None),
        check_vma=False,
    )
```

profile of v0, /device:TPU:6, one launch (start us, length us, event | category | flops | bytes accessed | tf_op | source)
XLA Modules:
  0.0 332.0 jit_solution(5131087407463624536)
XLA Ops:
  6.5 0.0 reduce-scatter.2.cloned.1.call-start
  6.5 0.7 convert_bitcast_fusion
  7.2 18.2 %all_gather.3 = bf16[1,256,256]{1,2,0:T(8,128)(2,1)S(1)} all-gather(bf16[1,256,16]{1,2,0:T(8,128)(2,1)} %param.6), channel_id=1, replica_groups=mesh['row'=16,'col'=8,'depth'=6] {'row'}, dimensions={2}, use_global_device_ids=true | all-gather | bytes 139264 | tf_op jit(solution)/shard_map/all_gather | solution.py:10
  25.4 1.0 broadcast_in_dim.7
  26.4 0.7 convert_element_type.28
  27.1 3.7 %fusion = f32[3072,256]{1,0:T(8,128)} fusion(bf16[1,256,3072]{2,1,0:T(8,128)(2,1)} %param.4, bf16[1,256,3072]{2,1,0:T(8,128)(2,1)S(1)} %convert_element_type.28, bf16[1,256,256]{1,2,0:T(8,128)(2,1)S(1)} %all_gather.3), kind=kOutput, calls=%fused_computation | convolution fusion | flops 403439616 | bytes 6422528 | tf_op jit(solution)/shard_map/dot_general | solution.py:12
  30.8 0.0 copy-start
  30.8 0.0 reduce-scatter.2.cloned.1.call-update
  30.8 292.8 %reduce-scatter.2.cloned.1.call-done = f32[64,256]{1,0:T(8,128)} async-done(((f32[3072,256]{1,0:T(8,128)}), f32[64,256]{1,0:T(8,128)}) %reduce-scatter.2.cloned.1.call-update) | async-done | bytes 65552 | tf_op jit(solution)/shard_map/reduce_scatter | solution.py:11
  323.7 0.0 copy-done
  323.7 1.5 multiply_add_fusion
  (1 shorter events, 0.0 us)
Async XLA Ops:
  6.5 317.1 %reduce-scatter.2.cloned.1.call-start = ((), (), s32[]{:S(2)}) async-start(), calls=%async_computation.1 | async-start | bytes 3211264 | tf_op jit(solution)/shard_map/reduce_scatter | solution.py:11
  30.8 292.8 %copy-start = (bf16[64,256]{1,0:T(8,128)(2,1)S(1)}, bf16[64,256]{1,0:T(8,128)(2,1)}, u32[]{:S(2)}) copy-start(bf16[64,256]{1,0:T(8,128)(2,1)} %param.7) | copy-start | bytes 98308
Sparse Core Ops, SparseCore 0:
  31.0 292.6 reduce-scatter.1
where the time goes:
time: 332 us
  waiting for transfers between devices  293 us (88%)
  blocking collectives  18.2 us (5%)
  between operations  13.4 us (4%)
  matrix products  3.71 us (1%)
    reduce_scatter x1, waiting for transfers between devices, local(): lax.psum_scatter(lax.dot_general(masked, classes_all, (((0,), (0,)), ((),...  293 us
    all_gather x1, blocking collectives, local(): classes_all = lax.all_gather(features, 'row', axis=2, tiled=True)[0]  18.2 us
  transfers between devices with their start and end apart: 1, of which 1 were waited for; matrix products, arithmetic and copies ran while one was open for 0% of the time, Pallas kernels for 0%

commit v1 on v0

v1 whole, which is shorter than its diff:
```python
import functools

import jax
import jax.numpy as jnp
from jax import lax
from jax.experimental import pallas as pl
from jax.experimental.pallas import tpu as pltpu
from jax.sharding import Mesh, PartitionSpec as P

X = 4
Z = 12
ZH = 2
ROWS = 64
SRC = 256
CLS = 256
TGT = Z * ROWS
SEG = TGT // ZH
TILE = 128
STEP = 8.0
TOP = 32000.0


def mask_kernel(mask_ref, a_ref, o_ref):
    i = pl.program_id(0)
    for j in range(ZH * X * SEG // TILE):
        seg, part = divmod(j * TILE, SEG)
        zh, x = divmod(seg, X)
        keep = mask_ref[i, j].astype(jnp.float32)
        tile = a_ref[:, j * TILE : (j + 1) * TILE].astype(jnp.float32) * keep
        o_ref[x, :, zh * SEG + part : zh * SEG + part + TILE] = tile.astype(jnp.bfloat16)


def mask_blocks(mask, a):
    return pl.pallas_call(
        mask_kernel,
        grid=(SRC // TILE,),
        in_specs=[
            pl.BlockSpec(memory_space=pltpu.SMEM),
            pl.BlockSpec((TILE, ZH * X * SEG), lambda i: (i, 0)),
        ],
        out_specs=pl.BlockSpec((X, TILE, TGT), lambda i: (0, i, 0)),
        out_shape=jax.ShapeDtypeStruct((X, SRC, TGT), jnp.bfloat16),
        name="mask_blocks",
    )(mask, a)


def product_kernel(a_ref, f_ref, o_ref):
    total = jnp.zeros((2 * ROWS, CLS), jnp.float32)
    for x in range(X):
        total += lax.dot_general(
            a_ref[x], f_ref[x], (((0,), (1,)), ((), ())), preferred_element_type=jnp.float32
        )
    top = jnp.max(jnp.abs(total), axis=1, keepdims=True)
    power = jnp.ceil(jnp.log2(jnp.maximum(top, 1e-30)) * STEP)
    coded = jnp.round(total * (TOP * jnp.exp2(power * (-1.0 / STEP)))).astype(jnp.int32)
    power = power.astype(jnp.int32)
    lane = lax.broadcasted_iota(jnp.int32, (16, TILE), 1)
    for b in range(2):
        rows = slice(b * ROWS, (b + 1) * ROWS)
        o_ref[b, 0:ROWS, :] = coded[rows, 0:TILE].astype(jnp.int16)
        o_ref[b, ROWS : 2 * ROWS, :] = coded[rows, TILE : 2 * TILE].astype(jnp.int16)
        scales = jnp.zeros((16, TILE), jnp.int32)
        for k in range(4):
            at = b * ROWS + 16 * k
            scales = jnp.where(lane // 32 == k, power[at : at + 16, :], scales)
        o_ref[b, 2 * ROWS : 2 * ROWS + 16, :] = scales.astype(jnp.int16)


def product(blocks, feats):
    return pl.pallas_call(
        product_kernel,
        grid=(Z // 2,),
        in_specs=[
            pl.BlockSpec((X, SRC, 2 * ROWS), lambda i: (0, 0, i)),
            pl.BlockSpec((X, CLS, SRC), lambda i: (0, 0, 0)),
        ],
        out_specs=pl.BlockSpec((2, 2 * ROWS + 16, TILE), lambda i: (i, 0, 0)),
        out_shape=jax.ShapeDtypeStruct((Z, 2 * ROWS + 16, TILE), jnp.int16),
        name="product",
    )(blocks, feats)


def finish_kernel(q_ref, t_ref, o_ref):
    left = jnp.zeros((ROWS, TILE), jnp.float32)
    right = jnp.zeros((ROWS, TILE), jnp.float32)
    for z in range(Z):
        power = q_ref[z, 2 * ROWS : 2 * ROWS + 16, :].astype(jnp.float32)
        scale = jnp.exp2(power * (1.0 / STEP)) * (1.0 / TOP)
        scale = jnp.concatenate([scale[:, 32 * k : 32 * k + 1] for k in range(4)], axis=0)
        left += q_ref[z, 0:ROWS, :].astype(jnp.float32) * scale
        right += q_ref[z, ROWS : 2 * ROWS, :].astype(jnp.float32) * scale
    o_ref[:, 0:TILE] = 0.9 * left + 0.1 * t_ref[:, 0:TILE].astype(jnp.float32)
    o_ref[:, TILE : 2 * TILE] = 0.9 * right + 0.1 * t_ref[:, TILE : 2 * TILE].astype(jnp.float32)


def finish(coded, teleport):
    return pl.pallas_call(
        finish_kernel,
        out_shape=jax.ShapeDtypeStruct((ROWS, CLS), jnp.float32),
        name="finish",
    )(coded, teleport)


def local(propagation, tile_mask, features, teleport):
    blocks = mask_blocks(tile_mask[0], propagation[0])
    blocks = lax.all_to_all(blocks, "x", 0, 0, tiled=True)
    mine = jnp.broadcast_to(features[0].T[None], (X * 16, 16, SRC))
    feats = lax.all_to_all(mine, ("x", "y", "c"), 0, 0, tiled=True).reshape(X, CLS, SRC)
    coded = product(blocks, feats)
    coded = lax.all_to_all(coded, ("zh", "zl"), 0, 0, tiled=True)
    return finish(coded, teleport)


def solution(mesh):
    devices = mesh.devices.reshape(8, 2, ZH, X, 6)
    fine = Mesh(devices, ("y", "c", "zh", "x", "zl"))
    row, col, depth = ("y", "c"), ("zh", "x"), "zl"
    spec = P(depth, col, row)
    return jax.shard_map(
        local,
        mesh=fine,
        in_specs=(spec, spec, spec, P((*row, *col, depth), None)),
        out_specs=P((*row, *col, depth), None),
        check_vma=False,
    )
```

time: 332 us -> 101 us (0.30)
  the two profiles are of different devices: /device:TPU:6 before, /device:TPU:24 now
where the time goes in v1:
time: 101 us; the launch traced here: 100 us
  blocking collectives  61.7 us (61%)
  waiting for transfers between devices  13.5 us (13%)
  starting transfers between devices  13.3 us (13%)
  Pallas kernels  10.2 us (10%)
  local copies, waits for them, and re-layouts  1.53 us (2%)
    all_to_all x1, blocking collectives, local(): coded = lax.all_to_all(coded, ('zh', 'zl'), 0, 0, tiled=True)  35.1 us
    all_to_all x1, blocking collectives, local(): blocks = lax.all_to_all(blocks, 'x', 0, 0, tiled=True)  26.5 us
    all_to_all x1, waiting for transfers between devices, local(): lax.all_to_all(mine, ('x', 'y', 'c'), 0, 0, tiled=True).reshape(X, CLS, SRC)  13.5 us
    all_to_all x1, starting transfers between devices, local(): lax.all_to_all(mine, ('x', 'y', 'c'), 0, 0, tiled=True).reshape(X, CLS, SRC)  13.3 us
    pallas_call x1, Pallas kernels, product(): pl.pallas_call(product_kernel, grid=(Z // 2,), in_specs=[pl.BlockSpec((X,...  5.59 us
    pallas_call x1, Pallas kernels, mask_blocks(): pl.pallas_call(mask_kernel, grid=(SRC // TILE,), in_specs=[pl.BlockSpec(m...  2.49 us
    pallas_call x1, Pallas kernels, finish(): pl.pallas_call(finish_kernel, out_shape=jax.ShapeDtypeStruct((ROWS, CLS),...  2.15 us
  transfers between devices with their start and end apart: 1, of which 1 were waited for; matrix products, arithmetic and copies ran while one was open for 0% of the time, Pallas kernels for 2%

profile of v1, /device:TPU:24, one launch (start us, length us, event | category | flops | bytes accessed | tf_op | source)
XLA Modules:
  0.0 100.3 jit_solution(7714934940765633542)
XLA Ops:
  0.0 1.5 %broadcast_in_dim.2 = bf16[64,16,256]{2,1,0:T(8,128)(2,1)} broadcast(bf16[16,256]{1,0:T(8,128)(2,1)} %bitcast.8), dimensions={1,2} | broadcast | bytes 532480 | tf_op jit(solution)/shard_map/broadcast_in_dim | solution.py:107
  1.5 13.3 %all-to-all-start.1 = ((bf16[64,16,256]{2,1,0:T(8,128)(2,1)}), bf16[64,16,256]{2,1,0:T(8,128)(2,1)S(1)}, u32[]{:S(2)}, u32[]{:S(2)}) async-start(bf16[64,16,256]{2,1,0:T(8,128)(2,1)} %broadcast_in_dim.2), calls=%async_computation.1 | async-start | bytes 1048576 | tf_op jit(solution)/shard_map/all_to_all | solution.py:108
  14.9 2.5 %mask_blocks.1 = bf16[4,256,768]{2,1,0:T(8,128)(2,1)} custom-call(s32[2,24]{1,0:T(2,128)} %bitcast.9, bf16[256,3072]{1,0:T(8,128)(2,1)} %bitcast.7), custom_call_target="tpu_custom_call" | custom-call | tf_op jit(solution)/shard_map/mask_blocks/pallas_call | solution.py:34
  17.4 13.5 %all-to-all-done.1 = bf16[64,16,256]{2,1,0:T(8,128)(2,1)S(1)} async-done(((bf16[64,16,256]{2,1,0:T(8,128)(2,1)}), bf16[64,16,256]{2,1,0:T(8,128)(2,1)S(1)}, u32[]{:S(2)}, u32[]{:S(2)}) %all-to-all-start.1) | async-done | bytes 524320 | tf_op jit(solution)/shard_map/all_to_all | solution.py:108
  30.8 0.0 copy-start
  30.8 26.5 %all_to_all.15.a_ref = bf16[4,256,768]{2,1,0:T(8,128)(2,1)} all-to-all(bf16[4,256,768]{2,1,0:T(8,128)(2,1)} %mask_blocks.1), channel_id=1, replica_groups=mesh['y'=8,'c'=2,'zh'=2,'x'=4,'zl'=6] {'x'}, dimensions={0} | all-to-all | bytes 3145728 | tf_op jit(solution)/shard_map/all_to_all | solution.py:106
  57.4 0.0 copy-done
  57.4 5.6 %product.1 = s16[12,144,128]{2,1,0:T(8,128)(2,1)} custom-call(bf16[4,256,768]{2,1,0:T(8,128)(2,1)} %all_to_all.15.a_ref, bf16[4,256,256]{2,1,0:T(8,128)(2,1)} %bitcast.6), custom_call_target="tpu_custom_call" | custom-call | tf_op jit(solution)/shard_map/product/pallas_call | solution.py:70
  63.0 35.1 %all_to_all.16.q_ref = s16[12,144,128]{2,1,0:T(8,128)(2,1)} all-to-all(s16[12,144,128]{2,1,0:T(8,128)(2,1)} %product.1), channel_id=1, replica_groups=mesh['y'=8,'c'=2,'zh'=2,'x'=4,'zl'=6] {'zh','zl'}, dimensions={0} | all-to-all | bytes 884736 | tf_op jit(solution)/shard_map/all_to_all | solution.py:110
  98.1 2.2 %finish.1 = f32[64,256]{1,0:T(8,128)} custom-call(s16[12,144,128]{2,1,0:T(8,128)(2,1)} %all_to_all.16.q_ref, bf16[64,256]{1,0:T(8,128)(2,1)} %t_ref.1), custom_call_target="tpu_custom_call" | custom-call | tf_op jit(solution)/shard_map/finish/pallas_call | solution.py:97
Async XLA Ops:
  1.5 29.3 %all-to-all-start.1 = ((bf16[64,16,256]{2,1,0:T(8,128)(2,1)}), bf16[64,16,256]{2,1,0:T(8,128)(2,1)S(1)}, u32[]{:S(2)}, u32[]{:S(2)}) async-start(bf16[64,16,256]{2,1,0:T(8,128)(2,1)} %broadcast_in_dim.2), calls=%async_computation.1 | async-start | bytes 1048576 | tf_op jit(solution)/shard_map/all_to_all | solution.py:108
  30.8 26.5 %copy-start = (bf16[64,16,256]{2,1,0:T(8,128)(2,1)}, bf16[64,16,256]{2,1,0:T(8,128)(2,1)S(1)}, u32[]{:S(2)}) copy-start(bf16[64,16,256]{2,1,0:T(8,128)(2,1)S(1)} %all-to-all-done.1) | copy-start | bytes 1572868

commit v2 on v1

v2 whole, which is shorter than its diff:
```python
import functools

import jax
import jax.numpy as jnp
from jax import lax
from jax.experimental import pallas as pl
from jax.experimental.pallas import tpu as pltpu
from jax.sharding import Mesh, PartitionSpec as P

X = 4
Y = 8
CORES = 2
Z = 12
ZH = 2
ROWS = 64
SRC = 256
CLS = 256
HELD = CLS // (Y * CORES)
TGT = Z * ROWS
SEG = TGT // ZH
TILE = 128
STEP = 8.0
TOP = 32000.0
MIB = 1 << 20


def mask_kernel(n, me_ref, mask_ref, *refs):
    i = pl.program_id(0)
    for k in range(n):
        for zh in range(ZH):
            a_ref = refs[k * ZH + zh]
            first = (zh * X + lax.rem(me_ref[0] + me_ref[1] + k, X)) * (SEG // TILE)
            for p in range(SEG // TILE):
                keep = mask_ref[i, first + p].astype(jnp.float32)
                tile = a_ref[:, p * TILE : (p + 1) * TILE].astype(jnp.float32) * keep
                to = zh * SEG + p * TILE
                refs[n * ZH + k][:, to : to + TILE] = tile.astype(jnp.bfloat16)


def own_kernel(me_ref, mask_ref, a0_ref, a1_ref, f_ref, o_ref, copies_ref):
    mask_kernel(1, me_ref, mask_ref, a0_ref, a1_ref, o_ref)
    copies_ref[...] = jnp.broadcast_to(f_ref[...][None], copies_ref.shape)


def mask_specs(n, first):
    def segment(k, zh):
        return pl.BlockSpec((TILE, SEG), lambda i, me: (i, zh * X + lax.rem(me[0] + first + k, X)))

    return [pl.BlockSpec(memory_space=pltpu.SMEM)] + [segment(k, zh) for k in range(n) for zh in range(ZH)]


def mask_others(me, mask, a):
    n = X - 1
    return pl.pallas_call(
        functools.partial(mask_kernel, n),
        grid_spec=pltpu.PrefetchScalarGridSpec(
            num_scalar_prefetch=1,
            grid=(SRC // TILE,),
            in_specs=mask_specs(n, 1),
            out_specs=[pl.BlockSpec((TILE, TGT), lambda i, me: (i, 0))] * n,
        ),
        out_shape=[jax.ShapeDtypeStruct((SRC, TGT), jnp.bfloat16)] * n,
        compiler_params=pltpu.CompilerParams(vmem_limit_bytes=16 * MIB),
        name="mask_others",
    )(jnp.stack([me, jnp.int32(1)]), mask, *[a] * (n * ZH))


def mask_own(me, mask, a, feats):
    half = X * Y * TILE // SRC
    return pl.pallas_call(
        own_kernel,
        grid_spec=pltpu.PrefetchScalarGridSpec(
            num_scalar_prefetch=1,
            grid=(SRC // TILE,),
            in_specs=mask_specs(1, 0) + [pl.BlockSpec((HELD, SRC), lambda i, me: (0, 0))],
            out_specs=[
                pl.BlockSpec((TILE, TGT), lambda i, me: (i, 0)),
                pl.BlockSpec((half, HELD, SRC), lambda i, me: (i, 0, 0)),
            ],
        ),
        out_shape=[
            jax.ShapeDtypeStruct((SRC, TGT), jnp.bfloat16),
            jax.ShapeDtypeStruct((X * Y, HELD, SRC), jnp.bfloat16),
        ],
        compiler_params=pltpu.CompilerParams(vmem_limit_bytes=16 * MIB),
        name="mask_own",
    )(jnp.stack([me, jnp.int32(0)]), mask, a, a, feats)


def product_kernel(me_ref, f_ref, *refs):
    o_ref = refs[X]
    feats = []
    for k in range(X):
        x = lax.rem(me_ref[0] + X - k, X)
        feats.append(jnp.concatenate([f_ref[c, x, y] for y in range(Y) for c in range(CORES)], axis=0))
    lane = lax.broadcasted_iota(jnp.int32, (16, TILE), 1)
    wide = 2 * TILE
    for i in range(TGT // wide):
        total = jnp.zeros((CLS, wide), jnp.float32)
        for k in range(X):
            total += jnp.dot(
                feats[k], refs[k][:, i * wide : (i + 1) * wide], preferred_element_type=jnp.float32
            )
        total = total.T
        top = jnp.max(jnp.abs(total), axis=1, keepdims=True)
        power = jnp.ceil(jnp.log2(jnp.maximum(top, 1e-30)) * STEP)
        coded = jnp.round(total * (TOP * jnp.exp2(power * (-1.0 / STEP)))).astype(jnp.int32)
        power = power.astype(jnp.int32)
        for b in range(wide // ROWS):
            z = i * (wide // ROWS) + b
            rows = slice(b * ROWS, (b + 1) * ROWS)
            o_ref[z, 0:ROWS, :] = coded[rows, 0:TILE].astype(jnp.int16)
            o_ref[z, ROWS : 2 * ROWS, :] = coded[rows, TILE : 2 * TILE].astype(jnp.int16)
            scales = jnp.zeros((16, TILE), jnp.int32)
            for k in range(4):
                at = b * ROWS + 16 * k
                scales = jnp.where(lane // 32 == k, power[at : at + 16, :], scales)
            o_ref[z, 2 * ROWS : 2 * ROWS + 16, :] = scales.astype(jnp.int16)


def product(me, feats, blocks):
    whole = pl.BlockSpec(memory_space=pltpu.VMEM)
    return pl.pallas_call(
        product_kernel,
        in_specs=[pl.BlockSpec(memory_space=pltpu.SMEM)] + [whole] * (1 + X),
        out_specs=whole,
        out_shape=jax.ShapeDtypeStruct((Z, 2 * ROWS + 16, TILE), jnp.int16),
        compiler_params=pltpu.CompilerParams(vmem_limit_bytes=16 * MIB),
        name="product",
    )(me, feats, *blocks)


def finish_kernel(q_ref, t_ref, o_ref):
    left = jnp.zeros((ROWS, TILE), jnp.float32)
    right = jnp.zeros((ROWS, TILE), jnp.float32)
    for z in range(Z):
        power = q_ref[z, 2 * ROWS : 2 * ROWS + 16, :].astype(jnp.float32)
        scale = jnp.exp2(power * (1.0 / STEP)) * (1.0 / TOP)
        scale = jnp.concatenate([scale[:, 32 * k : 32 * k + 1] for k in range(4)], axis=0)
        left += q_ref[z, 0:ROWS, :].astype(jnp.float32) * scale
        right += q_ref[z, ROWS : 2 * ROWS, :].astype(jnp.float32) * scale
    o_ref[:, 0:TILE] = 0.9 * left + 0.1 * t_ref[:, 0:TILE].astype(jnp.float32)
    o_ref[:, TILE : 2 * TILE] = 0.9 * right + 0.1 * t_ref[:, TILE : 2 * TILE].astype(jnp.float32)


def finish(coded, teleport):
    return pl.pallas_call(
        finish_kernel,
        out_shape=jax.ShapeDtypeStruct((ROWS, CLS), jnp.float32),
        compiler_params=pltpu.CompilerParams(vmem_limit_bytes=16 * MIB),
        name="finish",
    )(coded, teleport)


def local(propagation, tile_mask, features, teleport):
    me = lax.axis_index("x").astype(jnp.int32)
    others = mask_others(me, tile_mask[0], propagation[0])
    blocks = [lax.ppermute(b, "x", [(i, (i + k) % X) for i in range(X)]) for k, b in enumerate(others, 1)]
    mine = lax.optimization_barrier((features[0].T, *others))[0]
    own, copies = mask_own(me, tile_mask[0], propagation[0], mine)
    copies, blocks[0] = lax.optimization_barrier((copies, blocks[0]))
    feats = lax.all_to_all(copies, ("x", "y"), 0, 0, tiled=True)
    feats = lax.all_gather(feats, "c", axis=0).reshape(CORES, X, Y, HELD, SRC)
    coded = product(me[None], feats, [own, *blocks])
    coded = lax.all_to_all(coded, ("zh", "zl"), 0, 0, tiled=True)
    return finish(coded, teleport)


def solution(mesh):
    devices = mesh.devices.reshape(Y, CORES, ZH, X, Z // ZH)
    fine = Mesh(devices, ("y", "c", "zh", "x", "zl"))
    row, col, depth = ("y", "c"), ("zh", "x"), "zl"
    spec = P(depth, col, row)
    return jax.shard_map(
        local,
        mesh=fine,
        in_specs=(spec, spec, spec, P((*row, *col, depth), None)),
        out_specs=P((*row, *col, depth), None),
        check_vma=False,
    )
```

time: 101 us -> 90.3 us (0.89)
  the two profiles are of different devices: /device:TPU:24 before, /device:TPU:2 now
where the time goes in v2:
time: 90.3 us; the launch traced here: 90 us
  blocking collectives  39.8 us (44%)
  waiting for transfers between devices  24.6 us (27%)
  starting transfers between devices  17.6 us (19%)
  Pallas kernels  5.68 us (6%)
  local copies, waits for them, and re-layouts  2.1 us (2%)
    all_to_all x1, blocking collectives, local(): coded = lax.all_to_all(coded, ('zh', 'zl'), 0, 0, tiled=True)  37.7 us
    ppermute x3, waiting for transfers between devices, local(): lax.ppermute(b, 'x', [(i, (i + k) % X) for i in range(X)])  21.8 us
    ppermute x3, starting transfers between devices, local(): lax.ppermute(b, 'x', [(i, (i + k) % X) for i in range(X)])  10.8 us
    all_to_all x1, starting transfers between devices, local(): feats = lax.all_to_all(copies, ('x', 'y'), 0, 0, tiled=True)  6.79 us
    all_to_all x1, waiting for transfers between devices, local(): feats = lax.all_to_all(copies, ('x', 'y'), 0, 0, tiled=True)  2.79 us
    all_gather x1, blocking collectives, local(): feats = lax.all_gather(feats, 'c', axis=0).reshape(CORES, X, Y, HELD, SRC)  2.17 us
    unnamed x12, local copies, waits for them, and re-layouts  2.1 us
    pallas_call x1, Pallas kernels, mask_own(): pl.pallas_call(own_kernel, grid_spec=pltpu.PrefetchScalarGridSpec(num_sca...  1.93 us
  transfers between devices with their start and end apart: 4, of which 4 were waited for; matrix products, arithmetic and copies ran while one was open for 0% of the time, Pallas kernels for 2%

profile of v2, /device:TPU:2, one launch (start us, length us, event | category | flops | bytes accessed | tf_op | source)
XLA Modules:
  0.0 90.0 jit_solution(199558512443942109)
XLA Ops:
  0.0 0.1 pad_add_fusion
  0.1 0.0 copy-start
  0.1 1.4 %copy-done = bf16[1,256,3072]{2,1,0:T(8,128)(2,1)S(1)} copy-done((bf16[1,256,3072]{2,1,0:T(8,128)(2,1)S(1)}, bf16[1,256,3072]{2,1,0:T(8,128)(2,1)}, u32[]{:S(2)}) %copy-start) | copy-done | bytes 1572888
  1.5 0.0 copy-start.4
  1.5 0.7 copy-done.4
  2.2 0.0 copy-start.1
  2.2 0.0 copy-start.3
  2.2 0.0 copy-start.5
  2.2 1.6 %mask_others.1 = (bf16[256,768]{1,0:T(8,128)(2,1)S(1)}, bf16[256,768]{1,0:T(8,128)(2,1)S(1)}, bf16[256,768]{1,0:T(8,128)(2,1)S(1)}) custom-call(s32[2]{0:T(128)S(1)} %get-tuple-element.22.me_ref, s32[2,24]{1,0:T(2,128)S(1)} %bitcast.17, bf16[256,3072]{1,0:T(8,128)(2,1)S(1)} %bitcast.7, bf16[256,3072]{1,0:T(8,128)(2,1)S(1)} %bitcast.8, ...), custom_call_target="tpu_custom_call" | custom-call | tf_op jit(solution)/shard_map/mask_others/pallas_call | solution.py:54
  3.8 3.4 %collective-permute-start = (bf16[256,768]{1,0:T(8,128)(2,1)S(1)}, bf16[256,768]{1,0:T(8,128)(2,1)S(1)}, u32[]{:S(2)}, u32[]{:S(2)}) collective-permute-start(bf16[256,768]{1,0:T(8,128)(2,1)S(1)} %get-tuple-element.13), channel_id=1, source_target_pairs={{0,6},{6,12},{12,18},{18,0},{1,7},{7,13},{13,19},{19,1},{2,8},{8,1... | collective-permute-start | bytes 1179656 | tf_op jit(solution)/shard_map/ppermute | solution.py:158
  7.2 0.0 copy-done.1
  7.2 0.0 copy-done.3
  7.2 0.0 copy-done.5
  7.2 1.9 %mask_own.1 = (bf16[256,768]{1,0:T(8,128)(2,1)S(1)}, bf16[32,16,256]{2,1,0:T(8,128)(2,1)}) custom-call(s32[2]{0:T(128)S(1)} %get-tuple-element.21.me_ref, s32[2,24]{1,0:T(2,128)S(1)} %bitcast.18, bf16[256,3072]{1,0:T(8,128)(2,1)S(1)} %bitcast.13, bf16[256,3072]{1,0:T(8,128)(2,1)S(1)} %bitcast.14, bf16[16,256]{1,0:T(8,128)(2,1)S(1)} %bitcast.16), custom_call_target="tpu_custom_call" | custom-call | tf_op jit(solution)/shard_map/mask_own/pallas_call | solution.py:70
  9.2 11.8 %collective-permute-done.refs_1_ = bf16[256,768]{1,0:T(8,128)(2,1)S(1)} collective-permute-done((bf16[256,768]{1,0:T(8,128)(2,1)S(1)}, bf16[256,768]{1,0:T(8,128)(2,1)S(1)}, u32[]{:S(2)}, u32[]{:S(2)}) %collective-permute-start) | collective-permute-done | bytes 393248 | tf_op jit(solution)/shard_map/ppermute | solution.py:158
  21.0 6.8 %all-to-all-start = ((bf16[32,16,256]{2,1,0:T(8,128)(2,1)}), bf16[32,16,256]{2,1,0:T(8,128)(2,1)S(1)}, u32[]{:S(2)}, u32[]{:S(2)}) async-start(bf16[32,16,256]{2,1,0:T(8,128)(2,1)} %get-tuple-element.18), calls=%async_computation | async-start | bytes 524288 | tf_op jit(solution)/shard_map/all_to_all | solution.py:162
  27.8 4.1 %collective-permute-start.1 = (bf16[256,768]{1,0:T(8,128)(2,1)S(1)}, bf16[256,768]{1,0:T(8,128)(2,1)S(1)}, u32[]{:S(2)}, u32[]{:S(2)}) collective-permute-start(bf16[256,768]{1,0:T(8,128)(2,1)S(1)} %get-tuple-element.14), channel_id=1, source_target_pairs={{0,12},{6,18},{12,0},{18,6},{1,13},{7,19},{13,1},{19,7},{2,14},{8,... | collective-permute-start | bytes 1179656 | tf_op jit(solution)/shard_map/ppermute | solution.py:158
  31.9 3.3 %collective-permute-start.2 = (bf16[256,768]{1,0:T(8,128)(2,1)S(1)}, bf16[256,768]{1,0:T(8,128)(2,1)S(1)}, u32[]{:S(2)}, u32[]{:S(2)}) collective-permute-start(bf16[256,768]{1,0:T(8,128)(2,1)S(1)} %get-tuple-element.15), channel_id=1, source_target_pairs={{0,18},{6,0},{12,6},{18,12},{1,19},{7,1},{13,7},{19,13},{2,20},{8,... | collective-permute-start | bytes 1179656 | tf_op jit(solution)/shard_map/ppermute | solution.py:158
  35.2 2.8 %all-to-all-done = bf16[32,16,256]{2,1,0:T(8,128)(2,1)S(1)} async-done(((bf16[32,16,256]{2,1,0:T(8,128)(2,1)}), bf16[32,16,256]{2,1,0:T(8,128)(2,1)S(1)}, u32[]{:S(2)}, u32[]{:S(2)}) %all-to-all-start) | async-done | bytes 262176 | tf_op jit(solution)/shard_map/all_to_all | solution.py:162
  38.0 2.2 %all-gather = bf16[64,16,256]{2,1,0:T(8,128)(2,1)S(1)} all-gather(bf16[32,16,256]{2,1,0:T(8,128)(2,1)S(1)} %all-to-all-done), channel_id=2, replica_groups=mesh['y'=8,'c'=2,'zh'=2,'x'=4,'zl'=6] {'c'}, dimensions={0}, use_global_device_ids=true | all-gather | bytes 786432 | tf_op jit(solution)/shard_map/all_gather | solution.py:163
  40.2 3.8 %collective-permute-done.1.refs_2_ = bf16[256,768]{1,0:T(8,128)(2,1)S(1)} collective-permute-done((bf16[256,768]{1,0:T(8,128)(2,1)S(1)}, bf16[256,768]{1,0:T(8,128)(2,1)S(1)}, u32[]{:S(2)}, u32[]{:S(2)}) %collective-permute-start.1) | collective-permute-done | bytes 393248 | tf_op jit(solution)/shard_map/ppermute | solution.py:158
  44.0 6.2 %collective-permute-done.2.refs_3_ = bf16[256,768]{1,0:T(8,128)(2,1)S(1)} collective-permute-done((bf16[256,768]{1,0:T(8,128)(2,1)S(1)}, bf16[256,768]{1,0:T(8,128)(2,1)S(1)}, u32[]{:S(2)}, u32[]{:S(2)}) %collective-permute-start.2) | collective-permute-done | bytes 393248 | tf_op jit(solution)/shard_map/ppermute | solution.py:158
  50.2 0.0 copy-start.2
  50.2 0.9 %product.1 = s16[12,144,128]{2,1,0:T(8,128)(2,1)S(1)} custom-call(s32[1]{0:T(128)} %bitcast.me_ref, bf16[2,4,8,16,256]{4,3,2,1,0:T(8,128)(2,1)S(1)} %bitcast.15, bf16[256,768]{1,0:T(8,128)(2,1)S(1)} %get-tuple-element.19.refs_0_, bf16[256,768]{1,0:T(8,128)(2,1)S(1)} %collective-permute-done.refs_1_, bf16[256,768]{1,0:T(8,128)(2,1)S(1)} %collective-permute-done.1.refs_2_, ...), custom_call_target="tpu_custom_call" | custom-call | tf_op jit(solution)/shard_map/product/pallas_call | solution.py:123
  51.1 37.7 %all_to_all.10.q_ref = s16[12,144,128]{2,1,0:T(8,128)(2,1)S(1)} all-to-all(s16[12,144,128]{2,1,0:T(8,128)(2,1)S(1)} %product.1), channel_id=1, replica_groups=mesh['y'=8,'c'=2,'zh'=2,'x'=4,'zl'=6] {'zh','zl'}, dimensions={0} | all-to-all | bytes 884736 | tf_op jit(solution)/shard_map/all_to_all | solution.py:165
  88.8 0.0 copy-done.2
  88.8 1.2 %finish.1 = f32[64,256]{1,0:T(8,128)} custom-call(s16[12,144,128]{2,1,0:T(8,128)(2,1)S(1)} %all_to_all.10.q_ref, bf16[64,256]{1,0:T(8,128)(2,1)S(1)} %copy-done.2), custom_call_target="tpu_custom_call" | custom-call | tf_op jit(solution)/shard_map/finish/pallas_call | solution.py:147
Async XLA Ops:
  0.1 1.4 %copy-start = (bf16[1,256,3072]{2,1,0:T(8,128)(2,1)S(1)}, bf16[1,256,3072]{2,1,0:T(8,128)(2,1)}, u32[]{:S(2)}) copy-start(bf16[1,256,3072]{2,1,0:T(8,128)(2,1)} %param.4) | copy-start | bytes 4718596
  1.5 0.7 copy-start.4
  2.2 5.1 %copy-start.1 = (bf16[1,256,3072]{2,1,0:T(8,128)(2,1)S(1)}, bf16[1,256,3072]{2,1,0:T(8,128)(2,1)}, u32[]{:S(2)}) copy-start(bf16[1,256,3072]{2,1,0:T(8,128)(2,1)} %param.4) | copy-start | bytes 4718596
  2.2 5.1 %copy-start.3 = (bf16[1,256,16]{1,2,0:T(8,128)(2,1)S(1)}, bf16[1,256,16]{1,2,0:T(8,128)(2,1)}, u32[]{:S(2)}) copy-start(bf16[1,256,16]{1,2,0:T(8,128)(2,1)} %param.6) | copy-start | bytes 24580
  2.2 5.1 %copy-start.5 = (s32[1,2,24]{2,1,0:T(2,128)S(1)}, s32[1,2,24]{2,1,0:T(2,128)}, u32[]{:S(2)}) copy-start(s32[1,2,24]{2,1,0:T(2,128)} %param.5) | copy-start | bytes 580
  3.8 17.2 %collective-permute-start = (bf16[256,768]{1,0:T(8,128)(2,1)S(1)}, bf16[256,768]{1,0:T(8,128)(2,1)S(1)}, u32[]{:S(2)}, u32[]{:S(2)}) collective-permute-start(bf16[256,768]{1,0:T(8,128)(2,1)S(1)} %get-tuple-element.13), channel_id=1, source_target_pairs={{0,6},{6,12},{12,18},{18,0},{1,7},{7,13},{13,19},{19,1},{2,8},{8,1... | collective-permute-start | bytes 1179656 | tf_op jit(solution)/shard_map/ppermute | solution.py:158
  21.0 17.0 %all-to-all-start = ((bf16[32,16,256]{2,1,0:T(8,128)(2,1)}), bf16[32,16,256]{2,1,0:T(8,128)(2,1)S(1)}, u32[]{:S(2)}, u32[]{:S(2)}) async-start(bf16[32,16,256]{2,1,0:T(8,128)(2,1)} %get-tuple-element.18), calls=%async_computation | async-start | bytes 524288 | tf_op jit(solution)/shard_map/all_to_all | solution.py:162
  27.8 16.2 %collective-permute-start.1 = (bf16[256,768]{1,0:T(8,128)(2,1)S(1)}, bf16[256,768]{1,0:T(8,128)(2,1)S(1)}, u32[]{:S(2)}, u32[]{:S(2)}) collective-permute-start(bf16[256,768]{1,0:T(8,128)(2,1)S(1)} %get-tuple-element.14), channel_id=1, source_target_pairs={{0,12},{6,18},{12,0},{18,6},{1,13},{7,19},{13,1},{19,7},{2,14},{8,... | collective-permute-start | bytes 1179656 | tf_op jit(solution)/shard_map/ppermute | solution.py:158
  31.9 18.3 %collective-permute-start.2 = (bf16[256,768]{1,0:T(8,128)(2,1)S(1)}, bf16[256,768]{1,0:T(8,128)(2,1)S(1)}, u32[]{:S(2)}, u32[]{:S(2)}) collective-permute-start(bf16[256,768]{1,0:T(8,128)(2,1)S(1)} %get-tuple-element.15), channel_id=1, source_target_pairs={{0,18},{6,0},{12,6},{18,12},{1,19},{7,1},{13,7},{19,13},{2,20},{8,... | collective-permute-start | bytes 1179656 | tf_op jit(solution)/shard_map/ppermute | solution.py:158
  50.2 38.6 %copy-start.2 = (bf16[64,256]{1,0:T(8,128)(2,1)S(1)}, bf16[64,256]{1,0:T(8,128)(2,1)}, u32[]{:S(2)}) copy-start(bf16[64,256]{1,0:T(8,128)(2,1)} %t_ref.1) | copy-start | bytes 98308

commit v3 on v2

--- a/solution.py
+++ b/solution.py
@@ -158,9 +158,12 @@
     blocks = [lax.ppermute(b, "x", [(i, (i + k) % X) for i in range(X)]) for k, b in enumerate(others, 1)]
     mine = lax.optimization_barrier((features[0].T, *others))[0]
     own, copies = mask_own(me, tile_mask[0], propagation[0], mine)
-    copies, blocks[0] = lax.optimization_barrier((copies, blocks[0]))
-    feats = lax.all_to_all(copies, ("x", "y"), 0, 0, tiled=True)
-    feats = lax.all_gather(feats, "c", axis=0).reshape(CORES, X, Y, HELD, SRC)
+    feats = lax.cond(
+        me < X,
+        lambda c: lax.all_gather(lax.all_to_all(c, ("x", "y"), 0, 0, tiled=True), "c", axis=0),
+        lambda c: jnp.stack([c] * CORES),
+        copies,
+    ).reshape(CORES, X, Y, HELD, SRC)
     coded = product(me[None], feats, [own, *blocks])
     coded = lax.all_to_all(coded, ("zh", "zl"), 0, 0, tiled=True)
     return finish(coded, teleport)

time: 90.3 us -> 78.8 us (0.87)
  the two profiles are of different devices: /device:TPU:2 before, /device:TPU:8 now
where the time goes in v3:
time: 78.8 us; the launch traced here: 78.5 us
  blocking collectives  59.1 us (75%)
  starting transfers between devices  11.4 us (14%)
  Pallas kernels  5.74 us (7%)
  local copies, waits for them, and re-layouts  2.1 us (3%)
    all_to_all x1, blocking collectives, local(): coded = lax.all_to_all(coded, ('zh', 'zl'), 0, 0, tiled=True)  34.7 us
    all_to_all x1, blocking collectives, local(): lax.all_to_all(c, ('x', 'y'), 0, 0, tiled=True)  22.2 us
    ppermute x3, starting transfers between devices, local(): lax.ppermute(b, 'x', [(i, (i + k) % X) for i in range(X)])  11.4 us
    pallas_call x1, Pallas kernels, mask_others(): pl.pallas_call(functools.partial(mask_kernel, n), grid_spec=pltpu.Prefetc...  2.32 us
    all_gather x1, blocking collectives, local(): lax.all_gather(lax.all_to_all(c, ('x', 'y'), 0, 0, tiled=True), 'c', axis=0)  2.17 us
    unnamed x12, local copies, waits for them, and re-layouts  2.1 us
  transfers between devices with their start and end apart: 3, of which 0 were waited for; matrix products, arithmetic and copies ran while one was open for 0% of the time, Pallas kernels for 2%

profile of v3, /device:TPU:8, one launch (start us, length us, event | category | flops | bytes accessed | tf_op | source)
XLA Modules:
  0.0 78.5 jit_solution(12620652623458234796)
XLA Ops:
  0.0 0.1 pad_add_fusion
  0.1 0.0 copy-start
  0.1 1.4 %copy-done = bf16[1,256,3072]{2,1,0:T(8,128)(2,1)S(1)} copy-done((bf16[1,256,3072]{2,1,0:T(8,128)(2,1)S(1)}, bf16[1,256,3072]{2,1,0:T(8,128)(2,1)}, u32[]{:S(2)}) %copy-start) | copy-done | bytes 1572888
  1.5 0.0 copy-start.4
  1.5 0.7 copy-done.4
  2.2 0.0 copy-start.1
  2.2 0.0 copy-start.3
  2.2 0.0 copy-start.5
  2.2 2.3 %mask_others.1 = (bf16[256,768]{1,0:T(8,128)(2,1)}, bf16[256,768]{1,0:T(8,128)(2,1)}, bf16[256,768]{1,0:T(8,128)(2,1)S(1)}) custom-call(s32[2]{0:T(128)S(1)} %get-tuple-element.24.me_ref, s32[2,24]{1,0:T(2,128)S(1)} %bitcast.17, bf16[256,3072]{1,0:T(8,128)(2,1)S(1)} %bitcast.8, bf16[256,3072]{1,0:T(8,128)(2,1)S(1)} %bitcast.9, ...), custom_call_target="tpu_custom_call" | custom-call | tf_op jit(solution)/shard_map/mask_others/pallas_call | solution.py:54
  4.5 3.4 %collective-permute-start = (bf16[256,768]{1,0:T(8,128)(2,1)}, bf16[256,768]{1,0:T(8,128)(2,1)S(1)}, u32[]{:S(2)}, u32[]{:S(2)}) collective-permute-start(bf16[256,768]{1,0:T(8,128)(2,1)} %get-tuple-element.17), channel_id=1, source_target_pairs={{0,6},{6,12},{12,18},{18,0},{1,7},{7,13},{13,19},{19,1},{2,8},{8,1... | collective-permute-start | bytes 1179656 | tf_op jit(solution)/shard_map/ppermute | solution.py:158
  7.9 4.6 %collective-permute-start.1 = (bf16[256,768]{1,0:T(8,128)(2,1)}, bf16[256,768]{1,0:T(8,128)(2,1)S(1)}, u32[]{:S(2)}, u32[]{:S(2)}) collective-permute-start(bf16[256,768]{1,0:T(8,128)(2,1)} %get-tuple-element.18), channel_id=1, source_target_pairs={{0,12},{6,18},{12,0},{18,6},{1,13},{7,19},{13,1},{19,7},{2,14},{8,... | collective-permute-start | bytes 1179656 | tf_op jit(solution)/shard_map/ppermute | solution.py:158
  12.5 3.3 %collective-permute-start.2 = (bf16[256,768]{1,0:T(8,128)(2,1)S(1)}, bf16[256,768]{1,0:T(8,128)(2,1)S(1)}, u32[]{:S(2)}, u32[]{:S(2)}) collective-permute-start(bf16[256,768]{1,0:T(8,128)(2,1)S(1)} %get-tuple-element.19), channel_id=1, source_target_pairs={{0,18},{6,0},{12,6},{18,12},{1,19},{7,1},{13,7},{19,13},{2,20},{8,... | collective-permute-start | bytes 1179656 | tf_op jit(solution)/shard_map/ppermute | solution.py:158
  15.9 0.0 copy-done.1
  15.9 0.0 copy-done.3
  15.9 0.0 copy-done.5
  15.9 1.3 %mask_own.1 = (bf16[256,768]{1,0:T(8,128)(2,1)S(1)}, bf16[32,16,256]{2,1,0:T(8,128)(2,1)S(1)}) custom-call(s32[2]{0:T(128)S(1)} %get-tuple-element.23.me_ref, s32[2,24]{1,0:T(2,128)S(1)} %bitcast.18, bf16[256,3072]{1,0:T(8,128)(2,1)S(1)} %bitcast.14, bf16[256,3072]{1,0:T(8,128)(2,1)S(1)} %bitcast.15, bf16[16,256]{1,0:T(8,128)(2,1)S(1)} %bitcast.16), custom_call_target="tpu_custom_call" | custom-call | tf_op jit(solution)/shard_map/mask_own/pallas_call | solution.py:70
  17.2 24.4 %conditional.1 = (bf16[2,4,8,16,256]{4,3,2,1,0:T(8,128)(2,1)S(1)}) conditional(s32[]{:T(128)} %convert_element_type.3, bf16[32,16,256]{2,1,0:T(8,128)(2,1)S(1)} %get-tuple-element.21, bf16[32,16,256]{2,1,0:T(8,128)(2,1)S(1)} %get-tuple-element.21), branch_computations={%region_0.0_spmd, %region_1.0_spmd} | conditional | bytes 1310728 | solution.py:161
  17.2 22.2 %all_to_all.9 = bf16[32,16,256]{2,1,0:T(8,128)(2,1)S(1)} all-to-all(bf16[32,16,256]{2,1,0:T(8,128)(2,1)S(1)} %param.1), channel_id=1, replica_groups=mesh['y'=8,'c'=2,'zh'=2,'x'=4,'zl'=6] {'x','y'}, dimensions={0} | all-to-all | bytes 524288 | tf_op jit(solution)/shard_map/cond/branch_1_fun/all_to_all | solution.py:163
  39.4 2.2 %all-gather = bf16[64,16,256]{2,1,0:T(8,128)(2,1)S(1)} all-gather(bf16[32,16,256]{2,1,0:T(8,128)(2,1)S(1)} %all_to_all.9), channel_id=2, replica_groups=mesh['y'=8,'c'=2,'zh'=2,'x'=4,'zl'=6] {'c'}, dimensions={0}, use_global_device_ids=true | all-gather | bytes 786432 | tf_op jit(solution)/shard_map/cond/branch_1_fun/all_gather | solution.py:163
  41.6 0.0 collective-permute-done.refs_1_
  41.6 0.0 collective-permute-done.1.refs_2_
  41.6 0.0 collective-permute-done.2.refs_3_
  41.6 0.0 copy-start.2
  41.6 0.9 %product.1 = s16[12,144,128]{2,1,0:T(8,128)(2,1)S(1)} custom-call(s32[1]{0:T(128)} %bitcast.2.me_ref, bf16[2,4,8,16,256]{4,3,2,1,0:T(8,128)(2,1)S(1)} %get-tuple-element.25.f_ref, bf16[256,768]{1,0:T(8,128)(2,1)S(1)} %get-tuple-element.22.refs_0_, bf16[256,768]{1,0:T(8,128)(2,1)S(1)} %collective-permute-done.refs_1_, ...), custom_call_target="tpu_custom_call" | custom-call | tf_op jit(solution)/shard_map/product/pallas_call | solution.py:123
  42.5 34.7 %all_to_all.10.q_ref = s16[12,144,128]{2,1,0:T(8,128)(2,1)S(1)} all-to-all(s16[12,144,128]{2,1,0:T(8,128)(2,1)S(1)} %product.1), channel_id=1, replica_groups=mesh['y'=8,'c'=2,'zh'=2,'x'=4,'zl'=6] {'zh','zl'}, dimensions={0} | all-to-all | bytes 884736 | tf_op jit(solution)/shard_map/all_to_all | solution.py:168
  77.3 0.0 copy-done.2
  77.3 1.2 %finish.1 = f32[64,256]{1,0:T(8,128)} custom-call(s16[12,144,128]{2,1,0:T(8,128)(2,1)S(1)} %all_to_all.10.q_ref, bf16[64,256]{1,0:T(8,128)(2,1)S(1)} %copy-done.2), custom_call_target="tpu_custom_call" | custom-call | tf_op jit(solution)/shard_map/finish/pallas_call | solution.py:147
Async XLA Ops:
  0.1 1.4 %copy-start = (bf16[1,256,3072]{2,1,0:T(8,128)(2,1)S(1)}, bf16[1,256,3072]{2,1,0:T(8,128)(2,1)}, u32[]{:S(2)}) copy-start(bf16[1,256,3072]{2,1,0:T(8,128)(2,1)} %param.6) | copy-start | bytes 4718596
  1.5 0.7 copy-start.4
  2.2 13.7 %copy-start.1 = (bf16[1,256,3072]{2,1,0:T(8,128)(2,1)S(1)}, bf16[1,256,3072]{2,1,0:T(8,128)(2,1)}, u32[]{:S(2)}) copy-start(bf16[1,256,3072]{2,1,0:T(8,128)(2,1)} %param.6) | copy-start | bytes 4718596
  2.2 13.7 %copy-start.3 = (bf16[1,256,16]{1,2,0:T(8,128)(2,1)S(1)}, bf16[1,256,16]{1,2,0:T(8,128)(2,1)}, u32[]{:S(2)}) copy-start(bf16[1,256,16]{1,2,0:T(8,128)(2,1)} %param.8) | copy-start | bytes 24580
  2.2 13.7 %copy-start.5 = (s32[1,2,24]{2,1,0:T(2,128)S(1)}, s32[1,2,24]{2,1,0:T(2,128)}, u32[]{:S(2)}) copy-start(s32[1,2,24]{2,1,0:T(2,128)} %param.7) | copy-start | bytes 580
  4.5 37.1 %collective-permute-start = (bf16[256,768]{1,0:T(8,128)(2,1)}, bf16[256,768]{1,0:T(8,128)(2,1)S(1)}, u32[]{:S(2)}, u32[]{:S(2)}) collective-permute-start(bf16[256,768]{1,0:T(8,128)(2,1)} %get-tuple-element.17), channel_id=1, source_target_pairs={{0,6},{6,12},{12,18},{18,0},{1,7},{7,13},{13,19},{19,1},{2,8},{8,1... | collective-permute-start | bytes 1179656 | tf_op jit(solution)/shard_map/ppermute | solution.py:158
  7.9 33.7 %collective-permute-start.1 = (bf16[256,768]{1,0:T(8,128)(2,1)}, bf16[256,768]{1,0:T(8,128)(2,1)S(1)}, u32[]{:S(2)}, u32[]{:S(2)}) collective-permute-start(bf16[256,768]{1,0:T(8,128)(2,1)} %get-tuple-element.18), channel_id=1, source_target_pairs={{0,12},{6,18},{12,0},{18,6},{1,13},{7,19},{13,1},{19,7},{2,14},{8,... | collective-permute-start | bytes 1179656 | tf_op jit(solution)/shard_map/ppermute | solution.py:158
  12.5 29.1 %collective-permute-start.2 = (bf16[256,768]{1,0:T(8,128)(2,1)S(1)}, bf16[256,768]{1,0:T(8,128)(2,1)S(1)}, u32[]{:S(2)}, u32[]{:S(2)}) collective-permute-start(bf16[256,768]{1,0:T(8,128)(2,1)S(1)} %get-tuple-element.19), channel_id=1, source_target_pairs={{0,18},{6,0},{12,6},{18,12},{1,19},{7,1},{13,7},{19,13},{2,20},{8,... | collective-permute-start | bytes 1179656 | tf_op jit(solution)/shard_map/ppermute | solution.py:158
  41.6 35.7 %copy-start.2 = (bf16[64,256]{1,0:T(8,128)(2,1)S(1)}, bf16[64,256]{1,0:T(8,128)(2,1)}, u32[]{:S(2)}) copy-start(bf16[64,256]{1,0:T(8,128)(2,1)} %t_ref.1) | copy-start | bytes 98308

commit v4 on v2

--- a/solution.py
+++ b/solution.py
@@ -22,69 +22,58 @@
 STEP = 8.0
 TOP = 32000.0
 MIB = 1 << 20
+LIMIT = 60
 
 
-def mask_kernel(n, me_ref, mask_ref, *refs):
-    i = pl.program_id(0)
-    for k in range(n):
-        for zh in range(ZH):
-            a_ref = refs[k * ZH + zh]
-            first = (zh * X + lax.rem(me_ref[0] + me_ref[1] + k, X)) * (SEG // TILE)
+def mask_kernel(steps, mask_hbm, a_hbm, *refs):
+    n = len(steps)
+    o_refs, (mask_ref, a_ref, sems) = refs[:n], refs[-3:]
+    me = lax.axis_index("x")
+    mask_copy = pltpu.make_async_copy(mask_hbm, mask_ref, sems.at[0])
+    mask_copy.start()
+    copies = []
+    for b, (k, zh) in enumerate((k, zh) for k in steps for zh in range(ZH)):
+        first = (zh * X + lax.rem(me + k, X)) * (SEG // TILE)
+        columns = pl.ds(pl.multiple_of(first * TILE, TILE), SEG)
+        copy = pltpu.make_async_copy(a_hbm.at[:, columns], a_ref.at[b], sems.at[1 + b])
+        copy.start()
+        copies.append((b, zh, first, copy))
+    mask_copy.wait()
+    for b, zh, first, copy in copies:
+        copy.wait()
+        for i in range(SRC // TILE):
+            rows = slice(i * TILE, (i + 1) * TILE)
             for p in range(SEG // TILE):
                 keep = mask_ref[i, first + p].astype(jnp.float32)
-                tile = a_ref[:, p * TILE : (p + 1) * TILE].astype(jnp.float32) * keep
+                tile = a_ref[b, rows, p * TILE : (p + 1) * TILE].astype(jnp.float32) * keep
                 to = zh * SEG + p * TILE
-                refs[n * ZH + k][:, to : to + TILE] = tile.astype(jnp.bfloat16)
+                o_refs[b // ZH][rows, to : to + TILE] = tile.astype(jnp.bfloat16)
 
 
-def own_kernel(me_ref, mask_ref, a0_ref, a1_ref, f_ref, o_ref, copies_ref):
-    mask_kernel(1, me_ref, mask_ref, a0_ref, a1_ref, o_ref)
-    copies_ref[...] = jnp.broadcast_to(f_ref[...][None], copies_ref.shape)
+def spread_kernel(steps, mask_hbm, a_hbm, f_ref, *refs):
+    n = len(steps)
+    refs[n][...] = jnp.broadcast_to(f_ref[...][None], refs[n].shape)
+    mask_kernel(steps, mask_hbm, a_hbm, *refs[:n], *refs[n + 1 :])
 
 
-def mask_specs(n, first):
-    def segment(k, zh):
-        return pl.BlockSpec((TILE, SEG), lambda i, me: (i, zh * X + lax.rem(me[0] + first + k, X)))
-
-    return [pl.BlockSpec(memory_space=pltpu.SMEM)] + [segment(k, zh) for k in range(n) for zh in range(ZH)]
-
-
-def mask_others(me, mask, a):
-    n = X - 1
+def mask_blocks(steps, mask, a, feats=None):
+    n = len(steps)
+    whole = pl.BlockSpec(memory_space=pltpu.VMEM)
+    more = [] if feats is None else [feats]
     return pl.pallas_call(
-        functools.partial(mask_kernel, n),
-        grid_spec=pltpu.PrefetchScalarGridSpec(
-            num_scalar_prefetch=1,
-            grid=(SRC // TILE,),
-            in_specs=mask_specs(n, 1),
-            out_specs=[pl.BlockSpec((TILE, TGT), lambda i, me: (i, 0))] * n,
-        ),
-        out_shape=[jax.ShapeDtypeStruct((SRC, TGT), jnp.bfloat16)] * n,
-        compiler_params=pltpu.CompilerParams(vmem_limit_bytes=16 * MIB),
-        name="mask_others",
-    )(jnp.stack([me, jnp.int32(1)]), mask, *[a] * (n * ZH))
-
-
-def mask_own(me, mask, a, feats):
-    half = X * Y * TILE // SRC
-    return pl.pallas_call(
-        own_kernel,
-        grid_spec=pltpu.PrefetchScalarGridSpec(
-            num_scalar_prefetch=1,
-            grid=(SRC // TILE,),
-            in_specs=mask_specs(1, 0) + [pl.BlockSpec((HELD, SRC), lambda i, me: (0, 0))],
-            out_specs=[
-                pl.BlockSpec((TILE, TGT), lambda i, me: (i, 0)),
-                pl.BlockSpec((half, HELD, SRC), lambda i, me: (i, 0, 0)),
-            ],
-        ),
-        out_shape=[
-            jax.ShapeDtypeStruct((SRC, TGT), jnp.bfloat16),
-            jax.ShapeDtypeStruct((X * Y, HELD, SRC), jnp.bfloat16),
+        functools.partial(spread_kernel if more else mask_kernel, steps),
+        in_specs=[pl.BlockSpec(memory_space=pl.ANY)] * 2 + [whole] * len(more),
+        out_specs=[whole] * (n + len(more)),
+        out_shape=[jax.ShapeDtypeStruct((SRC, TGT), jnp.bfloat16)] * n
+        + [jax.ShapeDtypeStruct((X * Y, HELD, SRC), jnp.bfloat16)] * len(more),
+        scratch_shapes=[
+            pltpu.SMEM(mask.shape, jnp.int32),
+            pltpu.VMEM((n * ZH, SRC, SEG), jnp.bfloat16),
+            pltpu.SemaphoreType.DMA((1 + n * ZH,)),
         ],
-        compiler_params=pltpu.CompilerParams(vmem_limit_bytes=16 * MIB),
-        name="mask_own",
-    )(jnp.stack([me, jnp.int32(0)]), mask, a, a, feats)
+        compiler_params=pltpu.CompilerParams(vmem_limit_bytes=LIMIT * MIB),
+        name="mask_blocks",
+    )(mask, a, *more)
 
 
 def product_kernel(me_ref, f_ref, *refs):
@@ -152,16 +141,22 @@
     )(coded, teleport)
 
 
+def gather(copies):
+    return lax.all_gather(lax.all_to_all(copies, ("x", "y"), 0, 0, tiled=True), "c", axis=0)
+
+
+def shift(block, k):
+    return lax.ppermute(block, "x", [(i, (i + k) % X) for i in range(X)])
+
+
 def local(propagation, tile_mask, features, teleport):
+    mask, a, feats = tile_mask[0], propagation[0], features[0].T
+    (far,) = mask_blocks((2,), mask, a)
+    up, down, own, copies = mask_blocks((1, 3, 0), mask, a, lax.optimization_barrier((feats, far))[0])
+    blocks = [own, shift(up, 1), shift(far, 2), shift(down, 3)]
     me = lax.axis_index("x").astype(jnp.int32)
-    others = mask_others(me, tile_mask[0], propagation[0])
-    blocks = [lax.ppermute(b, "x", [(i, (i + k) % X) for i in range(X)]) for k, b in enumerate(others, 1)]
-    mine = lax.optimization_barrier((features[0].T, *others))[0]
-    own, copies = mask_own(me, tile_mask[0], propagation[0], mine)
-    copies, blocks[0] = lax.optimization_barrier((copies, blocks[0]))
-    feats = lax.all_to_all(copies, ("x", "y"), 0, 0, tiled=True)
-    feats = lax.all_gather(feats, "c", axis=0).reshape(CORES, X, Y, HELD, SRC)
-    coded = product(me[None], feats, [own, *blocks])
+    feats = lax.cond(me < X, gather, lambda c: jnp.stack([c] * CORES), copies)
+    coded = product(me[None], feats.reshape(CORES, X, Y, HELD, SRC), blocks)
     coded = lax.all_to_all(coded, ("zh", "zl"), 0, 0, tiled=True)
     return finish(coded, teleport)
 

time: 90.3 us -> 78.8 us (0.87)
  the two profiles are of different devices: /device:TPU:2 before, /device:TPU:8 now
where the time goes in v4:
time: 78.8 us; the launch traced here: 78.4 us
  blocking collectives  59.1 us (75%)
  starting transfers between devices  12.1 us (15%)
  Pallas kernels  7.12 us (9%)
    all_to_all x1, blocking collectives, local(): coded = lax.all_to_all(coded, ('zh', 'zl'), 0, 0, tiled=True)  35.9 us
    all_to_all x1, blocking collectives, gather(): lax.all_to_all(copies, ('x', 'y'), 0, 0, tiled=True)  21 us
    ppermute x3, starting transfers between devices, shift(): return lax.ppermute(block, 'x', [(i, (i + k) % X) for i in range(X)])  12.1 us
    pallas_call x2, Pallas kernels, mask_blocks(): pl.pallas_call(functools.partial(spread_kernel if more else mask_kernel,...  5.01 us
    all_gather x1, blocking collectives, gather(): lax.all_gather(lax.all_to_all(copies, ('x', 'y'), 0, 0, tiled=True), 'c',...  2.17 us
  transfers between devices with their start and end apart: 3, of which 0 were waited for; matrix products, arithmetic and copies ran while one was open for 0% of the time, Pallas kernels for 4%

profile of v4, /device:TPU:8, one launch (start us, length us, event | category | flops | bytes accessed | tf_op | source)
XLA Modules:
  0.0 78.4 jit_solution(8017337453869205057)
XLA Ops:
  0.0 1.8 %mask_blocks.2 = bf16[256,768]{1,0:T(8,128)(2,1)} custom-call(s32[2,24]{1,0:T(2,128)} %bitcast.13, bf16[256,3072]{1,0:T(8,128)(2,1)} %bitcast.8), custom_call_target="tpu_custom_call" | custom-call | tf_op jit(solution)/shard_map/mask_blocks/pallas_call | solution.py:63
  1.9 4.9 %collective-permute-start.1 = (bf16[256,768]{1,0:T(8,128)(2,1)}, bf16[256,768]{1,0:T(8,128)(2,1)S(1)}, u32[]{:S(2)}, u32[]{:S(2)}) collective-permute-start(bf16[256,768]{1,0:T(8,128)(2,1)} %mask_blocks.2), channel_id=1, source_target_pairs={{0,12},{6,18},{12,0},{18,6},{1,13},{7,19},{13,1},{19,7},{2,14},{8,... | collective-permute-start | bytes 1179656 | tf_op jit(solution)/shard_map/ppermute | solution.py:149
  6.8 3.2 %mask_blocks.3 = (bf16[256,768]{1,0:T(8,128)(2,1)}, bf16[256,768]{1,0:T(8,128)(2,1)}, bf16[256,768]{1,0:T(8,128)(2,1)}, bf16[32,16,256]{2,1,0:T(8,128)(2,1)S(1)}) custom-call(s32[2,24]{1,0:T(2,128)} %bitcast.14, bf16[256,3072]{1,0:T(8,128)(2,1)} %bitcast.9, bf16[16,256]{1,0:T(8,128)(2,1)} %bitcast.12), custom_call_target="tpu_custom_call" | custom-call | tf_op jit(solution)/shard_map/mask_blocks/pallas_call | solution.py:63
  10.0 0.0 copy-start
  10.0 2.6 %collective-permute-start = (bf16[256,768]{1,0:T(8,128)(2,1)}, bf16[256,768]{1,0:T(8,128)(2,1)S(1)}, u32[]{:S(2)}, u32[]{:S(2)}) collective-permute-start(bf16[256,768]{1,0:T(8,128)(2,1)} %get-tuple-element.19), channel_id=1, source_target_pairs={{0,6},{6,12},{12,18},{18,0},{1,7},{7,13},{13,19},{19,1},{2,8},{8,1... | collective-permute-start | bytes 1179656 | tf_op jit(solution)/shard_map/ppermute | solution.py:149
  12.6 4.6 %collective-permute-start.2 = (bf16[256,768]{1,0:T(8,128)(2,1)}, bf16[256,768]{1,0:T(8,128)(2,1)S(1)}, u32[]{:S(2)}, u32[]{:S(2)}) collective-permute-start(bf16[256,768]{1,0:T(8,128)(2,1)} %get-tuple-element.20), channel_id=1, source_target_pairs={{0,18},{6,0},{12,6},{18,12},{1,19},{7,1},{13,7},{19,13},{2,20},{8,... | collective-permute-start | bytes 1179656 | tf_op jit(solution)/shard_map/ppermute | solution.py:149
  17.2 23.1 %conditional.1 = (bf16[2,4,8,16,256]{4,3,2,1,0:T(8,128)(2,1)S(1)}) conditional(s32[]{:T(128)} %convert_element_type.3, bf16[32,16,256]{2,1,0:T(8,128)(2,1)S(1)} %get-tuple-element.17, bf16[32,16,256]{2,1,0:T(8,128)(2,1)S(1)} %get-tuple-element.17), branch_computations={%region_0.0_spmd, %region_1.0_spmd} | conditional | bytes 1310728 | solution.py:158
  17.2 21.0 %all_to_all.9 = bf16[32,16,256]{2,1,0:T(8,128)(2,1)S(1)} all-to-all(bf16[32,16,256]{2,1,0:T(8,128)(2,1)S(1)} %param.1), channel_id=1, replica_groups=mesh['y'=8,'c'=2,'zh'=2,'x'=4,'zl'=6] {'x','y'}, dimensions={0} | all-to-all | bytes 524288 | tf_op jit(solution)/shard_map/cond/branch_1_fun/all_to_all | solution.py:145
  38.2 2.2 %all-gather = bf16[64,16,256]{2,1,0:T(8,128)(2,1)S(1)} all-gather(bf16[32,16,256]{2,1,0:T(8,128)(2,1)S(1)} %all_to_all.9), channel_id=2, replica_groups=mesh['y'=8,'c'=2,'zh'=2,'x'=4,'zl'=6] {'c'}, dimensions={0}, use_global_device_ids=true | all-gather | bytes 786432 | tf_op jit(solution)/shard_map/cond/branch_1_fun/all_gather | solution.py:145
  40.3 0.0 collective-permute-done.1.refs_2_
  40.3 0.0 collective-permute-done.refs_1_
  40.3 0.0 collective-permute-done.2.refs_3_
  40.3 0.0 copy-done
  40.4 0.0 copy-start.1
  40.4 0.9 %product.1 = s16[12,144,128]{2,1,0:T(8,128)(2,1)S(1)} custom-call(s32[1]{0:T(128)} %bitcast.2.me_ref, bf16[2,4,8,16,256]{4,3,2,1,0:T(8,128)(2,1)S(1)} %get-tuple-element.21.f_ref, bf16[256,768]{1,0:T(8,128)(2,1)S(1)} %copy-done, bf16[256,768]{1,0:T(8,128)(2,1)S(1)} %collective-permute-done.refs_1_, bf16[256,768]{1,0:T(8,128)(2,1)S(1)} %collective-permute-done.1.refs_2_, ...), custom_call_target="tpu_custom_call" | custom-call | tf_op jit(solution)/shard_map/product/pallas_call | solution.py:112
  41.3 35.9 %all_to_all.10.q_ref = s16[12,144,128]{2,1,0:T(8,128)(2,1)S(1)} all-to-all(s16[12,144,128]{2,1,0:T(8,128)(2,1)S(1)} %product.1), channel_id=1, replica_groups=mesh['y'=8,'c'=2,'zh'=2,'x'=4,'zl'=6] {'zh','zl'}, dimensions={0} | all-to-all | bytes 884736 | tf_op jit(solution)/shard_map/all_to_all | solution.py:160
  77.2 0.0 copy-done.1
  77.2 1.2 %finish.1 = f32[64,256]{1,0:T(8,128)} custom-call(s16[12,144,128]{2,1,0:T(8,128)(2,1)S(1)} %all_to_all.10.q_ref, bf16[64,256]{1,0:T(8,128)(2,1)S(1)} %copy-done.1), custom_call_target="tpu_custom_call" | custom-call | tf_op jit(solution)/shard_map/finish/pallas_call | solution.py:136
Async XLA Ops:
  1.9 38.5 %collective-permute-start.1 = (bf16[256,768]{1,0:T(8,128)(2,1)}, bf16[256,768]{1,0:T(8,128)(2,1)S(1)}, u32[]{:S(2)}, u32[]{:S(2)}) collective-permute-start(bf16[256,768]{1,0:T(8,128)(2,1)} %mask_blocks.2), channel_id=1, source_target_pairs={{0,12},{6,18},{12,0},{18,6},{1,13},{7,19},{13,1},{19,7},{2,14},{8,... | collective-permute-start | bytes 1179656 | tf_op jit(solution)/shard_map/ppermute | solution.py:149
  10.0 30.4 %copy-start = (bf16[256,768]{1,0:T(8,128)(2,1)S(1)}, bf16[256,768]{1,0:T(8,128)(2,1)}, u32[]{:S(2)}) copy-start(bf16[256,768]{1,0:T(8,128)(2,1)} %get-tuple-element.18.refs_0_) | copy-start | bytes 1179652
  10.0 30.4 %collective-permute-start = (bf16[256,768]{1,0:T(8,128)(2,1)}, bf16[256,768]{1,0:T(8,128)(2,1)S(1)}, u32[]{:S(2)}, u32[]{:S(2)}) collective-permute-start(bf16[256,768]{1,0:T(8,128)(2,1)} %get-tuple-element.19), channel_id=1, source_target_pairs={{0,6},{6,12},{12,18},{18,0},{1,7},{7,13},{13,19},{19,1},{2,8},{8,1... | collective-permute-start | bytes 1179656 | tf_op jit(solution)/shard_map/ppermute | solution.py:149
  12.6 27.7 %collective-permute-start.2 = (bf16[256,768]{1,0:T(8,128)(2,1)}, bf16[256,768]{1,0:T(8,128)(2,1)S(1)}, u32[]{:S(2)}, u32[]{:S(2)}) collective-permute-start(bf16[256,768]{1,0:T(8,128)(2,1)} %get-tuple-element.20), channel_id=1, source_target_pairs={{0,18},{6,0},{12,6},{18,12},{1,19},{7,1},{13,7},{19,13},{2,20},{8,... | collective-permute-start | bytes 1179656 | tf_op jit(solution)/shard_map/ppermute | solution.py:149
  40.4 36.8 %copy-start.1 = (bf16[64,256]{1,0:T(8,128)(2,1)S(1)}, bf16[64,256]{1,0:T(8,128)(2,1)}, u32[]{:S(2)}) copy-start(bf16[64,256]{1,0:T(8,128)(2,1)} %t_ref.1) | copy-start | bytes 98308

commit v5 on v4

--- a/solution.py
+++ b/solution.py
@@ -22,7 +22,6 @@
 STEP = 8.0
 TOP = 32000.0
 MIB = 1 << 20
-LIMIT = 60
 
 
 def mask_kernel(steps, mask_hbm, a_hbm, *refs):
@@ -44,10 +43,9 @@
         for i in range(SRC // TILE):
             rows = slice(i * TILE, (i + 1) * TILE)
             for p in range(SEG // TILE):
-                keep = mask_ref[i, first + p].astype(jnp.float32)
-                tile = a_ref[b, rows, p * TILE : (p + 1) * TILE].astype(jnp.float32) * keep
+                tile = a_ref[b, rows, p * TILE : (p + 1) * TILE]
                 to = zh * SEG + p * TILE
-                o_refs[b // ZH][rows, to : to + TILE] = tile.astype(jnp.bfloat16)
+                o_refs[b // ZH][rows, to : to + TILE] = jnp.where(mask_ref[i, first + p] != 0, tile, 0)
 
 
 def spread_kernel(steps, mask_hbm, a_hbm, f_ref, *refs):
@@ -56,7 +54,7 @@
     mask_kernel(steps, mask_hbm, a_hbm, *refs[:n], *refs[n + 1 :])
 
 
-def mask_blocks(steps, mask, a, feats=None):
+def mask_blocks(steps, mask, a, feats=None, limit=60):
     n = len(steps)
     whole = pl.BlockSpec(memory_space=pltpu.VMEM)
     more = [] if feats is None else [feats]
@@ -71,7 +69,7 @@
             pltpu.VMEM((n * ZH, SRC, SEG), jnp.bfloat16),
             pltpu.SemaphoreType.DMA((1 + n * ZH,)),
         ],
-        compiler_params=pltpu.CompilerParams(vmem_limit_bytes=LIMIT * MIB),
+        compiler_params=pltpu.CompilerParams(vmem_limit_bytes=limit * MIB),
         name="mask_blocks",
     )(mask, a, *more)
 
@@ -141,22 +139,22 @@
     )(coded, teleport)
 
 
-def gather(copies):
-    return lax.all_gather(lax.all_to_all(copies, ("x", "y"), 0, 0, tiled=True), "c", axis=0)
-
-
 def shift(block, k):
     return lax.ppermute(block, "x", [(i, (i + k) % X) for i in range(X)])
 
 
 def local(propagation, tile_mask, features, teleport):
-    mask, a, feats = tile_mask[0], propagation[0], features[0].T
-    (far,) = mask_blocks((2,), mask, a)
-    up, down, own, copies = mask_blocks((1, 3, 0), mask, a, lax.optimization_barrier((feats, far))[0])
+    mask, a = tile_mask[0], propagation[0]
+    far, copies = mask_blocks((2,), mask, a, features[0].T)
+    feats = lax.all_to_all(copies, ("x", "y"), 0, 0, tiled=True)
+    feats = lax.all_gather(feats, "c", axis=0).reshape(CORES, X, Y, HELD, SRC)
+    near_a, _ = lax.optimization_barrier((a, far))
+    up, down = mask_blocks((1, 3), mask, near_a, limit=16)
+    own_a, _ = lax.optimization_barrier((a, up))
+    (own,) = mask_blocks((0,), mask, own_a, limit=16)
     blocks = [own, shift(up, 1), shift(far, 2), shift(down, 3)]
     me = lax.axis_index("x").astype(jnp.int32)
-    feats = lax.cond(me < X, gather, lambda c: jnp.stack([c] * CORES), copies)
-    coded = product(me[None], feats.reshape(CORES, X, Y, HELD, SRC), blocks)
+    coded = product(me[None], feats, blocks)
     coded = lax.all_to_all(coded, ("zh", "zl"), 0, 0, tiled=True)
     return finish(coded, teleport)
 

time: 78.8 us -> 77.7 us (0.986)
  the two profiles are of different devices: /device:TPU:8 before, /device:TPU:2 now
where the time goes in v5:
time: 77.7 us; the launch traced here: 77.3 us
  blocking collectives  40 us (51%)
  starting transfers between devices  23.7 us (31%)
  Pallas kernels  7.07 us (9%)
  waiting for transfers between devices  6.38 us (8%)
    all_to_all x1, blocking collectives, local(): coded = lax.all_to_all(coded, ('zh', 'zl'), 0, 0, tiled=True)  37.6 us
    all_to_all x1, starting transfers between devices, local(): feats = lax.all_to_all(copies, ('x', 'y'), 0, 0, tiled=True)  13.8 us
    ppermute x3, starting transfers between devices, shift(): return lax.ppermute(block, 'x', [(i, (i + k) % X) for i in range(X)])  9.93 us
    ppermute x3, waiting for transfers between devices, shift(): return lax.ppermute(block, 'x', [(i, (i + k) % X) for i in range(X)])  6.38 us
    pallas_call x3, Pallas kernels, mask_blocks(): pl.pallas_call(functools.partial(spread_kernel if more else mask_kernel,...  4.96 us
    all_gather x1, blocking collectives, local(): feats = lax.all_gather(feats, 'c', axis=0).reshape(CORES, X, Y, HELD, SRC)  2.39 us
  transfers between devices with their start and end apart: 4, of which 2 were waited for; matrix products, arithmetic and copies ran while one was open for 0% of the time, Pallas kernels for 3%

profile of v5, /device:TPU:2, one launch (start us, length us, event | category | flops | bytes accessed | tf_op | source)
XLA Modules:
  0.0 77.3 jit_solution(13179774729139372167)
XLA Ops:
  0.0 0.0 copy-start.2
  0.0 0.0 copy-start
  0.0 2.8 %mask_blocks.3 = (bf16[256,768]{1,0:T(8,128)(2,1)}, bf16[32,16,256]{2,1,0:T(8,128)(2,1)}) custom-call(s32[2,24]{1,0:T(2,128)} %bitcast.11, bf16[256,3072]{1,0:T(8,128)(2,1)} %bitcast.7, bf16[16,256]{1,0:T(8,128)(2,1)} %bitcast.14), custom_call_target="tpu_custom_call" | custom-call | tf_op jit(solution)/shard_map/mask_blocks/pallas_call | solution.py:61
  2.8 13.8 %all-to-all-start = ((bf16[32,16,256]{2,1,0:T(8,128)(2,1)}), bf16[32,16,256]{2,1,0:T(8,128)(2,1)}, u32[]{:S(2)}, u32[]{:S(2)}) async-start(bf16[32,16,256]{2,1,0:T(8,128)(2,1)} %get-tuple-element.11), calls=%async_computation | async-start | bytes 524288 | tf_op jit(solution)/shard_map/all_to_all | solution.py:149
  16.6 4.1 %collective-permute-start.1 = (bf16[256,768]{1,0:T(8,128)(2,1)}, bf16[256,768]{1,0:T(8,128)(2,1)S(1)}, u32[]{:S(2)}, u32[]{:S(2)}) collective-permute-start(bf16[256,768]{1,0:T(8,128)(2,1)} %get-tuple-element.12), channel_id=1, source_target_pairs={{0,12},{6,18},{12,0},{18,6},{1,13},{7,19},{13,1},{19,7},{2,14},{8,... | collective-permute-start | bytes 1179656 | tf_op jit(solution)/shard_map/ppermute | solution.py:143
  20.7 0.0 copy-done.2
  20.7 0.0 copy-done
  20.7 1.5 %mask_blocks.4 = (bf16[256,768]{1,0:T(8,128)(2,1)S(1)}, bf16[256,768]{1,0:T(8,128)(2,1)}) custom-call(s32[2,24]{1,0:T(2,128)S(1)} %bitcast.12, bf16[256,3072]{1,0:T(8,128)(2,1)S(1)} %bitcast.8), custom_call_target="tpu_custom_call" | custom-call | tf_op jit(solution)/shard_map/mask_blocks/pallas_call | solution.py:61
  22.2 3.3 %collective-permute-start.2 = (bf16[256,768]{1,0:T(8,128)(2,1)}, bf16[256,768]{1,0:T(8,128)(2,1)S(1)}, u32[]{:S(2)}, u32[]{:S(2)}) collective-permute-start(bf16[256,768]{1,0:T(8,128)(2,1)} %get-tuple-element.16), channel_id=1, source_target_pairs={{0,18},{6,0},{12,6},{18,12},{1,19},{7,1},{13,7},{19,13},{2,20},{8,... | collective-permute-start | bytes 1179656 | tf_op jit(solution)/shard_map/ppermute | solution.py:143
  25.5 2.5 %collective-permute-start = (bf16[256,768]{1,0:T(8,128)(2,1)S(1)}, bf16[256,768]{1,0:T(8,128)(2,1)S(1)}, u32[]{:S(2)}, u32[]{:S(2)}) collective-permute-start(bf16[256,768]{1,0:T(8,128)(2,1)S(1)} %get-tuple-element.14), channel_id=1, source_target_pairs={{0,6},{6,12},{12,18},{18,0},{1,7},{7,13},{13,19},{19,1},{2,8},{8,1... | collective-permute-start | bytes 1179656 | tf_op jit(solution)/shard_map/ppermute | solution.py:143
  28.1 0.7 mask_blocks.5.refs_0_
  28.8 0.0 all-to-all-done
  28.8 2.4 %all-gather = bf16[64,16,256]{2,1,0:T(8,128)(2,1)S(1)} all-gather(bf16[32,16,256]{2,1,0:T(8,128)(2,1)} %all-to-all-done), channel_id=2, replica_groups=mesh['y'=8,'c'=2,'zh'=2,'x'=4,'zl'=6] {'c'}, dimensions={0}, use_global_device_ids=true | all-gather | bytes 786432 | tf_op jit(solution)/shard_map/all_gather | solution.py:150
  31.2 1.8 %collective-permute-done.1.refs_2_ = bf16[256,768]{1,0:T(8,128)(2,1)S(1)} collective-permute-done((bf16[256,768]{1,0:T(8,128)(2,1)}, bf16[256,768]{1,0:T(8,128)(2,1)S(1)}, u32[]{:S(2)}, u32[]{:S(2)}) %collective-permute-start.1) | collective-permute-done | bytes 393248 | tf_op jit(solution)/shard_map/ppermute | solution.py:143
  32.9 4.6 %collective-permute-done.2.refs_3_ = bf16[256,768]{1,0:T(8,128)(2,1)S(1)} collective-permute-done((bf16[256,768]{1,0:T(8,128)(2,1)}, bf16[256,768]{1,0:T(8,128)(2,1)S(1)}, u32[]{:S(2)}, u32[]{:S(2)}) %collective-permute-start.2) | collective-permute-done | bytes 393248 | tf_op jit(solution)/shard_map/ppermute | solution.py:143
  37.5 0.0 collective-permute-done.refs_1_
  37.5 0.0 copy-start.1
  37.5 0.9 %product.1 = s16[12,144,128]{2,1,0:T(8,128)(2,1)S(1)} custom-call(s32[1]{0:T(128)} %bitcast.me_ref, bf16[2,4,8,16,256]{4,3,2,1,0:T(8,128)(2,1)S(1)} %bitcast.10, bf16[256,768]{1,0:T(8,128)(2,1)S(1)} %mask_blocks.5.refs_0_, bf16[256,768]{1,0:T(8,128)(2,1)S(1)} %collective-permute-done.refs_1_, bf16[256,768]{1,0:T(8,128)(2,1)S(1)} %collective-permute-done.1.refs_2_, ...), custom_call_target="tpu_custom_call" | custom-call | tf_op jit(solution)/shard_map/product/pallas_call | solution.py:110
  38.5 37.6 %all_to_all.10.q_ref = s16[12,144,128]{2,1,0:T(8,128)(2,1)S(1)} all-to-all(s16[12,144,128]{2,1,0:T(8,128)(2,1)S(1)} %product.1), channel_id=1, replica_groups=mesh['y'=8,'c'=2,'zh'=2,'x'=4,'zl'=6] {'zh','zl'}, dimensions={0} | all-to-all | bytes 884736 | tf_op jit(solution)/shard_map/all_to_all | solution.py:158
  76.1 0.0 copy-done.1
  76.1 1.2 %finish.1 = f32[64,256]{1,0:T(8,128)} custom-call(s16[12,144,128]{2,1,0:T(8,128)(2,1)S(1)} %all_to_all.10.q_ref, bf16[64,256]{1,0:T(8,128)(2,1)S(1)} %copy-done.1), custom_call_target="tpu_custom_call" | custom-call | tf_op jit(solution)/shard_map/finish/pallas_call | solution.py:134
Async XLA Ops:
  0.0 20.7 %copy-start.2 = (s32[1,2,24]{2,1,0:T(2,128)S(1)}, s32[1,2,24]{2,1,0:T(2,128)}, u32[]{:S(2)}) copy-start(s32[1,2,24]{2,1,0:T(2,128)} %param.5) | copy-start | bytes 580
  0.0 20.7 %copy-start = (bf16[1,256,3072]{2,1,0:T(8,128)(2,1)S(1)}, bf16[1,256,3072]{2,1,0:T(8,128)(2,1)}, u32[]{:S(2)}) copy-start(bf16[1,256,3072]{2,1,0:T(8,128)(2,1)} %param.4) | copy-start | bytes 4718596
  2.8 26.0 %all-to-all-start = ((bf16[32,16,256]{2,1,0:T(8,128)(2,1)}), bf16[32,16,256]{2,1,0:T(8,128)(2,1)}, u32[]{:S(2)}, u32[]{:S(2)}) async-start(bf16[32,16,256]{2,1,0:T(8,128)(2,1)} %get-tuple-element.11), calls=%async_computation | async-start | bytes 524288 | tf_op jit(solution)/shard_map/all_to_all | solution.py:149
  16.6 16.4 %collective-permute-start.1 = (bf16[256,768]{1,0:T(8,128)(2,1)}, bf16[256,768]{1,0:T(8,128)(2,1)S(1)}, u32[]{:S(2)}, u32[]{:S(2)}) collective-permute-start(bf16[256,768]{1,0:T(8,128)(2,1)} %get-tuple-element.12), channel_id=1, source_target_pairs={{0,12},{6,18},{12,0},{18,6},{1,13},{7,19},{13,1},{19,7},{2,14},{8,... | collective-permute-start | bytes 1179656 | tf_op jit(solution)/shard_map/ppermute | solution.py:143
  22.2 15.3 %collective-permute-start.2 = (bf16[256,768]{1,0:T(8,128)(2,1)}, bf16[256,768]{1,0:T(8,128)(2,1)S(1)}, u32[]{:S(2)}, u32[]{:S(2)}) collective-permute-start(bf16[256,768]{1,0:T(8,128)(2,1)} %get-tuple-element.16), channel_id=1, source_target_pairs={{0,18},{6,0},{12,6},{18,12},{1,19},{7,1},{13,7},{19,13},{2,20},{8,... | collective-permute-start | bytes 1179656 | tf_op jit(solution)/shard_map/ppermute | solution.py:143
  25.5 12.0 %collective-permute-start = (bf16[256,768]{1,0:T(8,128)(2,1)S(1)}, bf16[256,768]{1,0:T(8,128)(2,1)S(1)}, u32[]{:S(2)}, u32[]{:S(2)}) collective-permute-start(bf16[256,768]{1,0:T(8,128)(2,1)S(1)} %get-tuple-element.14), channel_id=1, source_target_pairs={{0,6},{6,12},{12,18},{18,0},{1,7},{7,13},{13,19},{19,1},{2,8},{8,1... | collective-permute-start | bytes 1179656 | tf_op jit(solution)/shard_map/ppermute | solution.py:143
  37.5 38.6 %copy-start.1 = (bf16[64,256]{1,0:T(8,128)(2,1)S(1)}, bf16[64,256]{1,0:T(8,128)(2,1)}, u32[]{:S(2)}) copy-start(bf16[64,256]{1,0:T(8,128)(2,1)} %t_ref.1) | copy-start | bytes 98308

commit v6 on v5

--- a/solution.py
+++ b/solution.py
@@ -143,18 +143,30 @@
     return lax.ppermute(block, "x", [(i, (i + k) % X) for i in range(X)])
 
 
+def others(operands):
+    mask, a, feats = operands
+    copies = jnp.broadcast_to(feats[None], (X * Y, HELD, SRC))
+    feats = lax.all_to_all(copies, ("x", "y"), 0, 0, tiled=True)
+    feats = lax.all_gather(feats, "c", axis=0)
+    up, down = mask_blocks((1, 3), mask, a, limit=16)
+    own_a, _ = lax.optimization_barrier((a, up))
+    (own,) = mask_blocks((0,), mask, own_a, limit=16)
+    return feats, own, shift(up, 1), shift(down, 3)
+
+
+def nothing(operands):
+    block = jnp.zeros((SRC, TGT), jnp.bfloat16)
+    return jnp.zeros((CORES, X * Y, HELD, SRC), jnp.bfloat16), block, block, block
+
+
 def local(propagation, tile_mask, features, teleport):
     mask, a = tile_mask[0], propagation[0]
-    far, copies = mask_blocks((2,), mask, a, features[0].T)
-    feats = lax.all_to_all(copies, ("x", "y"), 0, 0, tiled=True)
-    feats = lax.all_gather(feats, "c", axis=0).reshape(CORES, X, Y, HELD, SRC)
-    near_a, _ = lax.optimization_barrier((a, far))
-    up, down = mask_blocks((1, 3), mask, near_a, limit=16)
-    own_a, _ = lax.optimization_barrier((a, up))
-    (own,) = mask_blocks((0,), mask, own_a, limit=16)
-    blocks = [own, shift(up, 1), shift(far, 2), shift(down, 3)]
+    (far,) = mask_blocks((2,), mask, a)
     me = lax.axis_index("x").astype(jnp.int32)
-    coded = product(me[None], feats, blocks)
+    a, _ = lax.optimization_barrier((a, far))
+    feats, own, up, down = lax.cond(me < X, others, nothing, (mask, a, features[0].T))
+    feats = feats.reshape(CORES, X, Y, HELD, SRC)
+    coded = product(me[None], feats, [own, up, shift(far, 2), down])
     coded = lax.all_to_all(coded, ("zh", "zl"), 0, 0, tiled=True)
     return finish(coded, teleport)
 

time: 77.7 us -> 74.6 us (0.960)
  the two profiles are of different devices: /device:TPU:2 before, /device:TPU:8 now
where the time goes in v6:
time: 74.6 us; the launch traced here: 74.3 us
  blocking collectives  37.6 us (50%)
  starting transfers between devices  22.9 us (31%)
  Pallas kernels  7.52 us (10%)
  waiting for transfers between devices  5.46 us (7%)
    all_to_all x1, blocking collectives, local(): coded = lax.all_to_all(coded, ('zh', 'zl'), 0, 0, tiled=True)  35.4 us
    ppermute x3, starting transfers between devices, shift(): return lax.ppermute(block, 'x', [(i, (i + k) % X) for i in range(X)])  11.5 us
    all_to_all x1, starting transfers between devices, others(): feats = lax.all_to_all(copies, ('x', 'y'), 0, 0, tiled=True)  11.4 us
    pallas_call x3, Pallas kernels, mask_blocks(): pl.pallas_call(functools.partial(spread_kernel if more else mask_kernel,...  4.18 us
    ppermute x3, waiting for transfers between devices, shift(): return lax.ppermute(block, 'x', [(i, (i + k) % X) for i in range(X)])  3.27 us
    all_to_all x1, waiting for transfers between devices, others(): feats = lax.all_to_all(copies, ('x', 'y'), 0, 0, tiled=True)  2.19 us
    all_gather x1, blocking collectives, others(): feats = lax.all_gather(feats, 'c', axis=0)  2.17 us
    pallas_call x1, Pallas kernels, product(): pl.pallas_call(product_kernel, in_specs=[pl.BlockSpec(memory_space=pltpu....  2.15 us
  transfers between devices with their start and end apart: 4, of which 2 were waited for; matrix products, arithmetic and copies ran while one was open for 1% of the time, Pallas kernels for 3%

profile of v6, /device:TPU:8, one launch (start us, length us, event | category | flops | bytes accessed | tf_op | source)
XLA Modules:
  0.0 74.3 jit_solution(5625639271278858155)
XLA Ops:
  0.0 0.0 copy-start.2
  0.0 0.0 copy-start.1
  0.0 0.0 copy-start.3
  0.0 2.0 %mask_blocks.5 = bf16[256,768]{1,0:T(8,128)(2,1)} custom-call(s32[2,24]{1,0:T(2,128)} %bitcast.10, bf16[256,3072]{1,0:T(8,128)(2,1)} %bitcast.7), custom_call_target="tpu_custom_call" | custom-call | tf_op jit(solution)/shard_map/mask_blocks/pallas_call | solution.py:61
  2.0 4.9 %collective-permute-start.2 = (bf16[256,768]{1,0:T(8,128)(2,1)}, bf16[256,768]{1,0:T(8,128)(2,1)S(1)}, u32[]{:S(2)}, u32[]{:S(2)}) collective-permute-start(bf16[256,768]{1,0:T(8,128)(2,1)} %mask_blocks.5), channel_id=1, source_target_pairs={{0,12},{6,18},{12,0},{18,6},{1,13},{7,19},{13,1},{19,7},{2,14},{8,... | collective-permute-start | bytes 1179656 | tf_op jit(solution)/shard_map/ppermute | solution.py:143
  6.9 0.0 copy-done.2
  6.9 0.0 copy-done.1
  7.0 0.0 copy-done.3
  7.0 28.5 %conditional.1 = (bf16[256,768]{1,0:T(8,128)(2,1)}, bf16[256,768]{1,0:T(8,128)(2,1)}, bf16[256,768]{1,0:T(8,128)(2,1)}, bf16[2,4,8,16,256]{4,3,2,1,0:T(8,128)(2,1)S(1)}) conditional(s32[]{:T(128)} %convert_element_type.3, () %tuple.17, (s32[2,24]{1,0:T(2,128)S(1)}, bf16[256,3072]{1,0:T(8,128)(2,1)S(1)}, bf16[16,256]{1,0:T(8,128)(2,1)S(1)}) %tuple.24), branch_computations={%region_0.0_spmd, %region_1.0_spmd} | conditional | bytes 4989072 | solution.py:167
  7.0 0.7 broadcast_in_dim.0
  7.7 11.4 %all-to-all-start = ((bf16[32,16,256]{2,1,0:T(8,128)(2,1)}), bf16[32,16,256]{2,1,0:T(8,128)(2,1)S(1)}, u32[]{:S(2)}, u32[]{:S(2)}) async-start(bf16[32,16,256]{2,1,0:T(8,128)(2,1)} %broadcast_in_dim.0), calls=%async_computation | async-start | bytes 524288 | tf_op jit(solution)/shard_map/cond/branch_1_fun/all_to_all | solution.py:149
  19.1 0.8 %mask_blocks.3 = (bf16[256,768]{1,0:T(8,128)(2,1)S(1)}, bf16[256,768]{1,0:T(8,128)(2,1)S(1)}) custom-call(s32[2,24]{1,0:T(2,128)S(1)} %get-tuple-element.12.mask_hbm, bf16[256,3072]{1,0:T(8,128)(2,1)S(1)} %get-tuple-element.15.a_hbm), custom_call_target="tpu_custom_call" | custom-call | tf_op jit(solution)/shard_map/cond/branch_1_fun/mask_blocks/pallas_call | solution.py:61
  19.9 4.6 %collective-permute-start.1 = (bf16[256,768]{1,0:T(8,128)(2,1)S(1)}, bf16[256,768]{1,0:T(8,128)(2,1)}, u32[]{:S(2)}, u32[]{:S(2)}) collective-permute-start(bf16[256,768]{1,0:T(8,128)(2,1)S(1)} %get-tuple-element.16), channel_id=1, source_target_pairs={{0,18},{6,0},{12,6},{18,12},{1,19},{7,1},{13,7},{19,13},{2,20},{8,... | collective-permute-start | bytes 1179656 | tf_op jit(solution)/shard_map/cond/branch_1_fun/ppermute | solution.py:143
  24.5 1.9 %collective-permute-start = (bf16[256,768]{1,0:T(8,128)(2,1)S(1)}, bf16[256,768]{1,0:T(8,128)(2,1)}, u32[]{:S(2)}, u32[]{:S(2)}) collective-permute-start(bf16[256,768]{1,0:T(8,128)(2,1)S(1)} %get-tuple-element.14), channel_id=1, source_target_pairs={{0,6},{6,12},{12,18},{18,0},{1,7},{7,13},{13,19},{19,1},{2,8},{8,1... | collective-permute-start | bytes 1179656 | tf_op jit(solution)/shard_map/cond/branch_1_fun/ppermute | solution.py:143
  26.4 1.4 %mask_blocks.4 = bf16[256,768]{1,0:T(8,128)(2,1)} custom-call(s32[2,24]{1,0:T(2,128)S(1)} %get-tuple-element.12.mask_hbm, bf16[256,3072]{1,0:T(8,128)(2,1)S(1)} %get-tuple-element.15.a_hbm), custom_call_target="tpu_custom_call" | custom-call | tf_op jit(solution)/shard_map/cond/branch_1_fun/mask_blocks/pallas_call | solution.py:61
  27.9 2.2 %all-to-all-done = bf16[32,16,256]{2,1,0:T(8,128)(2,1)S(1)} async-done(((bf16[32,16,256]{2,1,0:T(8,128)(2,1)}), bf16[32,16,256]{2,1,0:T(8,128)(2,1)S(1)}, u32[]{:S(2)}, u32[]{:S(2)}) %all-to-all-start) | async-done | bytes 262176 | tf_op jit(solution)/shard_map/cond/branch_1_fun/all_to_all | solution.py:149
  30.1 2.2 %all-gather = bf16[64,16,256]{2,1,0:T(8,128)(2,1)S(1)} all-gather(bf16[32,16,256]{2,1,0:T(8,128)(2,1)S(1)} %all-to-all-done), channel_id=2, replica_groups=mesh['y'=8,'c'=2,'zh'=2,'x'=4,'zl'=6] {'c'}, dimensions={0}, use_global_device_ids=true | all-gather | bytes 786432 | tf_op jit(solution)/shard_map/cond/branch_1_fun/all_gather | solution.py:150
  32.2 0.0 collective-permute-done.1
  32.2 3.3 %collective-permute-done = bf16[256,768]{1,0:T(8,128)(2,1)} collective-permute-done((bf16[256,768]{1,0:T(8,128)(2,1)S(1)}, bf16[256,768]{1,0:T(8,128)(2,1)}, u32[]{:S(2)}, u32[]{:S(2)}) %collective-permute-start) | collective-permute-done | bytes 393248 | tf_op jit(solution)/shard_map/cond/branch_1_fun/ppermute | solution.py:143
  35.5 0.0 collective-permute-done.2.refs_2_
  35.5 0.0 copy-start
  35.5 2.1 %product.1 = s16[12,144,128]{2,1,0:T(8,128)(2,1)S(1)} custom-call(s32[1]{0:T(128)} %bitcast.1.me_ref, bf16[2,4,8,16,256]{4,3,2,1,0:T(8,128)(2,1)S(1)} %get-tuple-element.24.f_ref, bf16[256,768]{1,0:T(8,128)(2,1)} %get-tuple-element.25.refs_0_, bf16[256,768]{1,0:T(8,128)(2,1)} %get-tuple-element.26.refs_1_, ...), custom_call_target="tpu_custom_call" | custom-call | tf_op jit(solution)/shard_map/product/pallas_call | solution.py:110
  37.7 35.4 %all_to_all.9.q_ref = s16[12,144,128]{2,1,0:T(8,128)(2,1)S(1)} all-to-all(s16[12,144,128]{2,1,0:T(8,128)(2,1)S(1)} %product.1), channel_id=1, replica_groups=mesh['y'=8,'c'=2,'zh'=2,'x'=4,'zl'=6] {'zh','zl'}, dimensions={0} | all-to-all | bytes 884736 | tf_op jit(solution)/shard_map/all_to_all | solution.py:170
  73.1 0.0 copy-done
  73.1 1.2 %finish.1 = f32[64,256]{1,0:T(8,128)} custom-call(s16[12,144,128]{2,1,0:T(8,128)(2,1)S(1)} %all_to_all.9.q_ref, bf16[64,256]{1,0:T(8,128)(2,1)S(1)} %copy-done), custom_call_target="tpu_custom_call" | custom-call | tf_op jit(solution)/shard_map/finish/pallas_call | solution.py:134
Async XLA Ops:
  0.0 6.9 %copy-start.2 = (s32[1,2,24]{2,1,0:T(2,128)S(1)}, s32[1,2,24]{2,1,0:T(2,128)}, u32[]{:S(2)}) copy-start(s32[1,2,24]{2,1,0:T(2,128)} %param.7) | copy-start | bytes 580
  0.0 6.9 %copy-start.1 = (bf16[1,256,3072]{2,1,0:T(8,128)(2,1)S(1)}, bf16[1,256,3072]{2,1,0:T(8,128)(2,1)}, u32[]{:S(2)}) copy-start(bf16[1,256,3072]{2,1,0:T(8,128)(2,1)} %param.6) | copy-start | bytes 4718596
  0.0 7.0 %copy-start.3 = (bf16[1,256,16]{1,2,0:T(8,128)(2,1)S(1)}, bf16[1,256,16]{1,2,0:T(8,128)(2,1)}, u32[]{:S(2)}) copy-start(bf16[1,256,16]{1,2,0:T(8,128)(2,1)} %param.8) | copy-start | bytes 24580
  2.0 33.5 %collective-permute-start.2 = (bf16[256,768]{1,0:T(8,128)(2,1)}, bf16[256,768]{1,0:T(8,128)(2,1)S(1)}, u32[]{:S(2)}, u32[]{:S(2)}) collective-permute-start(bf16[256,768]{1,0:T(8,128)(2,1)} %mask_blocks.5), channel_id=1, source_target_pairs={{0,12},{6,18},{12,0},{18,6},{1,13},{7,19},{13,1},{19,7},{2,14},{8,... | collective-permute-start | bytes 1179656 | tf_op jit(solution)/shard_map/ppermute | solution.py:143
  7.7 22.4 %all-to-all-start = ((bf16[32,16,256]{2,1,0:T(8,128)(2,1)}), bf16[32,16,256]{2,1,0:T(8,128)(2,1)S(1)}, u32[]{:S(2)}, u32[]{:S(2)}) async-start(bf16[32,16,256]{2,1,0:T(8,128)(2,1)} %broadcast_in_dim.0), calls=%async_computation | async-start | bytes 524288 | tf_op jit(solution)/shard_map/cond/branch_1_fun/all_to_all | solution.py:149
  19.9 12.4 %collective-permute-start.1 = (bf16[256,768]{1,0:T(8,128)(2,1)S(1)}, bf16[256,768]{1,0:T(8,128)(2,1)}, u32[]{:S(2)}, u32[]{:S(2)}) collective-permute-start(bf16[256,768]{1,0:T(8,128)(2,1)S(1)} %get-tuple-element.16), channel_id=1, source_target_pairs={{0,18},{6,0},{12,6},{18,12},{1,19},{7,1},{13,7},{19,13},{2,20},{8,... | collective-permute-start | bytes 1179656 | tf_op jit(solution)/shard_map/cond/branch_1_fun/ppermute | solution.py:143
  24.5 11.0 %collective-permute-start = (bf16[256,768]{1,0:T(8,128)(2,1)S(1)}, bf16[256,768]{1,0:T(8,128)(2,1)}, u32[]{:S(2)}, u32[]{:S(2)}) collective-permute-start(bf16[256,768]{1,0:T(8,128)(2,1)S(1)} %get-tuple-element.14), channel_id=1, source_target_pairs={{0,6},{6,12},{12,18},{18,0},{1,7},{7,13},{13,19},{19,1},{2,8},{8,1... | collective-permute-start | bytes 1179656 | tf_op jit(solution)/shard_map/cond/branch_1_fun/ppermute | solution.py:143
  35.5 37.6 %copy-start = (bf16[64,256]{1,0:T(8,128)(2,1)S(1)}, bf16[64,256]{1,0:T(8,128)(2,1)}, u32[]{:S(2)}) copy-start(bf16[64,256]{1,0:T(8,128)(2,1)} %t_ref.1) | copy-start | bytes 98308

commit v7 on v6

--- a/solution.py
+++ b/solution.py
@@ -74,20 +74,27 @@
     )(mask, a, *more)
 
 
-def product_kernel(me_ref, f_ref, *refs):
-    o_ref = refs[X]
+def product_kernel(me_ref, f_ref, own_ref, far_ref, up_ref, down_ref, o_ref, near_ref, sems):
+    wide = 2 * TILE
+    copies = []
+    for i in range(TGT // wide):
+        columns = pl.ds(i * wide, wide)
+        for n, ref in enumerate((up_ref, down_ref)):
+            copy = pltpu.make_async_copy(ref.at[:, columns], near_ref.at[n, :, columns], sems.at[i, n])
+            copy.start()
+            copies.append(copy)
     feats = []
-    for k in range(X):
+    for k in (0, 2, 1, 3):
         x = lax.rem(me_ref[0] + X - k, X)
         feats.append(jnp.concatenate([f_ref[c, x, y] for y in range(Y) for c in range(CORES)], axis=0))
     lane = lax.broadcasted_iota(jnp.int32, (16, TILE), 1)
-    wide = 2 * TILE
     for i in range(TGT // wide):
-        total = jnp.zeros((CLS, wide), jnp.float32)
-        for k in range(X):
-            total += jnp.dot(
-                feats[k], refs[k][:, i * wide : (i + 1) * wide], preferred_element_type=jnp.float32
-            )
+        columns = slice(i * wide, (i + 1) * wide)
+        total = jnp.dot(feats[0], own_ref[:, columns], preferred_element_type=jnp.float32)
+        total += jnp.dot(feats[1], far_ref[:, columns], preferred_element_type=jnp.float32)
+        for n in range(2):
+            copies[2 * i + n].wait()
+            total += jnp.dot(feats[2 + n], near_ref[n, :, columns], preferred_element_type=jnp.float32)
         total = total.T
         top = jnp.max(jnp.abs(total), axis=1, keepdims=True)
         power = jnp.ceil(jnp.log2(jnp.maximum(top, 1e-30)) * STEP)
@@ -105,16 +112,20 @@
             o_ref[z, 2 * ROWS : 2 * ROWS + 16, :] = scales.astype(jnp.int16)
 
 
-def product(me, feats, blocks):
-    whole = pl.BlockSpec(memory_space=pltpu.VMEM)
+def product(me, feats, own, far, up, down):
+    whole, anywhere = pl.BlockSpec(memory_space=pltpu.VMEM), pl.BlockSpec(memory_space=pl.ANY)
     return pl.pallas_call(
         product_kernel,
-        in_specs=[pl.BlockSpec(memory_space=pltpu.SMEM)] + [whole] * (1 + X),
+        in_specs=[pl.BlockSpec(memory_space=pltpu.SMEM)] + [whole] * 3 + [anywhere] * 2,
         out_specs=whole,
         out_shape=jax.ShapeDtypeStruct((Z, 2 * ROWS + 16, TILE), jnp.int16),
+        scratch_shapes=[
+            pltpu.VMEM((2, SRC, TGT), jnp.bfloat16),
+            pltpu.SemaphoreType.DMA((TGT // (2 * TILE), 2)),
+        ],
         compiler_params=pltpu.CompilerParams(vmem_limit_bytes=16 * MIB),
         name="product",
-    )(me, feats, *blocks)
+    )(me, feats, own, far, up, down)
 
 
 def finish_kernel(q_ref, t_ref, o_ref):
@@ -161,12 +172,12 @@
 
 def local(propagation, tile_mask, features, teleport):
     mask, a = tile_mask[0], propagation[0]
-    (far,) = mask_blocks((2,), mask, a)
+    (far,) = mask_blocks((2,), mask, a, limit=40)
     me = lax.axis_index("x").astype(jnp.int32)
     a, _ = lax.optimization_barrier((a, far))
     feats, own, up, down = lax.cond(me < X, others, nothing, (mask, a, features[0].T))
     feats = feats.reshape(CORES, X, Y, HELD, SRC)
-    coded = product(me[None], feats, [own, up, shift(far, 2), down])
+    coded = product(me[None], feats, own, shift(far, 2), up, down)
     coded = lax.all_to_all(coded, ("zh", "zl"), 0, 0, tiled=True)
     return finish(coded, teleport)
 

time: 74.6 us -> 76.3 us (1.023)
  local copies, waits for them, and re-layouts: 0.73 us -> 1.55 us
    pallas_call x1, Pallas kernels: 2.15 us -> 3.71 us  [product(): pl.pallas_call(product_kernel, in_specs=[pl.BlockSpec(memory_space=pltpu....]
    pallas_call x3, Pallas kernels: 4.18 us -> 2.7 us  [mask_blocks(): pl.pallas_call(functools.partial(spread_kernel if more else mask_kernel,...]
    unnamed x8 -> x10, local copies, waits for them, and re-layouts: 0.01 us -> 0.82 us
    all_to_all x1, waiting for transfers between devices: 2.19 us -> 2.98 us  [others(): feats = lax.all_to_all(copies, ('x', 'y'), 0, 0, tiled=True)]
  transfers between devices with their start and end apart: 4 -> 4, of which waited for: 2 -> 2; matrix products, arithmetic and copies ran while one was open for 1% -> 1% of each run, Pallas kernels for 3% -> 2%
where the time goes in v7:
time: 76.3 us; the launch traced here: 76 us
  blocking collectives  37.8 us (50%)
  starting transfers between devices  22.9 us (30%)
  Pallas kernels  7.6 us (10%)
  waiting for transfers between devices  6 us (8%)
  local copies, waits for them, and re-layouts  1.55 us (2%)
    all_to_all x1, blocking collectives, local(): coded = lax.all_to_all(coded, ('zh', 'zl'), 0, 0, tiled=True)  35.4 us
    ppermute x3, starting transfers between devices, shift(): return lax.ppermute(block, 'x', [(i, (i + k) % X) for i in range(X)])  11.5 us
    all_to_all x1, starting transfers between devices, others(): feats = lax.all_to_all(copies, ('x', 'y'), 0, 0, tiled=True)  11.4 us
    pallas_call x1, Pallas kernels, product(): pl.pallas_call(product_kernel, in_specs=[pl.BlockSpec(memory_space=pltpu....  3.71 us
    ppermute x3, waiting for transfers between devices, shift(): return lax.ppermute(block, 'x', [(i, (i + k) % X) for i in range(X)])  3.01 us
    all_to_all x1, waiting for transfers between devices, others(): feats = lax.all_to_all(copies, ('x', 'y'), 0, 0, tiled=True)  2.98 us
    pallas_call x3, Pallas kernels, mask_blocks(): pl.pallas_call(functools.partial(spread_kernel if more else mask_kernel,...  2.7 us
    all_gather x1, blocking collectives, others(): feats = lax.all_gather(feats, 'c', axis=0)  2.38 us
  transfers between devices with their start and end apart: 4, of which 2 were waited for; matrix products, arithmetic and copies ran while one was open for 1% of the time, Pallas kernels for 2%

profile of v7, /device:TPU:8, one launch (start us, length us, event | category | flops | bytes accessed | tf_op | source)
XLA Modules:
  0.0 76.0 jit_solution(2946282458903014040)
XLA Ops:
  0.0 0.0 copy-start.3
  0.0 0.0 copy-start.1
  0.0 0.0 copy-start.4
  0.0 1.2 %mask_blocks.5 = bf16[256,768]{1,0:T(8,128)(2,1)S(1)} custom-call(s32[2,24]{1,0:T(2,128)} %bitcast.10, bf16[256,3072]{1,0:T(8,128)(2,1)} %bitcast.7), custom_call_target="tpu_custom_call" | custom-call | tf_op jit(solution)/shard_map/mask_blocks/pallas_call | solution.py:61
  1.2 4.9 %collective-permute-start.2 = (bf16[256,768]{1,0:T(8,128)(2,1)S(1)}, bf16[256,768]{1,0:T(8,128)(2,1)S(1)}, u32[]{:S(2)}, u32[]{:S(2)}) collective-permute-start(bf16[256,768]{1,0:T(8,128)(2,1)S(1)} %mask_blocks.5), channel_id=1, source_target_pairs={{0,12},{6,18},{12,0},{18,6},{1,13},{7,19},{13,1},{19,7},{2,14},{8,... | collective-permute-start | bytes 1179656 | tf_op jit(solution)/shard_map/ppermute | solution.py:154
  6.2 0.0 copy-done.3
  6.2 0.0 copy-done.1
  6.2 0.0 copy-done.4
  6.2 28.6 %conditional.1 = (bf16[256,768]{1,0:T(8,128)(2,1)S(1)}, bf16[256,768]{1,0:T(8,128)(2,1)}, bf16[256,768]{1,0:T(8,128)(2,1)}, bf16[2,4,8,16,256]{4,3,2,1,0:T(8,128)(2,1)S(1)}) conditional(s32[]{:T(128)} %convert_element_type.3, () %tuple.17, (s32[2,24]{1,0:T(2,128)S(1)}, bf16[256,3072]{1,0:T(8,128)(2,1)S(1)}, bf16[16,256]{1,0:T(8,128)(2,1)S(1)}) %tuple.24), branch_computations={%region_0.0_spmd, %region_1.0_spmd} | conditional | bytes 4989072 | solution.py:178
  6.2 0.7 broadcast_in_dim.0
  7.0 11.4 %all-to-all-start = ((bf16[32,16,256]{2,1,0:T(8,128)(2,1)}), bf16[32,16,256]{2,1,0:T(8,128)(2,1)}, u32[]{:S(2)}, u32[]{:S(2)}) async-start(bf16[32,16,256]{2,1,0:T(8,128)(2,1)} %broadcast_in_dim.0), calls=%async_computation | async-start | bytes 524288 | tf_op jit(solution)/shard_map/cond/branch_1_fun/all_to_all | solution.py:160
  18.4 0.8 %mask_blocks.3 = (bf16[256,768]{1,0:T(8,128)(2,1)S(1)}, bf16[256,768]{1,0:T(8,128)(2,1)S(1)}) custom-call(s32[2,24]{1,0:T(2,128)S(1)} %get-tuple-element.12.mask_hbm, bf16[256,3072]{1,0:T(8,128)(2,1)S(1)} %get-tuple-element.15.a_hbm), custom_call_target="tpu_custom_call" | custom-call | tf_op jit(solution)/shard_map/cond/branch_1_fun/mask_blocks/pallas_call | solution.py:61
  19.2 4.6 %collective-permute-start.1 = (bf16[256,768]{1,0:T(8,128)(2,1)S(1)}, bf16[256,768]{1,0:T(8,128)(2,1)}, u32[]{:S(2)}, u32[]{:S(2)}) collective-permute-start(bf16[256,768]{1,0:T(8,128)(2,1)S(1)} %get-tuple-element.16), channel_id=1, source_target_pairs={{0,18},{6,0},{12,6},{18,12},{1,19},{7,1},{13,7},{19,13},{2,20},{8,... | collective-permute-start | bytes 1179656 | tf_op jit(solution)/shard_map/cond/branch_1_fun/ppermute | solution.py:154
  23.8 1.9 %collective-permute-start = (bf16[256,768]{1,0:T(8,128)(2,1)S(1)}, bf16[256,768]{1,0:T(8,128)(2,1)}, u32[]{:S(2)}, u32[]{:S(2)}) collective-permute-start(bf16[256,768]{1,0:T(8,128)(2,1)S(1)} %get-tuple-element.14), channel_id=1, source_target_pairs={{0,6},{6,12},{12,18},{18,0},{1,7},{7,13},{13,19},{19,1},{2,8},{8,1... | collective-permute-start | bytes 1179656 | tf_op jit(solution)/shard_map/cond/branch_1_fun/ppermute | solution.py:154
  25.8 0.7 mask_blocks.4
  26.5 3.0 %all-to-all-done = bf16[32,16,256]{2,1,0:T(8,128)(2,1)} async-done(((bf16[32,16,256]{2,1,0:T(8,128)(2,1)}), bf16[32,16,256]{2,1,0:T(8,128)(2,1)}, u32[]{:S(2)}, u32[]{:S(2)}) %all-to-all-start) | async-done | bytes 262176 | tf_op jit(solution)/shard_map/cond/branch_1_fun/all_to_all | solution.py:160
  29.4 2.4 %all-gather = bf16[64,16,256]{2,1,0:T(8,128)(2,1)S(1)} all-gather(bf16[32,16,256]{2,1,0:T(8,128)(2,1)} %all-to-all-done), channel_id=2, replica_groups=mesh['y'=8,'c'=2,'zh'=2,'x'=4,'zl'=6] {'c'}, dimensions={0}, use_global_device_ids=true | all-gather | bytes 786432 | tf_op jit(solution)/shard_map/cond/branch_1_fun/all_gather | solution.py:161
  31.8 0.0 collective-permute-done.1
  31.8 3.0 %collective-permute-done = bf16[256,768]{1,0:T(8,128)(2,1)} collective-permute-done((bf16[256,768]{1,0:T(8,128)(2,1)S(1)}, bf16[256,768]{1,0:T(8,128)(2,1)}, u32[]{:S(2)}, u32[]{:S(2)}) %collective-permute-start) | collective-permute-done | bytes 393248 | tf_op jit(solution)/shard_map/cond/branch_1_fun/ppermute | solution.py:154
  34.8 0.0 copy-start.2
  34.8 0.0 collective-permute-done.2.far_ref
  34.8 0.8 %copy-done.2 = bf16[2,4,8,16,256]{4,3,2,1,0:T(8,128)(2,1)} copy-done((bf16[2,4,8,16,256]{4,3,2,1,0:T(8,128)(2,1)}, bf16[2,4,8,16,256]{4,3,2,1,0:T(8,128)(2,1)S(1)}, u32[]{:S(2)}) %copy-start.2) | copy-done | bytes 524312
  35.6 0.0 copy-start
  35.6 3.7 %product.1 = s16[12,144,128]{2,1,0:T(8,128)(2,1)S(1)} custom-call(s32[1]{0:T(128)} %bitcast.1.me_ref, bf16[2,4,8,16,256]{4,3,2,1,0:T(8,128)(2,1)} %copy-done.2, bf16[256,768]{1,0:T(8,128)(2,1)S(1)} %get-tuple-element.25.own_ref, bf16[256,768]{1,0:T(8,128)(2,1)S(1)} %collective-permute-done.2.far_ref, bf16[256,768]{1,0:T(8,128)(2,1)} %get-tuple-element.26.up_ref, ...), custom_call_target="tpu_custom_call" | custom-call | tf_op jit(solution)/shard_map/product/pallas_call | solution.py:117
  39.4 35.4 %all_to_all.9.q_ref = s16[12,144,128]{2,1,0:T(8,128)(2,1)S(1)} all-to-all(s16[12,144,128]{2,1,0:T(8,128)(2,1)S(1)} %product.1), channel_id=1, replica_groups=mesh['y'=8,'c'=2,'zh'=2,'x'=4,'zl'=6] {'zh','zl'}, dimensions={0} | all-to-all | bytes 884736 | tf_op jit(solution)/shard_map/all_to_all | solution.py:181
  74.8 0.0 copy-done
  74.8 1.2 %finish.1 = f32[64,256]{1,0:T(8,128)} custom-call(s16[12,144,128]{2,1,0:T(8,128)(2,1)S(1)} %all_to_all.9.q_ref, bf16[64,256]{1,0:T(8,128)(2,1)S(1)} %copy-done), custom_call_target="tpu_custom_call" | custom-call | tf_op jit(solution)/shard_map/finish/pallas_call | solution.py:145
Async XLA Ops:
  0.0 6.2 %copy-start.3 = (s32[1,2,24]{2,1,0:T(2,128)S(1)}, s32[1,2,24]{2,1,0:T(2,128)}, u32[]{:S(2)}) copy-start(s32[1,2,24]{2,1,0:T(2,128)} %param.7) | copy-start | bytes 580
  0.0 6.2 %copy-start.1 = (bf16[1,256,3072]{2,1,0:T(8,128)(2,1)S(1)}, bf16[1,256,3072]{2,1,0:T(8,128)(2,1)}, u32[]{:S(2)}) copy-start(bf16[1,256,3072]{2,1,0:T(8,128)(2,1)} %param.6) | copy-start | bytes 4718596
  0.0 6.2 %copy-start.4 = (bf16[1,256,16]{1,2,0:T(8,128)(2,1)S(1)}, bf16[1,256,16]{1,2,0:T(8,128)(2,1)}, u32[]{:S(2)}) copy-start(bf16[1,256,16]{1,2,0:T(8,128)(2,1)} %param.8) | copy-start | bytes 24580
  1.2 33.6 %collective-permute-start.2 = (bf16[256,768]{1,0:T(8,128)(2,1)S(1)}, bf16[256,768]{1,0:T(8,128)(2,1)S(1)}, u32[]{:S(2)}, u32[]{:S(2)}) collective-permute-start(bf16[256,768]{1,0:T(8,128)(2,1)S(1)} %mask_blocks.5), channel_id=1, source_target_pairs={{0,12},{6,18},{12,0},{18,6},{1,13},{7,19},{13,1},{19,7},{2,14},{8,... | collective-permute-start | bytes 1179656 | tf_op jit(solution)/shard_map/ppermute | solution.py:154
  7.0 22.5 %all-to-all-start = ((bf16[32,16,256]{2,1,0:T(8,128)(2,1)}), bf16[32,16,256]{2,1,0:T(8,128)(2,1)}, u32[]{:S(2)}, u32[]{:S(2)}) async-start(bf16[32,16,256]{2,1,0:T(8,128)(2,1)} %broadcast_in_dim.0), calls=%async_computation | async-start | bytes 524288 | tf_op jit(solution)/shard_map/cond/branch_1_fun/all_to_all | solution.py:160
  19.2 12.6 %collective-permute-start.1 = (bf16[256,768]{1,0:T(8,128)(2,1)S(1)}, bf16[256,768]{1,0:T(8,128)(2,1)}, u32[]{:S(2)}, u32[]{:S(2)}) collective-permute-start(bf16[256,768]{1,0:T(8,128)(2,1)S(1)} %get-tuple-element.16), channel_id=1, source_target_pairs={{0,18},{6,0},{12,6},{18,12},{1,19},{7,1},{13,7},{19,13},{2,20},{8,... | collective-permute-start | bytes 1179656 | tf_op jit(solution)/shard_map/cond/branch_1_fun/ppermute | solution.py:154
  23.8 11.0 %collective-permute-start = (bf16[256,768]{1,0:T(8,128)(2,1)S(1)}, bf16[256,768]{1,0:T(8,128)(2,1)}, u32[]{:S(2)}, u32[]{:S(2)}) collective-permute-start(bf16[256,768]{1,0:T(8,128)(2,1)S(1)} %get-tuple-element.14), channel_id=1, source_target_pairs={{0,6},{6,12},{12,18},{18,0},{1,7},{7,13},{13,19},{19,1},{2,8},{8,1... | collective-permute-start | bytes 1179656 | tf_op jit(solution)/shard_map/cond/branch_1_fun/ppermute | solution.py:154
  34.8 0.8 %copy-start.2 = (bf16[2,4,8,16,256]{4,3,2,1,0:T(8,128)(2,1)}, bf16[2,4,8,16,256]{4,3,2,1,0:T(8,128)(2,1)S(1)}, u32[]{:S(2)}) copy-start(bf16[2,4,8,16,256]{4,3,2,1,0:T(8,128)(2,1)S(1)} %get-tuple-element.24.f_ref) | copy-start | bytes 1572868
  35.6 39.1 %copy-start = (bf16[64,256]{1,0:T(8,128)(2,1)S(1)}, bf16[64,256]{1,0:T(8,128)(2,1)}, u32[]{:S(2)}) copy-start(bf16[64,256]{1,0:T(8,128)(2,1)} %t_ref.1) | copy-start | bytes 98308

commit v8 on v6

--- a/solution.py
+++ b/solution.py
@@ -112,7 +112,7 @@
         in_specs=[pl.BlockSpec(memory_space=pltpu.SMEM)] + [whole] * (1 + X),
         out_specs=whole,
         out_shape=jax.ShapeDtypeStruct((Z, 2 * ROWS + 16, TILE), jnp.int16),
-        compiler_params=pltpu.CompilerParams(vmem_limit_bytes=16 * MIB),
+        compiler_params=pltpu.CompilerParams(vmem_limit_bytes=8 * MIB),
         name="product",
     )(me, feats, *blocks)
 
@@ -161,7 +161,7 @@
 
 def local(propagation, tile_mask, features, teleport):
     mask, a = tile_mask[0], propagation[0]
-    (far,) = mask_blocks((2,), mask, a)
+    (far,) = mask_blocks((2,), mask, a, limit=40)
     me = lax.axis_index("x").astype(jnp.int32)
     a, _ = lax.optimization_barrier((a, far))
     feats, own, up, down = lax.cond(me < X, others, nothing, (mask, a, features[0].T))

time: 74.6 us -> 73.8 us (0.989)
  Pallas kernels: 7.52 us -> 5.92 us
    pallas_call x3, Pallas kernels: 4.18 us -> 2.7 us  [mask_blocks(): pl.pallas_call(functools.partial(spread_kernel if more else mask_kernel,...]
    all_to_all x1, waiting for transfers between devices: 2.19 us -> 2.98 us  [others(): feats = lax.all_to_all(copies, ('x', 'y'), 0, 0, tiled=True)]
  transfers between devices with their start and end apart: 4 -> 4, of which waited for: 2 -> 2; matrix products, arithmetic and copies ran while one was open for 1% -> 1% of each run, Pallas kernels for 3% -> 2%
where the time goes in v8:
time: 73.8 us; the launch traced here: 73.5 us
  blocking collectives  37.8 us (51%)
  starting transfers between devices  22.9 us (31%)
  waiting for transfers between devices  6 us (8%)
  Pallas kernels  5.92 us (8%)
  local copies, waits for them, and re-layouts  0.74 us (1%)
    all_to_all x1, blocking collectives, local(): coded = lax.all_to_all(coded, ('zh', 'zl'), 0, 0, tiled=True)  35.4 us
    ppermute x3, starting transfers between devices, shift(): return lax.ppermute(block, 'x', [(i, (i + k) % X) for i in range(X)])  11.5 us
    all_to_all x1, starting transfers between devices, others(): feats = lax.all_to_all(copies, ('x', 'y'), 0, 0, tiled=True)  11.4 us
    ppermute x3, waiting for transfers between devices, shift(): return lax.ppermute(block, 'x', [(i, (i + k) % X) for i in range(X)])  3.01 us
    all_to_all x1, waiting for transfers between devices, others(): feats = lax.all_to_all(copies, ('x', 'y'), 0, 0, tiled=True)  2.98 us
    pallas_call x3, Pallas kernels, mask_blocks(): pl.pallas_call(functools.partial(spread_kernel if more else mask_kernel,...  2.7 us
    all_gather x1, blocking collectives, others(): feats = lax.all_gather(feats, 'c', axis=0)  2.38 us
    pallas_call x1, Pallas kernels, product(): pl.pallas_call(product_kernel, in_specs=[pl.BlockSpec(memory_space=pltpu....  2.03 us
  transfers between devices with their start and end apart: 4, of which 2 were waited for; matrix products, arithmetic and copies ran while one was open for 1% of the time, Pallas kernels for 2%

profile of v8, /device:TPU:8, one launch (start us, length us, event | category | flops | bytes accessed | tf_op | source)
XLA Modules:
  0.0 73.5 jit_solution(8857726710215225161)
XLA Ops:
  0.0 0.0 copy-start.2
  0.0 0.0 copy-start.1
  0.0 0.0 copy-start.3
  0.0 1.2 %mask_blocks.5 = bf16[256,768]{1,0:T(8,128)(2,1)S(1)} custom-call(s32[2,24]{1,0:T(2,128)} %bitcast.10, bf16[256,3072]{1,0:T(8,128)(2,1)} %bitcast.7), custom_call_target="tpu_custom_call" | custom-call | tf_op jit(solution)/shard_map/mask_blocks/pallas_call | solution.py:61
  1.2 4.9 %collective-permute-start.2 = (bf16[256,768]{1,0:T(8,128)(2,1)S(1)}, bf16[256,768]{1,0:T(8,128)(2,1)S(1)}, u32[]{:S(2)}, u32[]{:S(2)}) collective-permute-start(bf16[256,768]{1,0:T(8,128)(2,1)S(1)} %mask_blocks.5), channel_id=1, source_target_pairs={{0,12},{6,18},{12,0},{18,6},{1,13},{7,19},{13,1},{19,7},{2,14},{8,... | collective-permute-start | bytes 1179656 | tf_op jit(solution)/shard_map/ppermute | solution.py:143
  6.2 0.0 copy-done.2
  6.2 0.0 copy-done.1
  6.2 0.0 copy-done.3
  6.2 28.6 %conditional.1 = (bf16[256,768]{1,0:T(8,128)(2,1)S(1)}, bf16[256,768]{1,0:T(8,128)(2,1)}, bf16[256,768]{1,0:T(8,128)(2,1)}, bf16[2,4,8,16,256]{4,3,2,1,0:T(8,128)(2,1)S(1)}) conditional(s32[]{:T(128)} %convert_element_type.3, () %tuple.17, (s32[2,24]{1,0:T(2,128)S(1)}, bf16[256,3072]{1,0:T(8,128)(2,1)S(1)}, bf16[16,256]{1,0:T(8,128)(2,1)S(1)}) %tuple.24), branch_computations={%region_0.0_spmd, %region_1.0_spmd} | conditional | bytes 4989072 | solution.py:167
  6.2 0.7 broadcast_in_dim.0
  7.0 11.4 %all-to-all-start = ((bf16[32,16,256]{2,1,0:T(8,128)(2,1)}), bf16[32,16,256]{2,1,0:T(8,128)(2,1)}, u32[]{:S(2)}, u32[]{:S(2)}) async-start(bf16[32,16,256]{2,1,0:T(8,128)(2,1)} %broadcast_in_dim.0), calls=%async_computation | async-start | bytes 524288 | tf_op jit(solution)/shard_map/cond/branch_1_fun/all_to_all | solution.py:149
  18.4 0.8 %mask_blocks.3 = (bf16[256,768]{1,0:T(8,128)(2,1)S(1)}, bf16[256,768]{1,0:T(8,128)(2,1)S(1)}) custom-call(s32[2,24]{1,0:T(2,128)S(1)} %get-tuple-element.12.mask_hbm, bf16[256,3072]{1,0:T(8,128)(2,1)S(1)} %get-tuple-element.15.a_hbm), custom_call_target="tpu_custom_call" | custom-call | tf_op jit(solution)/shard_map/cond/branch_1_fun/mask_blocks/pallas_call | solution.py:61
  19.2 4.6 %collective-permute-start.1 = (bf16[256,768]{1,0:T(8,128)(2,1)S(1)}, bf16[256,768]{1,0:T(8,128)(2,1)}, u32[]{:S(2)}, u32[]{:S(2)}) collective-permute-start(bf16[256,768]{1,0:T(8,128)(2,1)S(1)} %get-tuple-element.16), channel_id=1, source_target_pairs={{0,18},{6,0},{12,6},{18,12},{1,19},{7,1},{13,7},{19,13},{2,20},{8,... | collective-permute-start | bytes 1179656 | tf_op jit(solution)/shard_map/cond/branch_1_fun/ppermute | solution.py:143
  23.8 1.9 %collective-permute-start = (bf16[256,768]{1,0:T(8,128)(2,1)S(1)}, bf16[256,768]{1,0:T(8,128)(2,1)}, u32[]{:S(2)}, u32[]{:S(2)}) collective-permute-start(bf16[256,768]{1,0:T(8,128)(2,1)S(1)} %get-tuple-element.14), channel_id=1, source_target_pairs={{0,6},{6,12},{12,18},{18,0},{1,7},{7,13},{13,19},{19,1},{2,8},{8,1... | collective-permute-start | bytes 1179656 | tf_op jit(solution)/shard_map/cond/branch_1_fun/ppermute | solution.py:143
  25.8 0.7 mask_blocks.4
  26.4 3.0 %all-to-all-done = bf16[32,16,256]{2,1,0:T(8,128)(2,1)} async-done(((bf16[32,16,256]{2,1,0:T(8,128)(2,1)}), bf16[32,16,256]{2,1,0:T(8,128)(2,1)}, u32[]{:S(2)}, u32[]{:S(2)}) %all-to-all-start) | async-done | bytes 262176 | tf_op jit(solution)/shard_map/cond/branch_1_fun/all_to_all | solution.py:149
  29.4 2.4 %all-gather = bf16[64,16,256]{2,1,0:T(8,128)(2,1)S(1)} all-gather(bf16[32,16,256]{2,1,0:T(8,128)(2,1)} %all-to-all-done), channel_id=2, replica_groups=mesh['y'=8,'c'=2,'zh'=2,'x'=4,'zl'=6] {'c'}, dimensions={0}, use_global_device_ids=true | all-gather | bytes 786432 | tf_op jit(solution)/shard_map/cond/branch_1_fun/all_gather | solution.py:150
  31.8 0.0 collective-permute-done.1
  31.8 3.0 %collective-permute-done = bf16[256,768]{1,0:T(8,128)(2,1)} collective-permute-done((bf16[256,768]{1,0:T(8,128)(2,1)S(1)}, bf16[256,768]{1,0:T(8,128)(2,1)}, u32[]{:S(2)}, u32[]{:S(2)}) %collective-permute-start) | collective-permute-done | bytes 393248 | tf_op jit(solution)/shard_map/cond/branch_1_fun/ppermute | solution.py:143
  34.8 0.0 collective-permute-done.2.refs_2_
  34.8 0.0 copy-start
  34.8 2.0 %product.1 = s16[12,144,128]{2,1,0:T(8,128)(2,1)S(1)} custom-call(s32[1]{0:T(128)} %bitcast.1.me_ref, bf16[2,4,8,16,256]{4,3,2,1,0:T(8,128)(2,1)S(1)} %get-tuple-element.24.f_ref, bf16[256,768]{1,0:T(8,128)(2,1)S(1)} %get-tuple-element.25.refs_0_, bf16[256,768]{1,0:T(8,128)(2,1)} %get-tuple-element.26.refs_1_, ...), custom_call_target="tpu_custom_call" | custom-call | tf_op jit(solution)/shard_map/product/pallas_call | solution.py:110
  36.9 35.4 %all_to_all.9.q_ref = s16[12,144,128]{2,1,0:T(8,128)(2,1)S(1)} all-to-all(s16[12,144,128]{2,1,0:T(8,128)(2,1)S(1)} %product.1), channel_id=1, replica_groups=mesh['y'=8,'c'=2,'zh'=2,'x'=4,'zl'=6] {'zh','zl'}, dimensions={0} | all-to-all | bytes 884736 | tf_op jit(solution)/shard_map/all_to_all | solution.py:170
  72.3 0.0 copy-done
  72.3 1.2 %finish.1 = f32[64,256]{1,0:T(8,128)} custom-call(s16[12,144,128]{2,1,0:T(8,128)(2,1)S(1)} %all_to_all.9.q_ref, bf16[64,256]{1,0:T(8,128)(2,1)S(1)} %copy-done), custom_call_target="tpu_custom_call" | custom-call | tf_op jit(solution)/shard_map/finish/pallas_call | solution.py:134
Async XLA Ops:
  0.0 6.2 %copy-start.2 = (s32[1,2,24]{2,1,0:T(2,128)S(1)}, s32[1,2,24]{2,1,0:T(2,128)}, u32[]{:S(2)}) copy-start(s32[1,2,24]{2,1,0:T(2,128)} %param.7) | copy-start | bytes 580
  0.0 6.2 %copy-start.1 = (bf16[1,256,3072]{2,1,0:T(8,128)(2,1)S(1)}, bf16[1,256,3072]{2,1,0:T(8,128)(2,1)}, u32[]{:S(2)}) copy-start(bf16[1,256,3072]{2,1,0:T(8,128)(2,1)} %param.6) | copy-start | bytes 4718596
  0.0 6.2 %copy-start.3 = (bf16[1,256,16]{1,2,0:T(8,128)(2,1)S(1)}, bf16[1,256,16]{1,2,0:T(8,128)(2,1)}, u32[]{:S(2)}) copy-start(bf16[1,256,16]{1,2,0:T(8,128)(2,1)} %param.8) | copy-start | bytes 24580
  1.2 33.6 %collective-permute-start.2 = (bf16[256,768]{1,0:T(8,128)(2,1)S(1)}, bf16[256,768]{1,0:T(8,128)(2,1)S(1)}, u32[]{:S(2)}, u32[]{:S(2)}) collective-permute-start(bf16[256,768]{1,0:T(8,128)(2,1)S(1)} %mask_blocks.5), channel_id=1, source_target_pairs={{0,12},{6,18},{12,0},{18,6},{1,13},{7,19},{13,1},{19,7},{2,14},{8,... | collective-permute-start | bytes 1179656 | tf_op jit(solution)/shard_map/ppermute | solution.py:143
  7.0 22.5 %all-to-all-start = ((bf16[32,16,256]{2,1,0:T(8,128)(2,1)}), bf16[32,16,256]{2,1,0:T(8,128)(2,1)}, u32[]{:S(2)}, u32[]{:S(2)}) async-start(bf16[32,16,256]{2,1,0:T(8,128)(2,1)} %broadcast_in_dim.0), calls=%async_computation | async-start | bytes 524288 | tf_op jit(solution)/shard_map/cond/branch_1_fun/all_to_all | solution.py:149
  19.2 12.6 %collective-permute-start.1 = (bf16[256,768]{1,0:T(8,128)(2,1)S(1)}, bf16[256,768]{1,0:T(8,128)(2,1)}, u32[]{:S(2)}, u32[]{:S(2)}) collective-permute-start(bf16[256,768]{1,0:T(8,128)(2,1)S(1)} %get-tuple-element.16), channel_id=1, source_target_pairs={{0,18},{6,0},{12,6},{18,12},{1,19},{7,1},{13,7},{19,13},{2,20},{8,... | collective-permute-start | bytes 1179656 | tf_op jit(solution)/shard_map/cond/branch_1_fun/ppermute | solution.py:143
  23.8 11.0 %collective-permute-start = (bf16[256,768]{1,0:T(8,128)(2,1)S(1)}, bf16[256,768]{1,0:T(8,128)(2,1)}, u32[]{:S(2)}, u32[]{:S(2)}) collective-permute-start(bf16[256,768]{1,0:T(8,128)(2,1)S(1)} %get-tuple-element.14), channel_id=1, source_target_pairs={{0,6},{6,12},{12,18},{18,0},{1,7},{7,13},{13,19},{19,1},{2,8},{8,1... | collective-permute-start | bytes 1179656 | tf_op jit(solution)/shard_map/cond/branch_1_fun/ppermute | solution.py:143
  34.8 37.4 %copy-start = (bf16[64,256]{1,0:T(8,128)(2,1)S(1)}, bf16[64,256]{1,0:T(8,128)(2,1)}, u32[]{:S(2)}) copy-start(bf16[64,256]{1,0:T(8,128)(2,1)} %t_ref.1) | copy-start | bytes 98308

commit v9 on v8

--- a/solution.py
+++ b/solution.py
@@ -148,25 +148,25 @@
     copies = jnp.broadcast_to(feats[None], (X * Y, HELD, SRC))
     feats = lax.all_to_all(copies, ("x", "y"), 0, 0, tiled=True)
     feats = lax.all_gather(feats, "c", axis=0)
-    up, down = mask_blocks((1, 3), mask, a, limit=16)
-    own_a, _ = lax.optimization_barrier((a, up))
+    (down,) = mask_blocks((3,), mask, a, limit=16)
+    own_a, _ = lax.optimization_barrier((a, down))
     (own,) = mask_blocks((0,), mask, own_a, limit=16)
-    return feats, own, shift(up, 1), shift(down, 3)
+    return feats, own, shift(down, 3)
 
 
 def nothing(operands):
     block = jnp.zeros((SRC, TGT), jnp.bfloat16)
-    return jnp.zeros((CORES, X * Y, HELD, SRC), jnp.bfloat16), block, block, block
+    return jnp.zeros((CORES, X * Y, HELD, SRC), jnp.bfloat16), block, block
 
 
 def local(propagation, tile_mask, features, teleport):
     mask, a = tile_mask[0], propagation[0]
-    (far,) = mask_blocks((2,), mask, a, limit=40)
+    far, up = mask_blocks((2, 1), mask, a, limit=40)
     me = lax.axis_index("x").astype(jnp.int32)
     a, _ = lax.optimization_barrier((a, far))
-    feats, own, up, down = lax.cond(me < X, others, nothing, (mask, a, features[0].T))
+    feats, own, down = lax.cond(me < X, others, nothing, (mask, a, features[0].T))
     feats = feats.reshape(CORES, X, Y, HELD, SRC)
-    coded = product(me[None], feats, [own, up, shift(far, 2), down])
+    coded = product(me[None], feats, [own, shift(up, 1), shift(far, 2), down])
     coded = lax.all_to_all(coded, ("zh", "zl"), 0, 0, tiled=True)
     return finish(coded, teleport)
 

time: 73.8 us -> 74.6 us (1.011)
  waiting for transfers between devices: 6 us -> 4.37 us
  blocking collectives: 37.8 us -> 38.8 us
  Pallas kernels: 5.92 us -> 6.76 us
    ppermute x3, waiting for transfers between devices: 3.01 us -> 0.01 us  [shift(): return lax.ppermute(block, 'x', [(i, (i + k) % X) for i in range(X)])]
    all_to_all x1, waiting for transfers between devices: 2.98 us -> 4.36 us  [others(): feats = lax.all_to_all(copies, ('x', 'y'), 0, 0, tiled=True)]
    ppermute x3, starting transfers between devices: 11.5 us -> 12.7 us  [shift(): return lax.ppermute(block, 'x', [(i, (i + k) % X) for i in range(X)])]
    all_to_all x1, blocking collectives: 35.4 us -> 36.4 us  [local(): coded = lax.all_to_all(coded, ('zh', 'zl'), 0, 0, tiled=True)]
    pallas_call x3, Pallas kernels: 2.7 us -> 3.53 us  [mask_blocks(): pl.pallas_call(functools.partial(spread_kernel if more else mask_kernel,...]
  transfers between devices with their start and end apart: 4 -> 4, of which waited for: 2 -> 1; matrix products, arithmetic and copies ran while one was open for 1% -> 1% of each run, Pallas kernels for 2% -> 3%
where the time goes in v9:
time: 74.6 us; the launch traced here: 74.3 us
  blocking collectives  38.8 us (52%)
  starting transfers between devices  23.5 us (32%)
  Pallas kernels  6.76 us (9%)
  waiting for transfers between devices  4.37 us (6%)
    all_to_all x1, blocking collectives, local(): coded = lax.all_to_all(coded, ('zh', 'zl'), 0, 0, tiled=True)  36.4 us
    ppermute x3, starting transfers between devices, shift(): return lax.ppermute(block, 'x', [(i, (i + k) % X) for i in range(X)])  12.7 us
    all_to_all x1, starting transfers between devices, others(): feats = lax.all_to_all(copies, ('x', 'y'), 0, 0, tiled=True)  10.8 us
    all_to_all x1, waiting for transfers between devices, others(): feats = lax.all_to_all(copies, ('x', 'y'), 0, 0, tiled=True)  4.36 us
    pallas_call x3, Pallas kernels, mask_blocks(): pl.pallas_call(functools.partial(spread_kernel if more else mask_kernel,...  3.53 us
    all_gather x1, blocking collectives, others(): feats = lax.all_gather(feats, 'c', axis=0)  2.38 us
    pallas_call x1, Pallas kernels, product(): pl.pallas_call(product_kernel, in_specs=[pl.BlockSpec(memory_space=pltpu....  2.03 us
  transfers between devices with their start and end apart: 4, of which 1 were waited for; matrix products, arithmetic and copies ran while one was open for 1% of the time, Pallas kernels for 3%

profile of v9, /device:TPU:8, one launch (start us, length us, event | category | flops | bytes accessed | tf_op | source)
XLA Modules:
  0.0 74.3 jit_solution(16686938726813806208)
XLA Ops:
  0.0 0.0 copy-start.2
  0.0 0.0 copy-start.1
  0.0 0.0 copy-start.3
  0.0 1.4 %mask_blocks.5 = (bf16[256,768]{1,0:T(8,128)(2,1)S(1)}, bf16[256,768]{1,0:T(8,128)(2,1)S(1)}) custom-call(s32[2,24]{1,0:T(2,128)} %bitcast.10, bf16[256,3072]{1,0:T(8,128)(2,1)} %bitcast.7), custom_call_target="tpu_custom_call" | custom-call | tf_op jit(solution)/shard_map/mask_blocks/pallas_call | solution.py:61
  1.5 3.4 %collective-permute-start.1 = (bf16[256,768]{1,0:T(8,128)(2,1)S(1)}, bf16[256,768]{1,0:T(8,128)(2,1)S(1)}, u32[]{:S(2)}, u32[]{:S(2)}) collective-permute-start(bf16[256,768]{1,0:T(8,128)(2,1)S(1)} %get-tuple-element.26), channel_id=1, source_target_pairs={{0,6},{6,12},{12,18},{18,0},{1,7},{7,13},{13,19},{19,1},{2,8},{8,1... | collective-permute-start | bytes 1179656 | tf_op jit(solution)/shard_map/ppermute | solution.py:143
  4.9 4.6 %collective-permute-start.2 = (bf16[256,768]{1,0:T(8,128)(2,1)S(1)}, bf16[256,768]{1,0:T(8,128)(2,1)S(1)}, u32[]{:S(2)}, u32[]{:S(2)}) collective-permute-start(bf16[256,768]{1,0:T(8,128)(2,1)S(1)} %get-tuple-element.22), channel_id=1, source_target_pairs={{0,12},{6,18},{12,0},{18,6},{1,13},{7,19},{13,1},{19,7},{2,14},{8,... | collective-permute-start | bytes 1179656 | tf_op jit(solution)/shard_map/ppermute | solution.py:143
  9.5 0.0 copy-done.2
  9.5 0.0 copy-done.1
  9.5 0.0 copy-done.3
  9.5 25.0 %conditional.1 = (bf16[256,768]{1,0:T(8,128)(2,1)}, bf16[256,768]{1,0:T(8,128)(2,1)}, bf16[2,4,8,16,256]{4,3,2,1,0:T(8,128)(2,1)S(1)}) conditional(s32[]{:T(128)} %convert_element_type.3, () %tuple.17, (s32[2,24]{1,0:T(2,128)S(1)}, bf16[256,3072]{1,0:T(8,128)(2,1)S(1)}, bf16[16,256]{1,0:T(8,128)(2,1)S(1)}) %tuple.24), branch_computations={%region_0.0_spmd, %region_1.0_spmd} | conditional | bytes 3416160 | solution.py:167
  9.6 0.7 broadcast_in_dim.0
  10.3 10.8 %all-to-all-start = ((bf16[32,16,256]{2,1,0:T(8,128)(2,1)}), bf16[32,16,256]{2,1,0:T(8,128)(2,1)}, u32[]{:S(2)}, u32[]{:S(2)}) async-start(bf16[32,16,256]{2,1,0:T(8,128)(2,1)} %broadcast_in_dim.0), calls=%async_computation | async-start | bytes 524288 | tf_op jit(solution)/shard_map/cond/branch_1_fun/all_to_all | solution.py:149
  21.1 0.7 mask_blocks.3
  21.8 4.6 %collective-permute-start = (bf16[256,768]{1,0:T(8,128)(2,1)S(1)}, bf16[256,768]{1,0:T(8,128)(2,1)}, u32[]{:S(2)}, u32[]{:S(2)}) collective-permute-start(bf16[256,768]{1,0:T(8,128)(2,1)S(1)} %mask_blocks.3), channel_id=1, source_target_pairs={{0,18},{6,0},{12,6},{18,12},{1,19},{7,1},{13,7},{19,13},{2,20},{8,... | collective-permute-start | bytes 1179656 | tf_op jit(solution)/shard_map/cond/branch_1_fun/ppermute | solution.py:143
  26.4 1.4 %mask_blocks.4 = bf16[256,768]{1,0:T(8,128)(2,1)} custom-call(s32[2,24]{1,0:T(2,128)S(1)} %get-tuple-element.12.mask_hbm, bf16[256,3072]{1,0:T(8,128)(2,1)S(1)} %get-tuple-element.14.a_hbm), custom_call_target="tpu_custom_call" | custom-call | tf_op jit(solution)/shard_map/cond/branch_1_fun/mask_blocks/pallas_call | solution.py:61
  27.8 4.4 %all-to-all-done = bf16[32,16,256]{2,1,0:T(8,128)(2,1)} async-done(((bf16[32,16,256]{2,1,0:T(8,128)(2,1)}), bf16[32,16,256]{2,1,0:T(8,128)(2,1)}, u32[]{:S(2)}, u32[]{:S(2)}) %all-to-all-start) | async-done | bytes 262176 | tf_op jit(solution)/shard_map/cond/branch_1_fun/all_to_all | solution.py:149
  32.2 2.4 %all-gather = bf16[64,16,256]{2,1,0:T(8,128)(2,1)S(1)} all-gather(bf16[32,16,256]{2,1,0:T(8,128)(2,1)} %all-to-all-done), channel_id=2, replica_groups=mesh['y'=8,'c'=2,'zh'=2,'x'=4,'zl'=6] {'c'}, dimensions={0}, use_global_device_ids=true | all-gather | bytes 786432 | tf_op jit(solution)/shard_map/cond/branch_1_fun/all_gather | solution.py:150
  34.6 0.0 collective-permute-done
  34.6 0.0 collective-permute-done.1.refs_1_
  34.6 0.0 collective-permute-done.2.refs_2_
  34.6 0.0 copy-start
  34.6 2.0 %product.1 = s16[12,144,128]{2,1,0:T(8,128)(2,1)S(1)} custom-call(s32[1]{0:T(128)} %bitcast.1.me_ref, bf16[2,4,8,16,256]{4,3,2,1,0:T(8,128)(2,1)S(1)} %get-tuple-element.24.f_ref, bf16[256,768]{1,0:T(8,128)(2,1)} %get-tuple-element.25.refs_0_, bf16[256,768]{1,0:T(8,128)(2,1)S(1)} %collective-permute-done.1.refs_1_, ...), custom_call_target="tpu_custom_call" | custom-call | tf_op jit(solution)/shard_map/product/pallas_call | solution.py:110
  36.6 36.4 %all_to_all.9.q_ref = s16[12,144,128]{2,1,0:T(8,128)(2,1)S(1)} all-to-all(s16[12,144,128]{2,1,0:T(8,128)(2,1)S(1)} %product.1), channel_id=1, replica_groups=mesh['y'=8,'c'=2,'zh'=2,'x'=4,'zl'=6] {'zh','zl'}, dimensions={0} | all-to-all | bytes 884736 | tf_op jit(solution)/shard_map/all_to_all | solution.py:170
  73.1 0.0 copy-done
  73.1 1.2 %finish.1 = f32[64,256]{1,0:T(8,128)} custom-call(s16[12,144,128]{2,1,0:T(8,128)(2,1)S(1)} %all_to_all.9.q_ref, bf16[64,256]{1,0:T(8,128)(2,1)S(1)} %copy-done), custom_call_target="tpu_custom_call" | custom-call | tf_op jit(solution)/shard_map/finish/pallas_call | solution.py:134
Async XLA Ops:
  0.0 9.5 %copy-start.2 = (s32[1,2,24]{2,1,0:T(2,128)S(1)}, s32[1,2,24]{2,1,0:T(2,128)}, u32[]{:S(2)}) copy-start(s32[1,2,24]{2,1,0:T(2,128)} %param.7) | copy-start | bytes 580
  0.0 9.5 %copy-start.1 = (bf16[1,256,3072]{2,1,0:T(8,128)(2,1)S(1)}, bf16[1,256,3072]{2,1,0:T(8,128)(2,1)}, u32[]{:S(2)}) copy-start(bf16[1,256,3072]{2,1,0:T(8,128)(2,1)} %param.6) | copy-start | bytes 4718596
  0.0 9.5 %copy-start.3 = (bf16[1,256,16]{1,2,0:T(8,128)(2,1)S(1)}, bf16[1,256,16]{1,2,0:T(8,128)(2,1)}, u32[]{:S(2)}) copy-start(bf16[1,256,16]{1,2,0:T(8,128)(2,1)} %param.8) | copy-start | bytes 24580
  1.5 33.1 %collective-permute-start.1 = (bf16[256,768]{1,0:T(8,128)(2,1)S(1)}, bf16[256,768]{1,0:T(8,128)(2,1)S(1)}, u32[]{:S(2)}, u32[]{:S(2)}) collective-permute-start(bf16[256,768]{1,0:T(8,128)(2,1)S(1)} %get-tuple-element.26), channel_id=1, source_target_pairs={{0,6},{6,12},{12,18},{18,0},{1,7},{7,13},{13,19},{19,1},{2,8},{8,1... | collective-permute-start | bytes 1179656 | tf_op jit(solution)/shard_map/ppermute | solution.py:143
  4.9 29.7 %collective-permute-start.2 = (bf16[256,768]{1,0:T(8,128)(2,1)S(1)}, bf16[256,768]{1,0:T(8,128)(2,1)S(1)}, u32[]{:S(2)}, u32[]{:S(2)}) collective-permute-start(bf16[256,768]{1,0:T(8,128)(2,1)S(1)} %get-tuple-element.22), channel_id=1, source_target_pairs={{0,12},{6,18},{12,0},{18,6},{1,13},{7,19},{13,1},{19,7},{2,14},{8,... | collective-permute-start | bytes 1179656 | tf_op jit(solution)/shard_map/ppermute | solution.py:143
  10.3 21.9 %all-to-all-start = ((bf16[32,16,256]{2,1,0:T(8,128)(2,1)}), bf16[32,16,256]{2,1,0:T(8,128)(2,1)}, u32[]{:S(2)}, u32[]{:S(2)}) async-start(bf16[32,16,256]{2,1,0:T(8,128)(2,1)} %broadcast_in_dim.0), calls=%async_computation | async-start | bytes 524288 | tf_op jit(solution)/shard_map/cond/branch_1_fun/all_to_all | solution.py:149
  21.8 12.8 %collective-permute-start = (bf16[256,768]{1,0:T(8,128)(2,1)S(1)}, bf16[256,768]{1,0:T(8,128)(2,1)}, u32[]{:S(2)}, u32[]{:S(2)}) collective-permute-start(bf16[256,768]{1,0:T(8,128)(2,1)S(1)} %mask_blocks.3), channel_id=1, source_target_pairs={{0,18},{6,0},{12,6},{18,12},{1,19},{7,1},{13,7},{19,13},{2,20},{8,... | collective-permute-start | bytes 1179656 | tf_op jit(solution)/shard_map/cond/branch_1_fun/ppermute | solution.py:143
  34.6 38.5 %copy-start = (bf16[64,256]{1,0:T(8,128)(2,1)S(1)}, bf16[64,256]{1,0:T(8,128)(2,1)}, u32[]{:S(2)}) copy-start(bf16[64,256]{1,0:T(8,128)(2,1)} %t_ref.1) | copy-start | bytes 98308

commit v10 on v8

--- a/solution.py
+++ b/solution.py
@@ -19,6 +19,7 @@
 TGT = Z * ROWS
 SEG = TGT // ZH
 TILE = 128
+SUB = 8
 STEP = 8.0
 TOP = 32000.0
 MIB = 1 << 20
@@ -80,7 +81,7 @@
     for k in range(X):
         x = lax.rem(me_ref[0] + X - k, X)
         feats.append(jnp.concatenate([f_ref[c, x, y] for y in range(Y) for c in range(CORES)], axis=0))
-    lane = lax.broadcasted_iota(jnp.int32, (16, TILE), 1)
+    lane = lax.broadcasted_iota(jnp.int32, (SUB, TILE), 1)
     wide = 2 * TILE
     for i in range(TGT // wide):
         total = jnp.zeros((CLS, wide), jnp.float32)
@@ -98,11 +99,11 @@
             rows = slice(b * ROWS, (b + 1) * ROWS)
             o_ref[z, 0:ROWS, :] = coded[rows, 0:TILE].astype(jnp.int16)
             o_ref[z, ROWS : 2 * ROWS, :] = coded[rows, TILE : 2 * TILE].astype(jnp.int16)
-            scales = jnp.zeros((16, TILE), jnp.int32)
-            for k in range(4):
-                at = b * ROWS + 16 * k
-                scales = jnp.where(lane // 32 == k, power[at : at + 16, :], scales)
-            o_ref[z, 2 * ROWS : 2 * ROWS + 16, :] = scales.astype(jnp.int16)
+            scales = jnp.zeros((SUB, TILE), jnp.int32)
+            for k in range(ROWS // SUB):
+                at = b * ROWS + SUB * k
+                scales = jnp.where(lane // (TILE * SUB // ROWS) == k, power[at : at + SUB, :], scales)
+            o_ref[z, 2 * ROWS : 2 * ROWS + SUB, :] = scales.astype(jnp.int16)
 
 
 def product(me, feats, blocks):
@@ -111,7 +112,7 @@
         product_kernel,
         in_specs=[pl.BlockSpec(memory_space=pltpu.SMEM)] + [whole] * (1 + X),
         out_specs=whole,
-        out_shape=jax.ShapeDtypeStruct((Z, 2 * ROWS + 16, TILE), jnp.int16),
+        out_shape=jax.ShapeDtypeStruct((Z, 2 * ROWS + SUB, TILE), jnp.int16),
         compiler_params=pltpu.CompilerParams(vmem_limit_bytes=8 * MIB),
         name="product",
     )(me, feats, *blocks)
@@ -121,9 +122,10 @@
     left = jnp.zeros((ROWS, TILE), jnp.float32)
     right = jnp.zeros((ROWS, TILE), jnp.float32)
     for z in range(Z):
-        power = q_ref[z, 2 * ROWS : 2 * ROWS + 16, :].astype(jnp.float32)
+        power = q_ref[z, 2 * ROWS : 2 * ROWS + SUB, :].astype(jnp.float32)
         scale = jnp.exp2(power * (1.0 / STEP)) * (1.0 / TOP)
-        scale = jnp.concatenate([scale[:, 32 * k : 32 * k + 1] for k in range(4)], axis=0)
+        step = TILE * SUB // ROWS
+        scale = jnp.concatenate([scale[:, k : k + 1] for k in range(0, TILE, step)], axis=0)
         left += q_ref[z, 0:ROWS, :].astype(jnp.float32) * scale
         right += q_ref[z, ROWS : 2 * ROWS, :].astype(jnp.float32) * scale
     o_ref[:, 0:TILE] = 0.9 * left + 0.1 * t_ref[:, 0:TILE].astype(jnp.float32)

time: 73.8 us -> 73.1 us (level)
  no operation moved by 1% of the time
where the time goes in v10:
time: 73.1 us; the launch traced here: 72.8 us
  blocking collectives  37.1 us (51%)
  starting transfers between devices  22.9 us (31%)
  waiting for transfers between devices  6 us (8%)
  Pallas kernels  5.93 us (8%)
  local copies, waits for them, and re-layouts  0.74 us (1%)
    all_to_all x1, blocking collectives, local(): coded = lax.all_to_all(coded, ('zh', 'zl'), 0, 0, tiled=True)  34.7 us
    ppermute x3, starting transfers between devices, shift(): return lax.ppermute(block, 'x', [(i, (i + k) % X) for i in range(X)])  11.5 us
    all_to_all x1, starting transfers between devices, others(): feats = lax.all_to_all(copies, ('x', 'y'), 0, 0, tiled=True)  11.4 us
    ppermute x3, waiting for transfers between devices, shift(): return lax.ppermute(block, 'x', [(i, (i + k) % X) for i in range(X)])  3.01 us
    all_to_all x1, waiting for transfers between devices, others(): feats = lax.all_to_all(copies, ('x', 'y'), 0, 0, tiled=True)  2.98 us
    pallas_call x3, Pallas kernels, mask_blocks(): pl.pallas_call(functools.partial(spread_kernel if more else mask_kernel,...  2.7 us
    all_gather x1, blocking collectives, others(): feats = lax.all_gather(feats, 'c', axis=0)  2.38 us
    pallas_call x1, Pallas kernels, product(): pl.pallas_call(product_kernel, in_specs=[pl.BlockSpec(memory_space=pltpu....  2.03 us
  transfers between devices with their start and end apart: 4, of which 2 were waited for; matrix products, arithmetic and copies ran while one was open for 1% of the time, Pallas kernels for 2%

profile of v10, /device:TPU:8, one launch (start us, length us, event | category | flops | bytes accessed | tf_op | source)
XLA Modules:
  0.0 72.8 jit_solution(16788535100194754678)
XLA Ops:
  0.0 0.0 copy-start.2
  0.0 0.0 copy-start.1
  0.0 0.0 copy-start.3
  0.0 1.2 %mask_blocks.5 = bf16[256,768]{1,0:T(8,128)(2,1)S(1)} custom-call(s32[2,24]{1,0:T(2,128)} %bitcast.10, bf16[256,3072]{1,0:T(8,128)(2,1)} %bitcast.7), custom_call_target="tpu_custom_call" | custom-call | tf_op jit(solution)/shard_map/mask_blocks/pallas_call | solution.py:62
  1.2 4.9 %collective-permute-start.2 = (bf16[256,768]{1,0:T(8,128)(2,1)S(1)}, bf16[256,768]{1,0:T(8,128)(2,1)S(1)}, u32[]{:S(2)}, u32[]{:S(2)}) collective-permute-start(bf16[256,768]{1,0:T(8,128)(2,1)S(1)} %mask_blocks.5), channel_id=1, source_target_pairs={{0,12},{6,18},{12,0},{18,6},{1,13},{7,19},{13,1},{19,7},{2,14},{8,... | collective-permute-start | bytes 1179656 | tf_op jit(solution)/shard_map/ppermute | solution.py:145
  6.2 0.0 copy-done.2
  6.2 0.0 copy-done.1
  6.2 0.0 copy-done.3
  6.2 28.6 %conditional.1 = (bf16[256,768]{1,0:T(8,128)(2,1)S(1)}, bf16[256,768]{1,0:T(8,128)(2,1)}, bf16[256,768]{1,0:T(8,128)(2,1)}, bf16[2,4,8,16,256]{4,3,2,1,0:T(8,128)(2,1)S(1)}) conditional(s32[]{:T(128)} %convert_element_type.3, () %tuple.17, (s32[2,24]{1,0:T(2,128)S(1)}, bf16[256,3072]{1,0:T(8,128)(2,1)S(1)}, bf16[16,256]{1,0:T(8,128)(2,1)S(1)}) %tuple.24), branch_computations={%region_0.0_spmd, %region_1.0_spmd} | conditional | bytes 4989072 | solution.py:169
  6.2 0.7 broadcast_in_dim.0
  7.0 11.4 %all-to-all-start = ((bf16[32,16,256]{2,1,0:T(8,128)(2,1)}), bf16[32,16,256]{2,1,0:T(8,128)(2,1)}, u32[]{:S(2)}, u32[]{:S(2)}) async-start(bf16[32,16,256]{2,1,0:T(8,128)(2,1)} %broadcast_in_dim.0), calls=%async_computation | async-start | bytes 524288 | tf_op jit(solution)/shard_map/cond/branch_1_fun/all_to_all | solution.py:151
  18.4 0.8 %mask_blocks.3 = (bf16[256,768]{1,0:T(8,128)(2,1)S(1)}, bf16[256,768]{1,0:T(8,128)(2,1)S(1)}) custom-call(s32[2,24]{1,0:T(2,128)S(1)} %get-tuple-element.12.mask_hbm, bf16[256,3072]{1,0:T(8,128)(2,1)S(1)} %get-tuple-element.15.a_hbm), custom_call_target="tpu_custom_call" | custom-call | tf_op jit(solution)/shard_map/cond/branch_1_fun/mask_blocks/pallas_call | solution.py:62
  19.2 4.6 %collective-permute-start.1 = (bf16[256,768]{1,0:T(8,128)(2,1)S(1)}, bf16[256,768]{1,0:T(8,128)(2,1)}, u32[]{:S(2)}, u32[]{:S(2)}) collective-permute-start(bf16[256,768]{1,0:T(8,128)(2,1)S(1)} %get-tuple-element.16), channel_id=1, source_target_pairs={{0,18},{6,0},{12,6},{18,12},{1,19},{7,1},{13,7},{19,13},{2,20},{8,... | collective-permute-start | bytes 1179656 | tf_op jit(solution)/shard_map/cond/branch_1_fun/ppermute | solution.py:145
  23.8 1.9 %collective-permute-start = (bf16[256,768]{1,0:T(8,128)(2,1)S(1)}, bf16[256,768]{1,0:T(8,128)(2,1)}, u32[]{:S(2)}, u32[]{:S(2)}) collective-permute-start(bf16[256,768]{1,0:T(8,128)(2,1)S(1)} %get-tuple-element.14), channel_id=1, source_target_pairs={{0,6},{6,12},{12,18},{18,0},{1,7},{7,13},{13,19},{19,1},{2,8},{8,1... | collective-permute-start | bytes 1179656 | tf_op jit(solution)/shard_map/cond/branch_1_fun/ppermute | solution.py:145
  25.8 0.7 mask_blocks.4
  26.4 3.0 %all-to-all-done = bf16[32,16,256]{2,1,0:T(8,128)(2,1)} async-done(((bf16[32,16,256]{2,1,0:T(8,128)(2,1)}), bf16[32,16,256]{2,1,0:T(8,128)(2,1)}, u32[]{:S(2)}, u32[]{:S(2)}) %all-to-all-start) | async-done | bytes 262176 | tf_op jit(solution)/shard_map/cond/branch_1_fun/all_to_all | solution.py:151
  29.4 2.4 %all-gather = bf16[64,16,256]{2,1,0:T(8,128)(2,1)S(1)} all-gather(bf16[32,16,256]{2,1,0:T(8,128)(2,1)} %all-to-all-done), channel_id=2, replica_groups=mesh['y'=8,'c'=2,'zh'=2,'x'=4,'zl'=6] {'c'}, dimensions={0}, use_global_device_ids=true | all-gather | bytes 786432 | tf_op jit(solution)/shard_map/cond/branch_1_fun/all_gather | solution.py:152
  31.8 0.0 collective-permute-done.1
  31.8 3.0 %collective-permute-done = bf16[256,768]{1,0:T(8,128)(2,1)} collective-permute-done((bf16[256,768]{1,0:T(8,128)(2,1)S(1)}, bf16[256,768]{1,0:T(8,128)(2,1)}, u32[]{:S(2)}, u32[]{:S(2)}) %collective-permute-start) | collective-permute-done | bytes 393248 | tf_op jit(solution)/shard_map/cond/branch_1_fun/ppermute | solution.py:145
  34.8 0.0 collective-permute-done.2.refs_2_
  34.8 0.0 copy-start
  34.8 2.0 %product.1 = s16[12,136,128]{2,1,0:T(8,128)(2,1)S(1)} custom-call(s32[1]{0:T(128)} %bitcast.1.me_ref, bf16[2,4,8,16,256]{4,3,2,1,0:T(8,128)(2,1)S(1)} %get-tuple-element.24.f_ref, bf16[256,768]{1,0:T(8,128)(2,1)S(1)} %get-tuple-element.25.refs_0_, bf16[256,768]{1,0:T(8,128)(2,1)} %get-tuple-element.26.refs_1_, ...), custom_call_target="tpu_custom_call" | custom-call | tf_op jit(solution)/shard_map/product/pallas_call | solution.py:111
  36.9 34.7 %all_to_all.9.q_ref = s16[12,136,128]{2,1,0:T(8,128)(2,1)S(1)} all-to-all(s16[12,136,128]{2,1,0:T(8,128)(2,1)S(1)} %product.1), channel_id=1, replica_groups=mesh['y'=8,'c'=2,'zh'=2,'x'=4,'zl'=6] {'zh','zl'}, dimensions={0} | all-to-all | bytes 835584 | tf_op jit(solution)/shard_map/all_to_all | solution.py:172
  71.6 0.0 copy-done
  71.6 1.2 %finish.1 = f32[64,256]{1,0:T(8,128)} custom-call(s16[12,136,128]{2,1,0:T(8,128)(2,1)S(1)} %all_to_all.9.q_ref, bf16[64,256]{1,0:T(8,128)(2,1)S(1)} %copy-done), custom_call_target="tpu_custom_call" | custom-call | tf_op jit(solution)/shard_map/finish/pallas_call | solution.py:136
Async XLA Ops:
  0.0 6.2 %copy-start.2 = (s32[1,2,24]{2,1,0:T(2,128)S(1)}, s32[1,2,24]{2,1,0:T(2,128)}, u32[]{:S(2)}) copy-start(s32[1,2,24]{2,1,0:T(2,128)} %param.7) | copy-start | bytes 580
  0.0 6.2 %copy-start.1 = (bf16[1,256,3072]{2,1,0:T(8,128)(2,1)S(1)}, bf16[1,256,3072]{2,1,0:T(8,128)(2,1)}, u32[]{:S(2)}) copy-start(bf16[1,256,3072]{2,1,0:T(8,128)(2,1)} %param.6) | copy-start | bytes 4718596
  0.0 6.2 %copy-start.3 = (bf16[1,256,16]{1,2,0:T(8,128)(2,1)S(1)}, bf16[1,256,16]{1,2,0:T(8,128)(2,1)}, u32[]{:S(2)}) copy-start(bf16[1,256,16]{1,2,0:T(8,128)(2,1)} %param.8) | copy-start | bytes 24580
  1.2 33.6 %collective-permute-start.2 = (bf16[256,768]{1,0:T(8,128)(2,1)S(1)}, bf16[256,768]{1,0:T(8,128)(2,1)S(1)}, u32[]{:S(2)}, u32[]{:S(2)}) collective-permute-start(bf16[256,768]{1,0:T(8,128)(2,1)S(1)} %mask_blocks.5), channel_id=1, source_target_pairs={{0,12},{6,18},{12,0},{18,6},{1,13},{7,19},{13,1},{19,7},{2,14},{8,... | collective-permute-start | bytes 1179656 | tf_op jit(solution)/shard_map/ppermute | solution.py:145
  7.0 22.5 %all-to-all-start = ((bf16[32,16,256]{2,1,0:T(8,128)(2,1)}), bf16[32,16,256]{2,1,0:T(8,128)(2,1)}, u32[]{:S(2)}, u32[]{:S(2)}) async-start(bf16[32,16,256]{2,1,0:T(8,128)(2,1)} %broadcast_in_dim.0), calls=%async_computation | async-start | bytes 524288 | tf_op jit(solution)/shard_map/cond/branch_1_fun/all_to_all | solution.py:151
  19.2 12.6 %collective-permute-start.1 = (bf16[256,768]{1,0:T(8,128)(2,1)S(1)}, bf16[256,768]{1,0:T(8,128)(2,1)}, u32[]{:S(2)}, u32[]{:S(2)}) collective-permute-start(bf16[256,768]{1,0:T(8,128)(2,1)S(1)} %get-tuple-element.16), channel_id=1, source_target_pairs={{0,18},{6,0},{12,6},{18,12},{1,19},{7,1},{13,7},{19,13},{2,20},{8,... | collective-permute-start | bytes 1179656 | tf_op jit(solution)/shard_map/cond/branch_1_fun/ppermute | solution.py:145
  23.8 11.0 %collective-permute-start = (bf16[256,768]{1,0:T(8,128)(2,1)S(1)}, bf16[256,768]{1,0:T(8,128)(2,1)}, u32[]{:S(2)}, u32[]{:S(2)}) collective-permute-start(bf16[256,768]{1,0:T(8,128)(2,1)S(1)} %get-tuple-element.14), channel_id=1, source_target_pairs={{0,6},{6,12},{12,18},{18,0},{1,7},{7,13},{13,19},{19,1},{2,8},{8,1... | collective-permute-start | bytes 1179656 | tf_op jit(solution)/shard_map/cond/branch_1_fun/ppermute | solution.py:145
  34.8 36.7 %copy-start = (bf16[64,256]{1,0:T(8,128)(2,1)S(1)}, bf16[64,256]{1,0:T(8,128)(2,1)}, u32[]{:S(2)}) copy-start(bf16[64,256]{1,0:T(8,128)(2,1)} %t_ref.1) | copy-start | bytes 98308

commit v11 on v10

--- a/solution.py
+++ b/solution.py
@@ -75,20 +75,30 @@
     )(mask, a, *more)
 
 
-def product_kernel(me_ref, f_ref, *refs):
-    o_ref = refs[X]
+def product_kernel(me_ref, f_ref, own_ref, far_ref, up_ref, down_ref, o_ref, near_ref, total_ref, sems):
+    copies = [
+        pltpu.make_async_copy(ref, near_ref.at[n], sems.at[n]) for n, ref in enumerate((up_ref, down_ref))
+    ]
+    for copy in copies:
+        copy.start()
     feats = []
-    for k in range(X):
+    for k in (0, 2, 1, 3):
         x = lax.rem(me_ref[0] + X - k, X)
         feats.append(jnp.concatenate([f_ref[c, x, y] for y in range(Y) for c in range(CORES)], axis=0))
     lane = lax.broadcasted_iota(jnp.int32, (SUB, TILE), 1)
     wide = 2 * TILE
     for i in range(TGT // wide):
-        total = jnp.zeros((CLS, wide), jnp.float32)
-        for k in range(X):
-            total += jnp.dot(
-                feats[k], refs[k][:, i * wide : (i + 1) * wide], preferred_element_type=jnp.float32
-            )
+        columns = slice(i * wide, (i + 1) * wide)
+        total = jnp.dot(feats[0], own_ref[:, columns], preferred_element_type=jnp.float32)
+        total += jnp.dot(feats[1], far_ref[:, columns], preferred_element_type=jnp.float32)
+        total_ref[i] = total
+    for copy in copies:
+        copy.wait()
+    for i in range(TGT // wide):
+        columns = slice(i * wide, (i + 1) * wide)
+        total = total_ref[i]
+        for n in range(2):
+            total += jnp.dot(feats[2 + n], near_ref[n, :, columns], preferred_element_type=jnp.float32)
         total = total.T
         top = jnp.max(jnp.abs(total), axis=1, keepdims=True)
         power = jnp.ceil(jnp.log2(jnp.maximum(top, 1e-30)) * STEP)
@@ -106,16 +116,21 @@
             o_ref[z, 2 * ROWS : 2 * ROWS + SUB, :] = scales.astype(jnp.int16)
 
 
-def product(me, feats, blocks):
-    whole = pl.BlockSpec(memory_space=pltpu.VMEM)
+def product(me, feats, own, far, up, down):
+    whole, anywhere = pl.BlockSpec(memory_space=pltpu.VMEM), pl.BlockSpec(memory_space=pl.ANY)
     return pl.pallas_call(
         product_kernel,
-        in_specs=[pl.BlockSpec(memory_space=pltpu.SMEM)] + [whole] * (1 + X),
+        in_specs=[pl.BlockSpec(memory_space=pltpu.SMEM)] + [whole] * 3 + [anywhere] * 2,
         out_specs=whole,
         out_shape=jax.ShapeDtypeStruct((Z, 2 * ROWS + SUB, TILE), jnp.int16),
+        scratch_shapes=[
+            pltpu.VMEM((2, SRC, TGT), jnp.bfloat16),
+            pltpu.VMEM((TGT // (2 * TILE), CLS, 2 * TILE), jnp.float32),
+            pltpu.SemaphoreType.DMA((2,)),
+        ],
         compiler_params=pltpu.CompilerParams(vmem_limit_bytes=8 * MIB),
         name="product",
-    )(me, feats, *blocks)
+    )(me, feats, own, far, up, down)
 
 
 def finish_kernel(q_ref, t_ref, o_ref):
@@ -168,7 +183,7 @@
     a, _ = lax.optimization_barrier((a, far))
     feats, own, up, down = lax.cond(me < X, others, nothing, (mask, a, features[0].T))
     feats = feats.reshape(CORES, X, Y, HELD, SRC)
-    coded = product(me[None], feats, [own, up, shift(far, 2), down])
+    coded = product(me[None], feats, own, shift(far, 2), up, down)
     coded = lax.all_to_all(coded, ("zh", "zl"), 0, 0, tiled=True)
     return finish(coded, teleport)
 

time: 73.1 us -> 73.2 us (level)
  no operation moved by 1% of the time
where the time goes in v11:
time: 73.2 us; the launch traced here: 72.9 us
  blocking collectives  37.1 us (51%)
  starting transfers between devices  22.9 us (31%)
  Pallas kernels  6.02 us (8%)
  waiting for transfers between devices  6 us (8%)
  local copies, waits for them, and re-layouts  0.74 us (1%)
    all_to_all x1, blocking collectives, local(): coded = lax.all_to_all(coded, ('zh', 'zl'), 0, 0, tiled=True)  34.7 us
    ppermute x3, starting transfers between devices, shift(): return lax.ppermute(block, 'x', [(i, (i + k) % X) for i in range(X)])  11.5 us
    all_to_all x1, starting transfers between devices, others(): feats = lax.all_to_all(copies, ('x', 'y'), 0, 0, tiled=True)  11.4 us
    ppermute x3, waiting for transfers between devices, shift(): return lax.ppermute(block, 'x', [(i, (i + k) % X) for i in range(X)])  3.01 us
    all_to_all x1, waiting for transfers between devices, others(): feats = lax.all_to_all(copies, ('x', 'y'), 0, 0, tiled=True)  2.98 us
    pallas_call x3, Pallas kernels, mask_blocks(): pl.pallas_call(functools.partial(spread_kernel if more else mask_kernel,...  2.7 us
    all_gather x1, blocking collectives, others(): feats = lax.all_gather(feats, 'c', axis=0)  2.38 us
    pallas_call x1, Pallas kernels, product(): pl.pallas_call(product_kernel, in_specs=[pl.BlockSpec(memory_space=pltpu....  2.12 us
  transfers between devices with their start and end apart: 4, of which 2 were waited for; matrix products, arithmetic and copies ran while one was open for 1% of the time, Pallas kernels for 2%

profile of v11, /device:TPU:8, one launch (start us, length us, event | category | flops | bytes accessed | tf_op | source)
XLA Modules:
  0.0 72.9 jit_solution(6734717856123174246)
XLA Ops:
  0.0 0.0 copy-start.2
  0.0 0.0 copy-start.1
  0.0 0.0 copy-start.3
  0.0 1.2 %mask_blocks.5 = bf16[256,768]{1,0:T(8,128)(2,1)S(1)} custom-call(s32[2,24]{1,0:T(2,128)} %bitcast.10, bf16[256,3072]{1,0:T(8,128)(2,1)} %bitcast.7), custom_call_target="tpu_custom_call" | custom-call | tf_op jit(solution)/shard_map/mask_blocks/pallas_call | solution.py:62
  1.2 4.9 %collective-permute-start.2 = (bf16[256,768]{1,0:T(8,128)(2,1)S(1)}, bf16[256,768]{1,0:T(8,128)(2,1)S(1)}, u32[]{:S(2)}, u32[]{:S(2)}) collective-permute-start(bf16[256,768]{1,0:T(8,128)(2,1)S(1)} %mask_blocks.5), channel_id=1, source_target_pairs={{0,12},{6,18},{12,0},{18,6},{1,13},{7,19},{13,1},{19,7},{2,14},{8,... | collective-permute-start | bytes 1179656 | tf_op jit(solution)/shard_map/ppermute | solution.py:160
  6.2 0.0 copy-done.2
  6.2 0.0 copy-done.1
  6.2 0.0 copy-done.3
  6.2 28.6 %conditional.1 = (bf16[256,768]{1,0:T(8,128)(2,1)S(1)}, bf16[256,768]{1,0:T(8,128)(2,1)}, bf16[256,768]{1,0:T(8,128)(2,1)}, bf16[2,4,8,16,256]{4,3,2,1,0:T(8,128)(2,1)S(1)}) conditional(s32[]{:T(128)} %convert_element_type.3, () %tuple.17, (s32[2,24]{1,0:T(2,128)S(1)}, bf16[256,3072]{1,0:T(8,128)(2,1)S(1)}, bf16[16,256]{1,0:T(8,128)(2,1)S(1)}) %tuple.24), branch_computations={%region_0.0_spmd, %region_1.0_spmd} | conditional | bytes 4989072 | solution.py:184
  6.2 0.7 broadcast_in_dim.0
  7.0 11.4 %all-to-all-start = ((bf16[32,16,256]{2,1,0:T(8,128)(2,1)}), bf16[32,16,256]{2,1,0:T(8,128)(2,1)}, u32[]{:S(2)}, u32[]{:S(2)}) async-start(bf16[32,16,256]{2,1,0:T(8,128)(2,1)} %broadcast_in_dim.0), calls=%async_computation | async-start | bytes 524288 | tf_op jit(solution)/shard_map/cond/branch_1_fun/all_to_all | solution.py:166
  18.4 0.8 %mask_blocks.3 = (bf16[256,768]{1,0:T(8,128)(2,1)S(1)}, bf16[256,768]{1,0:T(8,128)(2,1)S(1)}) custom-call(s32[2,24]{1,0:T(2,128)S(1)} %get-tuple-element.12.mask_hbm, bf16[256,3072]{1,0:T(8,128)(2,1)S(1)} %get-tuple-element.15.a_hbm), custom_call_target="tpu_custom_call" | custom-call | tf_op jit(solution)/shard_map/cond/branch_1_fun/mask_blocks/pallas_call | solution.py:62
  19.2 4.6 %collective-permute-start.1 = (bf16[256,768]{1,0:T(8,128)(2,1)S(1)}, bf16[256,768]{1,0:T(8,128)(2,1)}, u32[]{:S(2)}, u32[]{:S(2)}) collective-permute-start(bf16[256,768]{1,0:T(8,128)(2,1)S(1)} %get-tuple-element.16), channel_id=1, source_target_pairs={{0,18},{6,0},{12,6},{18,12},{1,19},{7,1},{13,7},{19,13},{2,20},{8,... | collective-permute-start | bytes 1179656 | tf_op jit(solution)/shard_map/cond/branch_1_fun/ppermute | solution.py:160
  23.8 1.9 %collective-permute-start = (bf16[256,768]{1,0:T(8,128)(2,1)S(1)}, bf16[256,768]{1,0:T(8,128)(2,1)}, u32[]{:S(2)}, u32[]{:S(2)}) collective-permute-start(bf16[256,768]{1,0:T(8,128)(2,1)S(1)} %get-tuple-element.14), channel_id=1, source_target_pairs={{0,6},{6,12},{12,18},{18,0},{1,7},{7,13},{13,19},{19,1},{2,8},{8,1... | collective-permute-start | bytes 1179656 | tf_op jit(solution)/shard_map/cond/branch_1_fun/ppermute | solution.py:160
  25.8 0.7 mask_blocks.4
  26.4 3.0 %all-to-all-done = bf16[32,16,256]{2,1,0:T(8,128)(2,1)} async-done(((bf16[32,16,256]{2,1,0:T(8,128)(2,1)}), bf16[32,16,256]{2,1,0:T(8,128)(2,1)}, u32[]{:S(2)}, u32[]{:S(2)}) %all-to-all-start) | async-done | bytes 262176 | tf_op jit(solution)/shard_map/cond/branch_1_fun/all_to_all | solution.py:166
  29.4 2.4 %all-gather = bf16[64,16,256]{2,1,0:T(8,128)(2,1)S(1)} all-gather(bf16[32,16,256]{2,1,0:T(8,128)(2,1)} %all-to-all-done), channel_id=2, replica_groups=mesh['y'=8,'c'=2,'zh'=2,'x'=4,'zl'=6] {'c'}, dimensions={0}, use_global_device_ids=true | all-gather | bytes 786432 | tf_op jit(solution)/shard_map/cond/branch_1_fun/all_gather | solution.py:167
  31.8 0.0 collective-permute-done.1
  31.8 3.0 %collective-permute-done = bf16[256,768]{1,0:T(8,128)(2,1)} collective-permute-done((bf16[256,768]{1,0:T(8,128)(2,1)S(1)}, bf16[256,768]{1,0:T(8,128)(2,1)}, u32[]{:S(2)}, u32[]{:S(2)}) %collective-permute-start) | collective-permute-done | bytes 393248 | tf_op jit(solution)/shard_map/cond/branch_1_fun/ppermute | solution.py:160
  34.8 0.0 collective-permute-done.2.far_ref
  34.8 0.0 copy-start
  34.8 2.1 %product.1 = s16[12,136,128]{2,1,0:T(8,128)(2,1)S(1)} custom-call(s32[1]{0:T(128)} %bitcast.1.me_ref, bf16[2,4,8,16,256]{4,3,2,1,0:T(8,128)(2,1)S(1)} %get-tuple-element.24.f_ref, bf16[256,768]{1,0:T(8,128)(2,1)S(1)} %get-tuple-element.25.own_ref, bf16[256,768]{1,0:T(8,128)(2,1)S(1)} %collective-permute-done.2.far_ref, ...), custom_call_target="tpu_custom_call" | custom-call | tf_op jit(solution)/shard_map/product/pallas_call | solution.py:121
  37.0 34.7 %all_to_all.9.q_ref = s16[12,136,128]{2,1,0:T(8,128)(2,1)S(1)} all-to-all(s16[12,136,128]{2,1,0:T(8,128)(2,1)S(1)} %product.1), channel_id=1, replica_groups=mesh['y'=8,'c'=2,'zh'=2,'x'=4,'zl'=6] {'zh','zl'}, dimensions={0} | all-to-all | bytes 835584 | tf_op jit(solution)/shard_map/all_to_all | solution.py:187
  71.7 0.0 copy-done
  71.7 1.2 %finish.1 = f32[64,256]{1,0:T(8,128)} custom-call(s16[12,136,128]{2,1,0:T(8,128)(2,1)S(1)} %all_to_all.9.q_ref, bf16[64,256]{1,0:T(8,128)(2,1)S(1)} %copy-done), custom_call_target="tpu_custom_call" | custom-call | tf_op jit(solution)/shard_map/finish/pallas_call | solution.py:151
Async XLA Ops:
  0.0 6.2 %copy-start.2 = (s32[1,2,24]{2,1,0:T(2,128)S(1)}, s32[1,2,24]{2,1,0:T(2,128)}, u32[]{:S(2)}) copy-start(s32[1,2,24]{2,1,0:T(2,128)} %param.7) | copy-start | bytes 580
  0.0 6.2 %copy-start.1 = (bf16[1,256,3072]{2,1,0:T(8,128)(2,1)S(1)}, bf16[1,256,3072]{2,1,0:T(8,128)(2,1)}, u32[]{:S(2)}) copy-start(bf16[1,256,3072]{2,1,0:T(8,128)(2,1)} %param.6) | copy-start | bytes 4718596
  0.0 6.2 %copy-start.3 = (bf16[1,256,16]{1,2,0:T(8,128)(2,1)S(1)}, bf16[1,256,16]{1,2,0:T(8,128)(2,1)}, u32[]{:S(2)}) copy-start(bf16[1,256,16]{1,2,0:T(8,128)(2,1)} %param.8) | copy-start | bytes 24580
  1.2 33.6 %collective-permute-start.2 = (bf16[256,768]{1,0:T(8,128)(2,1)S(1)}, bf16[256,768]{1,0:T(8,128)(2,1)S(1)}, u32[]{:S(2)}, u32[]{:S(2)}) collective-permute-start(bf16[256,768]{1,0:T(8,128)(2,1)S(1)} %mask_blocks.5), channel_id=1, source_target_pairs={{0,12},{6,18},{12,0},{18,6},{1,13},{7,19},{13,1},{19,7},{2,14},{8,... | collective-permute-start | bytes 1179656 | tf_op jit(solution)/shard_map/ppermute | solution.py:160
  7.0 22.5 %all-to-all-start = ((bf16[32,16,256]{2,1,0:T(8,128)(2,1)}), bf16[32,16,256]{2,1,0:T(8,128)(2,1)}, u32[]{:S(2)}, u32[]{:S(2)}) async-start(bf16[32,16,256]{2,1,0:T(8,128)(2,1)} %broadcast_in_dim.0), calls=%async_computation | async-start | bytes 524288 | tf_op jit(solution)/shard_map/cond/branch_1_fun/all_to_all | solution.py:166
  19.2 12.6 %collective-permute-start.1 = (bf16[256,768]{1,0:T(8,128)(2,1)S(1)}, bf16[256,768]{1,0:T(8,128)(2,1)}, u32[]{:S(2)}, u32[]{:S(2)}) collective-permute-start(bf16[256,768]{1,0:T(8,128)(2,1)S(1)} %get-tuple-element.16), channel_id=1, source_target_pairs={{0,18},{6,0},{12,6},{18,12},{1,19},{7,1},{13,7},{19,13},{2,20},{8,... | collective-permute-start | bytes 1179656 | tf_op jit(solution)/shard_map/cond/branch_1_fun/ppermute | solution.py:160
  23.8 11.0 %collective-permute-start = (bf16[256,768]{1,0:T(8,128)(2,1)S(1)}, bf16[256,768]{1,0:T(8,128)(2,1)}, u32[]{:S(2)}, u32[]{:S(2)}) collective-permute-start(bf16[256,768]{1,0:T(8,128)(2,1)S(1)} %get-tuple-element.14), channel_id=1, source_target_pairs={{0,6},{6,12},{12,18},{18,0},{1,7},{7,13},{13,19},{19,1},{2,8},{8,1... | collective-permute-start | bytes 1179656 | tf_op jit(solution)/shard_map/cond/branch_1_fun/ppermute | solution.py:160
  34.8 36.8 %copy-start = (bf16[64,256]{1,0:T(8,128)(2,1)S(1)}, bf16[64,256]{1,0:T(8,128)(2,1)}, u32[]{:S(2)}) copy-start(bf16[64,256]{1,0:T(8,128)(2,1)} %t_ref.1) | copy-start | bytes 98308

commit v12 on v10

--- a/solution.py
+++ b/solution.py
@@ -80,7 +80,7 @@
     feats = []
     for k in range(X):
         x = lax.rem(me_ref[0] + X - k, X)
-        feats.append(jnp.concatenate([f_ref[c, x, y] for y in range(Y) for c in range(CORES)], axis=0))
+        feats.append(jnp.concatenate([f_ref[c, y, x] for y in range(Y) for c in range(CORES)], axis=0))
     lane = lax.broadcasted_iota(jnp.int32, (SUB, TILE), 1)
     wide = 2 * TILE
     for i in range(TGT // wide):
@@ -148,7 +148,7 @@
 def others(operands):
     mask, a, feats = operands
     copies = jnp.broadcast_to(feats[None], (X * Y, HELD, SRC))
-    feats = lax.all_to_all(copies, ("x", "y"), 0, 0, tiled=True)
+    feats = lax.all_to_all(copies, ("y", "x"), 0, 0, tiled=True)
     feats = lax.all_gather(feats, "c", axis=0)
     up, down = mask_blocks((1, 3), mask, a, limit=16)
     own_a, _ = lax.optimization_barrier((a, up))
@@ -167,7 +167,7 @@
     me = lax.axis_index("x").astype(jnp.int32)
     a, _ = lax.optimization_barrier((a, far))
     feats, own, up, down = lax.cond(me < X, others, nothing, (mask, a, features[0].T))
-    feats = feats.reshape(CORES, X, Y, HELD, SRC)
+    feats = feats.reshape(CORES, Y, X, HELD, SRC)
     coded = product(me[None], feats, [own, up, shift(far, 2), down])
     coded = lax.all_to_all(coded, ("zh", "zl"), 0, 0, tiled=True)
     return finish(coded, teleport)

time: 73.1 us -> 73 us (level)
  no operation moved by 1% of the time
where the time goes in v12:
time: 73 us; the launch traced here: 72.7 us
  blocking collectives  37 us (51%)
  starting transfers between devices  22.9 us (31%)
  waiting for transfers between devices  6 us (8%)
  Pallas kernels  5.94 us (8%)
  local copies, waits for them, and re-layouts  0.74 us (1%)
    all_to_all x1, blocking collectives, local(): coded = lax.all_to_all(coded, ('zh', 'zl'), 0, 0, tiled=True)  34.6 us
    ppermute x3, starting transfers between devices, shift(): return lax.ppermute(block, 'x', [(i, (i + k) % X) for i in range(X)])  11.4 us
    all_to_all x1, starting transfers between devices, others(): feats = lax.all_to_all(copies, ('y', 'x'), 0, 0, tiled=True)  11.4 us
    ppermute x3, waiting for transfers between devices, shift(): return lax.ppermute(block, 'x', [(i, (i + k) % X) for i in range(X)])  3.14 us
    all_to_all x1, waiting for transfers between devices, others(): feats = lax.all_to_all(copies, ('y', 'x'), 0, 0, tiled=True)  2.85 us
    pallas_call x3, Pallas kernels, mask_blocks(): pl.pallas_call(functools.partial(spread_kernel if more else mask_kernel,...  2.7 us
    all_gather x1, blocking collectives, others(): feats = lax.all_gather(feats, 'c', axis=0)  2.38 us
    pallas_call x1, Pallas kernels, product(): pl.pallas_call(product_kernel, in_specs=[pl.BlockSpec(memory_space=pltpu....  2.04 us
  transfers between devices with their start and end apart: 4, of which 2 were waited for; matrix products, arithmetic and copies ran while one was open for 1% of the time, Pallas kernels for 2%

profile of v12, /device:TPU:8, one launch (start us, length us, event | category | flops | bytes accessed | tf_op | source)
XLA Modules:
  0.0 72.7 jit_solution(1331874708494551571)
XLA Ops:
  0.0 0.0 copy-start.2
  0.0 0.0 copy-start.1
  0.0 0.0 copy-start.3
  0.0 1.2 %mask_blocks.5 = bf16[256,768]{1,0:T(8,128)(2,1)S(1)} custom-call(s32[2,24]{1,0:T(2,128)} %bitcast.10, bf16[256,3072]{1,0:T(8,128)(2,1)} %bitcast.7), custom_call_target="tpu_custom_call" | custom-call | tf_op jit(solution)/shard_map/mask_blocks/pallas_call | solution.py:62
  1.2 4.9 %collective-permute-start.2 = (bf16[256,768]{1,0:T(8,128)(2,1)S(1)}, bf16[256,768]{1,0:T(8,128)(2,1)S(1)}, u32[]{:S(2)}, u32[]{:S(2)}) collective-permute-start(bf16[256,768]{1,0:T(8,128)(2,1)S(1)} %mask_blocks.5), channel_id=1, source_target_pairs={{0,12},{6,18},{12,0},{18,6},{1,13},{7,19},{13,1},{19,7},{2,14},{8,... | collective-permute-start | bytes 1179656 | tf_op jit(solution)/shard_map/ppermute | solution.py:145
  6.2 0.0 copy-done.2
  6.2 0.0 copy-done.1
  6.2 0.0 copy-done.3
  6.2 28.5 %conditional.1 = (bf16[256,768]{1,0:T(8,128)(2,1)S(1)}, bf16[256,768]{1,0:T(8,128)(2,1)}, bf16[256,768]{1,0:T(8,128)(2,1)}, bf16[2,8,4,16,256]{4,3,2,1,0:T(8,128)(2,1)S(1)}) conditional(s32[]{:T(128)} %convert_element_type.3, () %tuple.17, (s32[2,24]{1,0:T(2,128)S(1)}, bf16[256,3072]{1,0:T(8,128)(2,1)S(1)}, bf16[16,256]{1,0:T(8,128)(2,1)S(1)}) %tuple.24), branch_computations={%region_0.0_spmd, %region_1.0_spmd} | conditional | bytes 4989072 | solution.py:169
  6.2 0.7 broadcast_in_dim.0
  7.0 11.4 %all-to-all-start = ((bf16[32,16,256]{2,1,0:T(8,128)(2,1)}), bf16[32,16,256]{2,1,0:T(8,128)(2,1)}, u32[]{:S(2)}, u32[]{:S(2)}) async-start(bf16[32,16,256]{2,1,0:T(8,128)(2,1)} %broadcast_in_dim.0), calls=%async_computation | async-start | bytes 524288 | tf_op jit(solution)/shard_map/cond/branch_1_fun/all_to_all | solution.py:151
  18.4 0.8 %mask_blocks.3 = (bf16[256,768]{1,0:T(8,128)(2,1)S(1)}, bf16[256,768]{1,0:T(8,128)(2,1)S(1)}) custom-call(s32[2,24]{1,0:T(2,128)S(1)} %get-tuple-element.12.mask_hbm, bf16[256,3072]{1,0:T(8,128)(2,1)S(1)} %get-tuple-element.15.a_hbm), custom_call_target="tpu_custom_call" | custom-call | tf_op jit(solution)/shard_map/cond/branch_1_fun/mask_blocks/pallas_call | solution.py:62
  19.2 4.6 %collective-permute-start.1 = (bf16[256,768]{1,0:T(8,128)(2,1)S(1)}, bf16[256,768]{1,0:T(8,128)(2,1)}, u32[]{:S(2)}, u32[]{:S(2)}) collective-permute-start(bf16[256,768]{1,0:T(8,128)(2,1)S(1)} %get-tuple-element.16), channel_id=1, source_target_pairs={{0,18},{6,0},{12,6},{18,12},{1,19},{7,1},{13,7},{19,13},{2,20},{8,... | collective-permute-start | bytes 1179656 | tf_op jit(solution)/shard_map/cond/branch_1_fun/ppermute | solution.py:145
  23.8 1.9 %collective-permute-start = (bf16[256,768]{1,0:T(8,128)(2,1)S(1)}, bf16[256,768]{1,0:T(8,128)(2,1)}, u32[]{:S(2)}, u32[]{:S(2)}) collective-permute-start(bf16[256,768]{1,0:T(8,128)(2,1)S(1)} %get-tuple-element.14), channel_id=1, source_target_pairs={{0,6},{6,12},{12,18},{18,0},{1,7},{7,13},{13,19},{19,1},{2,8},{8,1... | collective-permute-start | bytes 1179656 | tf_op jit(solution)/shard_map/cond/branch_1_fun/ppermute | solution.py:145
  25.7 0.7 mask_blocks.4
  26.4 2.9 %all-to-all-done = bf16[32,16,256]{2,1,0:T(8,128)(2,1)} async-done(((bf16[32,16,256]{2,1,0:T(8,128)(2,1)}), bf16[32,16,256]{2,1,0:T(8,128)(2,1)}, u32[]{:S(2)}, u32[]{:S(2)}) %all-to-all-start) | async-done | bytes 262176 | tf_op jit(solution)/shard_map/cond/branch_1_fun/all_to_all | solution.py:151
  29.3 2.4 %all-gather = bf16[64,16,256]{2,1,0:T(8,128)(2,1)S(1)} all-gather(bf16[32,16,256]{2,1,0:T(8,128)(2,1)} %all-to-all-done), channel_id=2, replica_groups=mesh['y'=8,'c'=2,'zh'=2,'x'=4,'zl'=6] {'c'}, dimensions={0}, use_global_device_ids=true | all-gather | bytes 786432 | tf_op jit(solution)/shard_map/cond/branch_1_fun/all_gather | solution.py:152
  31.6 0.0 collective-permute-done.1
  31.6 3.1 %collective-permute-done = bf16[256,768]{1,0:T(8,128)(2,1)} collective-permute-done((bf16[256,768]{1,0:T(8,128)(2,1)S(1)}, bf16[256,768]{1,0:T(8,128)(2,1)}, u32[]{:S(2)}, u32[]{:S(2)}) %collective-permute-start) | collective-permute-done | bytes 393248 | tf_op jit(solution)/shard_map/cond/branch_1_fun/ppermute | solution.py:145
  34.8 0.0 collective-permute-done.2.refs_2_
  34.8 0.0 copy-start
  34.8 2.0 %product.1 = s16[12,136,128]{2,1,0:T(8,128)(2,1)S(1)} custom-call(s32[1]{0:T(128)} %bitcast.1.me_ref, bf16[2,8,4,16,256]{4,3,2,1,0:T(8,128)(2,1)S(1)} %get-tuple-element.24.f_ref, bf16[256,768]{1,0:T(8,128)(2,1)S(1)} %get-tuple-element.25.refs_0_, bf16[256,768]{1,0:T(8,128)(2,1)} %get-tuple-element.26.refs_1_, ...), custom_call_target="tpu_custom_call" | custom-call | tf_op jit(solution)/shard_map/product/pallas_call | solution.py:111
  36.8 34.6 %all_to_all.9.q_ref = s16[12,136,128]{2,1,0:T(8,128)(2,1)S(1)} all-to-all(s16[12,136,128]{2,1,0:T(8,128)(2,1)S(1)} %product.1), channel_id=1, replica_groups=mesh['y'=8,'c'=2,'zh'=2,'x'=4,'zl'=6] {'zh','zl'}, dimensions={0} | all-to-all | bytes 835584 | tf_op jit(solution)/shard_map/all_to_all | solution.py:172
  71.4 0.0 copy-done
  71.4 1.2 %finish.1 = f32[64,256]{1,0:T(8,128)} custom-call(s16[12,136,128]{2,1,0:T(8,128)(2,1)S(1)} %all_to_all.9.q_ref, bf16[64,256]{1,0:T(8,128)(2,1)S(1)} %copy-done), custom_call_target="tpu_custom_call" | custom-call | tf_op jit(solution)/shard_map/finish/pallas_call | solution.py:136
Async XLA Ops:
  0.0 6.2 %copy-start.2 = (s32[1,2,24]{2,1,0:T(2,128)S(1)}, s32[1,2,24]{2,1,0:T(2,128)}, u32[]{:S(2)}) copy-start(s32[1,2,24]{2,1,0:T(2,128)} %param.7) | copy-start | bytes 580
  0.0 6.2 %copy-start.1 = (bf16[1,256,3072]{2,1,0:T(8,128)(2,1)S(1)}, bf16[1,256,3072]{2,1,0:T(8,128)(2,1)}, u32[]{:S(2)}) copy-start(bf16[1,256,3072]{2,1,0:T(8,128)(2,1)} %param.6) | copy-start | bytes 4718596
  0.0 6.2 %copy-start.3 = (bf16[1,256,16]{1,2,0:T(8,128)(2,1)S(1)}, bf16[1,256,16]{1,2,0:T(8,128)(2,1)}, u32[]{:S(2)}) copy-start(bf16[1,256,16]{1,2,0:T(8,128)(2,1)} %param.8) | copy-start | bytes 24580
  1.2 33.5 %collective-permute-start.2 = (bf16[256,768]{1,0:T(8,128)(2,1)S(1)}, bf16[256,768]{1,0:T(8,128)(2,1)S(1)}, u32[]{:S(2)}, u32[]{:S(2)}) collective-permute-start(bf16[256,768]{1,0:T(8,128)(2,1)S(1)} %mask_blocks.5), channel_id=1, source_target_pairs={{0,12},{6,18},{12,0},{18,6},{1,13},{7,19},{13,1},{19,7},{2,14},{8,... | collective-permute-start | bytes 1179656 | tf_op jit(solution)/shard_map/ppermute | solution.py:145
  7.0 22.3 %all-to-all-start = ((bf16[32,16,256]{2,1,0:T(8,128)(2,1)}), bf16[32,16,256]{2,1,0:T(8,128)(2,1)}, u32[]{:S(2)}, u32[]{:S(2)}) async-start(bf16[32,16,256]{2,1,0:T(8,128)(2,1)} %broadcast_in_dim.0), calls=%async_computation | async-start | bytes 524288 | tf_op jit(solution)/shard_map/cond/branch_1_fun/all_to_all | solution.py:151
  19.2 12.4 %collective-permute-start.1 = (bf16[256,768]{1,0:T(8,128)(2,1)S(1)}, bf16[256,768]{1,0:T(8,128)(2,1)}, u32[]{:S(2)}, u32[]{:S(2)}) collective-permute-start(bf16[256,768]{1,0:T(8,128)(2,1)S(1)} %get-tuple-element.16), channel_id=1, source_target_pairs={{0,18},{6,0},{12,6},{18,12},{1,19},{7,1},{13,7},{19,13},{2,20},{8,... | collective-permute-start | bytes 1179656 | tf_op jit(solution)/shard_map/cond/branch_1_fun/ppermute | solution.py:145
  23.8 11.0 %collective-permute-start = (bf16[256,768]{1,0:T(8,128)(2,1)S(1)}, bf16[256,768]{1,0:T(8,128)(2,1)}, u32[]{:S(2)}, u32[]{:S(2)}) collective-permute-start(bf16[256,768]{1,0:T(8,128)(2,1)S(1)} %get-tuple-element.14), channel_id=1, source_target_pairs={{0,6},{6,12},{12,18},{18,0},{1,7},{7,13},{13,19},{19,1},{2,8},{8,1... | collective-permute-start | bytes 1179656 | tf_op jit(solution)/shard_map/cond/branch_1_fun/ppermute | solution.py:145
  34.8 36.7 %copy-start = (bf16[64,256]{1,0:T(8,128)(2,1)S(1)}, bf16[64,256]{1,0:T(8,128)(2,1)}, u32[]{:S(2)}) copy-start(bf16[64,256]{1,0:T(8,128)(2,1)} %t_ref.1) | copy-start | bytes 98308
